TPU v7x, 32 devices: a whole 2x2x4 slice. The times are simulated.
32 devices in a mesh: groups: 2 (over x), wide: 16 (over z, y, core).
Axes of the slice: x: 2, y: 2, z: 4, core: 2. Of those that a mesh axis runs over, the one named last changes fastest.
Arguments:
- charges: bfloat16 [16, 131072], P(None, ('groups', 'wide')), parts along dimension 1, may hold values from -6 to 6
- cell_offset: float32 [3, 131072], P(None, ('groups', 'wide')), parts along dimension 1, may hold values from 0 to 1
- base_cell: int32 [3, 131072], P(None, ('groups', 'wide')), parts along dimension 1, may hold values from 0 to 127, as said below
- counts: int32 [512], P(('groups', 'wide')), parts along dimension 0, may hold values from 128 to 256, as said below
- widths: float32 [16], replicated, may hold values from 0.75 to 2
Outputs:
- atom_potential: float32 [16, 131072], P(None, ('groups', 'wide')), parts along dimension 1
- forces: float32 [3, 131072], P(None, ('groups', 'wide')), parts along dimension 1
There are 2 independent parts, one for each index of `groups`. A program takes and returns all parts, laid end to end along the dimension named above; an argument that names none is the same for every part. Nothing has to cross between parts.
Inputs may be any that keep to these rules, and one draw needn't show every extreme that they name: For slot s on index i of wide (s // 4096 = i) in block b = (s // 256) mod 16: base_cell[0, s] lies in [i * 8, (i + 1) * 8), base_cell[1, s] in [b * 8, (b + 1) * 8), base_cell[2, s] in [0, 128). `counts`: each index of wide has a block whose 256 slots are all live.
All inputs are finite; a program needn't handle non-finite values.
Results may differ from a plain program's by a relative error of at most 0.002.
The roundings to bfloat16 on the way count: a program that leaves them out, or rounds other values in their place, can miss the bound.
Values may be sent and summed in bfloat16 or wider, within the bound.
No kernel may reach another device: no remote copies, remote signals or barrier semaphores. Data moves between devices by JAX's collectives and lax.ppermute only.
A program may use at most 128 MiB of HBM per device.

v0:
```python
import math

import jax
import jax.numpy as jnp
from jax import lax
from jax.sharding import PartitionSpec as P

MESH_X = 128
MESH_Y = 128
MESH_Z = 128
ORDER = 6


highest = lax.Precision.HIGHEST


def shifted(block, axis, distance):
    devices = range(lax.axis_size(axis))
    route = [((i - distance) % len(devices), i) for i in devices]
    return lax.ppermute(block, axis, route)


def spline_table(offset, order_count):
    weights = [1.0 - offset, offset]
    slopes = [-jnp.ones_like(offset), jnp.ones_like(offset)]
    for degree in range(3, order_count + 1):
        if degree == order_count:
            slopes = (
                [-weights[0]]
                + [weights[position - 1] - weights[position] for position in range(1, degree - 1)]
                + [weights[degree - 2]]
            )
        factor = 1.0 / (degree - 1)
        updated = [None] * degree
        updated[degree - 1] = factor * offset * weights[degree - 2]
        for position in range(1, degree - 1):
            updated[degree - position - 1] = factor * (
                (offset + position) * weights[degree - position - 2]
                + (degree - position - offset) * weights[degree - position - 1]
            )
        updated[0] = factor * (1.0 - offset) * weights[0]
        weights = updated
    return (jnp.stack(weights), jnp.stack(slopes))


def stencil_rows(weights, slopes, relative, extent, period):
    shifts = jnp.arange(weights.shape[0], dtype=jnp.int32)[None, :, None]
    targets = (relative[:, None, :] + shifts) % period
    points = jnp.arange(extent, dtype=jnp.int32)[None, :, None, None]
    matches = points == targets[:, None]
    plain_rows = jnp.sum(jnp.where(matches, jnp.moveaxis(weights, 0, 1)[:, None], 0.0), axis=2)
    slope_rows = jnp.sum(jnp.where(matches, jnp.moveaxis(slopes, 0, 1)[:, None], 0.0), axis=2)
    return (plain_rows, slope_rows)


def folded(points, length):
    values = jnp.where(points * 2 > length, points - length, points)
    return values.astype(jnp.float32) / length


def moduli(points, length):
    base_weights, base_slopes = spline_table(jnp.zeros((1,), jnp.float32), ORDER)
    shifts = jnp.arange(ORDER, dtype=jnp.int32)
    phases = points[:, None] * shifts[None, :] % length
    angles = phases.astype(jnp.float32) * (2.0 * math.pi / length)
    real_sum = jnp.sum(base_weights[:, 0][None, :] * jnp.cos(angles), axis=1)
    imag_sum = jnp.sum(base_weights[:, 0][None, :] * jnp.sin(angles), axis=1)
    return real_sum * real_sum + imag_sum * imag_sum


def kernel_table(widths, x_freq, y_freq, z_freq, x_mod, y_mod, z_mod):
    total = (
        x_freq[:, None, None, None] ** 2
        + y_freq[None, :, None, None] ** 2
        + z_freq[None, None, None, :] ** 2
    )
    positive = total > 0
    safe = jnp.where(positive, total, 1.0)
    beta = widths[None, None, :, None]
    divisor = x_mod[:, None, None, None] * y_mod[None, :, None, None] * z_mod[None, None, None, :]
    return jnp.where(
        positive,
        2.0 * jnp.exp(-math.pi**2 * total / (beta * beta)) / (math.pi * safe * divisor),
        0.0,
    )


def dft_tables(length):
    points = jnp.arange(length, dtype=jnp.int32)
    phases = points[:, None] * points[None, :] % length
    angles = phases.astype(jnp.float32) * (2.0 * math.pi / length)
    return (jnp.cos(angles), jnp.sin(angles))


def combine_blocks(block_grid, block_rows, border):
    owned = block_grid[:, :, :block_rows]
    overflow = jnp.roll(block_grid[:, :, block_rows:], 1, axis=0)
    owned = owned.at[:, :, :border].add(overflow)
    moved = jnp.moveaxis(owned, 0, 1)
    return moved.reshape((moved.shape[0], moved.shape[1] * moved.shape[2]) + moved.shape[3:])


def contract(data, x_weights, y_weights):
    return jnp.einsum("pycs,ps,ys->cs", data, x_weights, y_weights, precision=highest)


def turn(real_part, imag_part, cosines, sines, orient, pattern):

    def project(data, table):
        return jnp.einsum(pattern, data, table, precision=highest)

    real_out = project(real_part, cosines) - orient * project(imag_part, sines)
    imag_out = project(imag_part, cosines) + orient * project(real_part, sines)
    return jnp.stack([real_out, imag_out])


def shards(charges, cell_offset, base_cell, counts, widths):
    wide_size = lax.axis_size("wide")
    device = lax.axis_index("wide")
    channels, slot_count = charges.shape
    blocks = counts.shape[0]
    capacity = slot_count // blocks
    planes = MESH_X // wide_size
    border = ORDER - 1
    extent = planes + border
    block_rows = MESH_Y // blocks
    y_extent = block_rows + border
    rounds = (border + planes - 1) // planes
    y_local = MESH_Y // wide_size
    live_mask = jnp.arange(capacity, dtype=jnp.int32)[None, :] < counts[:, None]
    charge_blocks = jnp.where(
        live_mask[:, None, :],
        jnp.moveaxis(charges.reshape(channels, blocks, capacity), 0, 1),
        jnp.zeros((), jnp.bfloat16),
    )
    offsets = cell_offset.reshape(3, blocks, capacity)
    bases = base_cell.reshape(3, blocks, capacity)
    x_weights, x_slopes = spline_table(offsets[0], ORDER)
    y_weights, y_slopes = spline_table(offsets[1], ORDER)
    z_weights, z_slopes = spline_table(offsets[2], ORDER)
    row_start = jnp.arange(blocks, dtype=jnp.int32)[:, None] * block_rows
    x_rows, x_drows = stencil_rows(x_weights, x_slopes, bases[0] - device * planes, extent, extent)
    y_rows, y_drows = stencil_rows(y_weights, y_slopes, bases[1] - row_start, y_extent, y_extent)
    z_plain, z_slope = stencil_rows(z_weights, z_slopes, bases[2], MESH_Z, MESH_Z)
    z_table = jnp.stack([z_plain, z_slope], axis=2).astype(jnp.bfloat16)

    def spread_block(inputs):
        x_block, y_block, charge_block, table_block = inputs
        products = (
            x_block[:, None, None, :]
            * y_block[None, :, None, :]
            * charge_block.astype(jnp.float32)[None, None]
        ).astype(jnp.bfloat16)
        spread = jnp.einsum(
            "rs,zs->rz",
            products.reshape(-1, capacity),
            table_block[:, 0],
            preferred_element_type=jnp.float32,
        )
        return spread.reshape(extent, y_extent, channels, MESH_Z)

    block_grid = lax.map(spread_block, (x_rows, y_rows, charge_blocks, z_table))
    grid_ext = combine_blocks(block_grid, block_rows, border)
    z_cos, z_sin = dft_tables(MESH_Z)
    y_cos, y_sin = dft_tables(MESH_Y)
    x_cos, x_sin = dft_tables(MESH_X)
    x_points = jnp.arange(MESH_X, dtype=jnp.int32)
    y_points = device * y_local + jnp.arange(y_local, dtype=jnp.int32)
    z_points = jnp.arange(MESH_Z, dtype=jnp.int32)
    kernel = kernel_table(
        widths,
        folded(x_points, MESH_X),
        folded(y_points, MESH_Y),
        folded(z_points, MESH_Z),
        moduli(x_points, MESH_X),
        moduli(y_points, MESH_Y),
        moduli(z_points, MESH_Z),
    )
    kernel = kernel / float(MESH_X * MESH_Y * MESH_Z)
    owned = grid_ext[:planes]
    for hop_index in range(1, rounds + 1):
        outgoing = grid_ext[hop_index * planes : (hop_index + 1) * planes]
        outgoing = jnp.pad(outgoing, ((0, planes - outgoing.shape[0]), (0, 0), (0, 0), (0, 0)))
        owned = owned + shifted(outgoing, "wide", hop_index)
    real_z = jnp.dot(owned, z_cos, precision=highest)
    imag_z = -jnp.dot(owned, z_sin, precision=highest)
    columns = lax.all_to_all(
        turn(real_z, imag_z, y_cos, y_sin, -1.0, "pycz,yk->pkcz"),
        "wide",
        split_axis=2,
        concat_axis=1,
        tiled=True,
    )
    spectrum = turn(columns[0], columns[1], x_cos, x_sin, -1.0, "xycz,xk->kycz")
    filtered = turn(spectrum[0] * kernel, spectrum[1] * kernel, x_cos, x_sin, 1.0, "xycz,xk->kycz")
    returned = lax.all_to_all(filtered, "wide", split_axis=1, concat_axis=2, tiled=True)
    along_y = turn(returned[0], returned[1], y_cos, y_sin, 1.0, "pycz,yk->pkcz")
    potential_own = (
        jnp.dot(along_y[0], z_cos, precision=highest)
        - jnp.dot(along_y[1], z_sin, precision=highest)
    ).astype(jnp.bfloat16)
    pieces = [potential_own]
    for hop_index in range(1, rounds + 1):
        pieces.append(shifted(potential_own, "wide", -hop_index))
    potential_ext = jnp.concatenate(pieces, axis=0)[:extent]
    blocked = potential_ext.reshape(extent, blocks, block_rows, channels, MESH_Z)
    following = jnp.roll(blocked[:, :, :border], -1, axis=1)
    windows = jnp.moveaxis(jnp.concatenate([blocked, following], axis=2), 1, 0)

    def gather_block(inputs):
        window, x_block, x_dblock, y_block, y_dblock, table_block, charge_block, live_block = inputs
        values = jnp.dot(
            window.reshape(-1, MESH_Z),
            table_block.reshape(MESH_Z, -1),
            preferred_element_type=jnp.float32,
        )
        values = values.reshape(extent, y_extent, channels, 2, capacity)
        direct = values[:, :, :, 0]
        sloped = values[:, :, :, 1]
        potential = jnp.where(live_block[None], contract(direct, x_block, y_block), 0.0)
        gradient = jnp.stack(
            [
                contract(direct, x_dblock, y_block),
                contract(direct, x_block, y_dblock),
                contract(sloped, x_block, y_block),
            ]
        )
        forces = -jnp.sum(gradient * charge_block.astype(jnp.float32)[None], axis=1)
        return (potential, forces)

    potentials, forces = lax.map(
        gather_block, (windows, x_rows, x_drows, y_rows, y_drows, z_table, charge_blocks, live_mask)
    )
    atom_potential = jnp.moveaxis(potentials, 0, 1).reshape(channels, slot_count)
    atom_forces = jnp.moveaxis(forces, 0, 1).reshape(3, slot_count)
    return (atom_potential, atom_forces)


def solution(mesh):
    in_specs = (
        P(None, ("groups", "wide")),
        P(None, ("groups", "wide")),
        P(None, ("groups", "wide")),
        P(("groups", "wide")),
        P(),
    )
    out_specs = (P(None, ("groups", "wide")), P(None, ("groups", "wide")))
    return jax.shard_map(shards, mesh=mesh, in_specs=in_specs, out_specs=out_specs, check_vma=False)
```

profile of v0, /device:TPU:0, one launch (start us, length us, event | category | flops | bytes accessed | tf_op | source)
XLA Modules:
  0.0 1404.5 jit_solution(10154539111549712938)
XLA Ops:
  11.0 27.5 %while.23 = (s32[]{:T(128)}, f32[16,13,13,16,128]{4,3,2,0,1:T(8,128)}, f32[16,13,256]{2,1,0:T(8,128)S(1)}, f32[16,13,256]{2,1,0:T(8,128)S(1)}, bf16[16,16,256]{2...) while((s32[]{:T(128)}, f32[16,13,13,16,128]{4,3,2,0,1:T(8,128)}, ...), condition=%wide.region_5.6_spmd, body=%wide.region_4.5_spmd.sunk | while | flops 178641152 | bytes 2219609 | solution.py:162
  40.0 12.2 slice.130
  69.9 92.4 %collective-permute-done = f32[8,128,16,128]{3,2,1,0:T(8,128)} collective-permute-done((f32[8,128,16,128]{3,2,1,0:T(8,128)S(1)}, f32[8,128,16,128]{3,2,1,0:T(8,128)}, u32[]{:S(2)}, u32[]{:S(2)}) %collective-permute-start) | collective-permute-done | bytes 8388640 | tf_op jit(solution)/shard_map/ppermute | solution.py:20
  172.4 12.5 fusion.36
  193.6 10.4 fusion.82
  211.9 12.0 subtract_bitcast_fusion.1
  238.7 19.6 %copy.389 = f32[2,8,128,16,128]{4,3,1,0,2:T(8,128)} copy(f32[2,8,128,16,128]{4,2,3,1,0:T(8,128)S(1)} %pad_maximum_fusion) | data formatting | bytes 33554432 | tf_op jit(solution)/shard_map/stack | solution.py:114
  266.3 294.2 %all-to-all-done = f32[2,8,128,16,128]{4,3,1,0,2:T(8,128)} async-done(((f32[2,8,128,16,128]{4,3,1,0,2:T(8,128)}), f32[2,8,128,16,128]{4,3,1,0,2:T(8,128)}, u32[]{:S(2)}, u32[]{:S(2)}) %all-to-all-start) | async-done | bytes 16777248 | tf_op jit(solution)/shard_map/all_to_all | solution.py:187
  560.4 10.9 copy.522
  591.4 13.1 subtract_multiply_fusion
  614.5 14.0 add_multiply_fusion
  628.5 12.3 fusion.78
  650.8 12.5 add_bitcast_fusion
  668.2 18.1 %copy.399 = f32[2,128,8,16,128]{4,3,2,0,1:T(8,128)S(1)} copy(f32[2,128,8,16,128]{4,1,3,2,0:T(8,128)S(1)} %pad_maximum_fusion.1) | data formatting | bytes 33554432 | tf_op jit(solution)/shard_map/stack | solution.py:114
  686.2 431.9 %all_to_all.30 = f32[2,128,8,16,128]{4,3,2,0,1:T(8,128)S(1)} all-to-all(f32[2,128,8,16,128]{4,3,2,0,1:T(8,128)S(1)} %copy.399), channel_id=1, replica_groups=mesh['groups'=2,'wide'=16] {'wide'}, dimensions={1} | all-to-all | bytes 33554432 | tf_op jit(solution)/shard_map/all_to_all | solution.py:196
  1130.6 11.6 fusion.26
  1142.2 10.3 fusion.28
  1157.0 11.4 fusion.30
  1168.4 11.2 fusion.32
  1179.7 10.9 fusion.16
  1190.6 11.3 subtract_convert_fusion
  1206.9 46.3 %collective-permute-done.1 = bf16[8,128,16,128]{3,1,2,0:T(8,128)(2,1)} collective-permute-done((bf16[8,128,16,128]{3,1,2,0:T(8,128)(2,1)}, bf16[8,128,16,128]{3,1,2,0:T(8,128)(2,1)}, u32[]{:S(2)}, u32[]{:S(2)}) %collective-permute-start.1) | collective-permute-done | bytes 4194336 | tf_op jit(solution)/shard_map/ppermute | solution.py:20
  1259.6 10.8 copy.413
  1278.6 124.7 %while.24 = (s32[]{:T(128)}, f32[16,16,256]{2,1,0:T(8,128)S(1)}, f32[16,3,256]{2,1,0:T(4,128)S(1)}, pred[16,256]{1,0:T(8,128)(4,1)}, f32[16,13,256]{2,1,0:T(8,12...) while((s32[]{:T(128)}, f32[16,16,256]{2,1,0:T(8,128)S(1)}, ...), condition=%wide.region_14.15_spmd, body=%wide.region_12.14_spmd.sunk | while | flops 360127232 | bytes 14914193 | solution.py:231
  (474 shorter events, 311.1 us)
Async XLA Ops:
  6.4 4.3 copy-start.9
  38.5 1.4 copy-start.5
  38.5 1.4 copy-start.6
  38.5 1.5 copy-start.7
  38.5 13.6 copy-start.8
  52.1 7.3 copy-start.1
  65.6 96.7 %collective-permute-start = (f32[8,128,16,128]{3,2,1,0:T(8,128)S(1)}, f32[8,128,16,128]{3,2,1,0:T(8,128)}, u32[]{:S(2)}, u32[]{:S(2)}) collective-permute-start(f32[8,128,16,128]{3,2,1,0:T(8,128)S(1)} %pad.6), channel_id=1, source_target_pairs={{15,0},{0,1},{1,2},{2,3},{3,4},{4,5},{5,6},{6,7},{7,8},{8,9},{9,10... | collective-permute-start | bytes 25165832 | tf_op jit(solution)/shard_map/ppermute | solution.py:20
  172.4 12.5 copy-start
  258.3 5.5 copy-start.12
  258.3 5.6 copy-start.10
  258.3 302.2 %all-to-all-start = ((f32[2,8,128,16,128]{4,3,1,0,2:T(8,128)}), f32[2,8,128,16,128]{4,3,1,0,2:T(8,128)}, u32[]{:S(2)}, u32[]{:S(2)}) async-start(f32[2,8,128,16,128]{4,3,1,0,2:T(8,128)} %copy.389), calls=%async_computation | async-start | bytes 33554432 | tf_op jit(solution)/shard_map/all_to_all | solution.py:187
  628.5 12.3 copy-start.2
  628.5 12.3 copy-start.3
  650.8 12.5 copy-start.4
  1201.9 51.3 %collective-permute-start.1 = (bf16[8,128,16,128]{3,1,2,0:T(8,128)(2,1)}, bf16[8,128,16,128]{3,1,2,0:T(8,128)(2,1)}, u32[]{:S(2)}, u32[]{:S(2)}) collective-permute-start(bf16[8,128,16,128]{3,1,2,0:T(8,128)(2,1)} %subtract_convert_fusion), channel_id=1, source_target_pairs={{1,0},{2,1},{3,2},{4,3},{5,4},{6,5},{7,6},{8,7},{9,8},{10,9},{11,1... | collective-permute-start | bytes 12582920 | tf_op jit(solution)/shard_map/ppermute | solution.py:20
  1403.3 0.7 copy-start.11
where the time goes:
time: 1420 us; the launch traced here: 1400 us
  waiting for transfers between devices  433 us (30%)
  blocking collectives  432 us (30%)
  matrix products  279 us (20%)
  local copies, waits for them, and re-layouts  168 us (12%)
  other arithmetic  78.9 us (6%)
    all_to_all x1, blocking collectives, shards(): lax.all_to_all(filtered, 'wide', split_axis=1, concat_axis=2, tiled=True)  432 us
    all_to_all x1, waiting for transfers between devices, shards(): lax.all_to_all(turn(real_z, imag_z, y_cos, y_sin, -1.0, 'pycz,yk->pkcz'),...  294 us
    dot_general x16, matrix products, project(): return jnp.einsum(pattern, data, table, precision=highest)  177 us
    ppermute x2, waiting for transfers between devices, shifted(): return lax.ppermute(block, axis, route)  139 us
    another operation x2, local copies, waits for them, and re-layouts, turn(): return jnp.stack([real_out, imag_out])  37.7 us
    dynamic_slice x80, local copies, waits for them, and re-layouts, shards(): block_grid = lax.map(spread_block, (x_rows, y_rows, charge_blocks, z_table))  32.4 us
    dot_general x16, matrix products, gather_block(): jnp.dot(window.reshape(-1, MESH_Z), table_block.reshape(MESH_Z, -1), pref...  31.7 us
  transfers between devices with their start and end apart: 3, of which 3 were waited for; matrix products, arithmetic and copies ran while one was open for 0% of the time, Pallas kernels for 0%

commit v1 on v0

--- a/solution.py
+++ b/solution.py
@@ -1,8 +1,12 @@
+import functools
 import math
 
 import jax
 import jax.numpy as jnp
+import numpy as np
 from jax import lax
+from jax.experimental import pallas as pl
+from jax.experimental.pallas import tpu as pltpu
 from jax.sharding import PartitionSpec as P
 
 MESH_X = 128
@@ -20,7 +24,7 @@
     return lax.ppermute(block, axis, route)
 
 
-def spline_table(offset, order_count):
+def spline_lists(offset, order_count):
     weights = [1.0 - offset, offset]
     slopes = [-jnp.ones_like(offset), jnp.ones_like(offset)]
     for degree in range(3, order_count + 1):
@@ -40,6 +44,11 @@
             )
         updated[0] = factor * (1.0 - offset) * weights[0]
         weights = updated
+    return (weights, slopes)
+
+
+def spline_table(offset, order_count):
+    weights, slopes = spline_lists(offset, order_count)
     return (jnp.stack(weights), jnp.stack(slopes))
 
 
@@ -114,7 +123,7 @@
     return jnp.stack([real_out, imag_out])
 
 
-def shards(charges, cell_offset, base_cell, counts, widths):
+def slab_shards(charges, cell_offset, base_cell, counts, widths):
     wide_size = lax.axis_size("wide")
     device = lax.axis_index("wide")
     channels, slot_count = charges.shape
@@ -236,6 +245,296 @@
     return (atom_potential, atom_forces)
 
 
+def cas_terms(length):
+    points = np.arange(length)
+    angles = (points[:, None] * points[None, :] % length) * (2.0 * math.pi / length)
+    left = (np.cos(angles) + np.sin(angles)).astype(np.float32)
+    terms = []
+    for _ in range(3):
+        term = left.astype(jnp.bfloat16)
+        terms.append(term)
+        left = left - term.astype(np.float32)
+    return terms
+
+
+def split(values):
+    terms = []
+    for _ in range(3):
+        term = values.astype(jnp.bfloat16)
+        terms.append(term)
+        values = values - term.astype(jnp.float32)
+    return terms
+
+
+def dot32(a, b, contract_b=0):
+    return lax.dot_general(a, b, (((1,), (contract_b,)), ((), ())), preferred_element_type=jnp.float32)
+
+
+def cas_lanes(values, right_a, right_b):
+    first, second, third = split(values)
+    wide = dot32(jnp.concatenate([first, second], axis=1), right_a)
+    rest = dot32(jnp.concatenate([first, third], axis=1), right_b)
+    length = values.shape[1]
+    return wide[:, :length] + (wide[:, length:] + rest)
+
+
+def cas_rows(values, left_a, left_b):
+    first, second, third = split(values)
+    wide = dot32(left_a, jnp.concatenate([first, second], axis=0))
+    rest = dot32(left_b, jnp.concatenate([first, third], axis=0))
+    length = values.shape[0]
+    return wide[:length] + (wide[length:] + rest)
+
+
+def channel_kernel(
+    geometry_ref, charge_ref, pair_ref, square_ref, gain_ref, y_square_ref,
+    right_a_ref, right_b_ref, left_a_ref, left_b_ref, out_ref,
+    grid_ref, turned_ref, spline_ref, place_ref,
+):
+    slabs, _, blocks, capacity = geometry_ref.shape
+    planes = MESH_X // slabs
+    rows = MESH_Y // blocks
+    border = ORDER - 1
+    frame = 16
+    extent = planes + border
+    far = MESH_X + border
+
+    def prepare(slab, carry):
+        packed = geometry_ref[slab, 3].astype(jnp.int32)
+        span = pl.ds(pl.multiple_of(slab * blocks, blocks), blocks)
+        place_ref[0, span, :] = packed & 7
+        place_ref[1, span, :] = (packed >> 3) & 7
+        place_ref[2, span, :] = (packed >> 6) & 7
+        place_ref[3, span, :] = packed >> 9
+        for dimension in range(3):
+            weights, slopes = spline_lists(geometry_ref[slab, dimension], ORDER)
+            for position in range(ORDER):
+                spline_ref[dimension * 2 * ORDER + position, span, :] = weights[position]
+                spline_ref[(dimension * 2 + 1) * ORDER + position, span, :] = slopes[position]
+        return carry
+
+    lax.fori_loop(0, slabs, prepare, 0)
+
+    def clear(plane, carry):
+        grid_ref[plane] = jnp.zeros(grid_ref.shape[1:], jnp.float32)
+        return carry
+
+    lax.fori_loop(0, far, clear, 0)
+    points = lax.broadcasted_iota(jnp.int32, (frame, capacity), 0)
+
+    def local_table(dimension, block, kinds):
+        distance = points - place_ref[dimension, pl.ds(block, 1), :]
+        matches = [distance == position for position in range(ORDER)]
+        tables = []
+        for kind in kinds:
+            table = jnp.zeros((frame, capacity), jnp.float32)
+            for position in range(ORDER):
+                row = spline_ref[(dimension * 2 + kind) * ORDER + position, pl.ds(block, 1), :]
+                table = jnp.where(matches[position], row, table)
+            tables.append(table)
+        return tables
+
+    def z_tables(block, kinds):
+        tables = local_table(2, block, kinds)
+        tile = jnp.broadcast_to(place_ref[3, pl.ds(block, 1), :], (8, capacity))
+        here = [tile == index for index in range(MESH_Z // 8)]
+        results = []
+        for table in tables:
+            low, high = table[:8], table[8:]
+            pieces = [
+                jnp.where(here[index], low, jnp.where(here[index - 1], high, 0.0))
+                for index in range(MESH_Z // 8)
+            ]
+            results.append(jnp.concatenate(pieces, axis=0).astype(jnp.bfloat16))
+        return results
+
+    def spread(slab, block):
+        place = slab * blocks + block
+        (x_table,) = local_table(0, place, (0,))
+        (y_table,) = local_table(1, place, (0,))
+        (z_table,) = z_tables(place, (0,))
+        charge = charge_ref[slab, pl.ds(block, 1), :]
+        products = jnp.concatenate(
+            [
+                ((x_table[index : index + 1] * y_table) * charge).astype(jnp.bfloat16)
+                for index in range(extent)
+            ],
+            axis=0,
+        )
+        sums = dot32(products, z_table, 1)
+        row_span = pl.ds(pl.multiple_of(block * rows, rows), frame)
+        for index in range(extent):
+            grid_ref[slab * planes + index, row_span, :] += sums[index * frame : (index + 1) * frame]
+
+    def spread_step(step, carry):
+        spread(step // blocks, step % blocks)
+        return carry
+
+    lax.fori_loop(0, slabs * blocks, spread_step, 0)
+
+    for index in range(border):
+        grid_ref[index] += grid_ref[MESH_X + index]
+
+    right_a, right_b = right_a_ref[...], right_b_ref[...]
+    left_a, left_b = left_a_ref[...], left_b_ref[...]
+
+    def forward(step, carry):
+        both = []
+        for index in range(2):
+            plane = 2 * step + index
+            both.append(grid_ref[plane, 0:8, :] + grid_ref[plane, MESH_Y : MESH_Y + 8, :])
+            both.append(grid_ref[plane, 8:MESH_Y, :])
+        along_z = cas_lanes(jnp.concatenate(both, axis=0), right_a, right_b)
+        along_y = cas_rows(
+            jnp.concatenate([along_z[:MESH_Y], along_z[MESH_Y:]], axis=1), left_a, left_b
+        )
+        for index in range(2):
+            turned_ref[pl.ds(2 * step + index, MESH_Y, stride=MESH_X), :] = along_y[
+                :, index * MESH_Z : (index + 1) * MESH_Z
+            ]
+        return carry
+
+    lax.fori_loop(0, MESH_X // 2, forward, 0)
+
+    def filtering(step, carry):
+        spans = [pl.ds(pl.multiple_of((2 * step + index) * MESH_X, MESH_X), MESH_X) for index in range(2)]
+        lines = jnp.concatenate([turned_ref[span, :] for span in spans], axis=1)
+        spectrum = cas_rows(lines, left_a, left_b)
+        filters = []
+        for index in range(2):
+            total = square_ref[...] + y_square_ref[2 * step + index]
+            positive = total > 0
+            safe = jnp.where(positive, total, 1.0)
+            filters.append(jnp.where(positive, pair_ref[...] * gain_ref[2 * step + index] / safe, 0.0))
+        lines = cas_rows(spectrum * jnp.concatenate(filters, axis=1), left_a, left_b)
+        for index, span in enumerate(spans):
+            turned_ref[span, :] = lines[:, index * MESH_Z : (index + 1) * MESH_Z]
+        return carry
+
+    lax.fori_loop(0, MESH_Y // 2, filtering, 0)
+
+    def backward(step, carry):
+        both = jnp.concatenate(
+            [turned_ref[pl.ds(2 * step + index, MESH_Y, stride=MESH_X), :] for index in range(2)], axis=1
+        )
+        along_y = cas_rows(both, left_a, left_b)
+        field = cas_lanes(
+            jnp.concatenate([along_y[:, :MESH_Z], along_y[:, MESH_Z:]], axis=0), right_a, right_b
+        )
+        rounded = field.astype(jnp.bfloat16).astype(jnp.float32)
+        for index in range(2):
+            grid_ref[2 * step + index, 0:MESH_Y, :] = rounded[index * MESH_Y : (index + 1) * MESH_Y]
+            grid_ref[2 * step + index, MESH_Y : MESH_Y + 8, :] = rounded[index * MESH_Y : index * MESH_Y + 8]
+        return carry
+
+    lax.fori_loop(0, MESH_X // 2, backward, 0)
+
+    for index in range(border):
+        grid_ref[MESH_X + index] = grid_ref[index]
+
+    def gather(slab, block):
+        place = slab * blocks + block
+        x_table, x_slope = local_table(0, place, (0, 1))
+        y_table, y_slope = local_table(1, place, (0, 1))
+        z_table, z_slope = z_tables(place, (0, 1))
+        charge = charge_ref[slab, pl.ds(block, 1), :]
+        row_span = pl.ds(pl.multiple_of(block * rows, rows), frame)
+        window = jnp.concatenate(
+            [grid_ref[slab * planes + index, row_span, :] for index in range(extent)], axis=0
+        ).astype(jnp.bfloat16)
+        near = dot32(window, z_table)
+        near_z = dot32(window, z_slope)
+        plain = jnp.zeros((frame, capacity), jnp.float32)
+        sloped = jnp.zeros((frame, capacity), jnp.float32)
+        plain_z = jnp.zeros((frame, capacity), jnp.float32)
+        for index in range(extent):
+            part = near[index * frame : (index + 1) * frame]
+            plain += x_table[index : index + 1] * part
+            sloped += x_slope[index : index + 1] * part
+            plain_z += x_table[index : index + 1] * near_z[index * frame : (index + 1) * frame]
+        row = pl.ds(block, 1)
+        out_ref[slab, 0, row, :] = jnp.sum(y_table * plain, axis=0, keepdims=True)
+        out_ref[slab, 1, row, :] = -charge * jnp.sum(y_table * sloped, axis=0, keepdims=True)
+        out_ref[slab, 2, row, :] = -charge * jnp.sum(y_slope * plain, axis=0, keepdims=True)
+        out_ref[slab, 3, row, :] = -charge * jnp.sum(y_table * plain_z, axis=0, keepdims=True)
+
+    def gather_step(step, carry):
+        gather(step // blocks, step % blocks)
+        return carry
+
+    lax.fori_loop(0, slabs * blocks, gather_step, 0)
+
+
+def channel_shards(charges, cell_offset, base_cell, counts, widths):
+    device = lax.axis_index("wide")
+    channels, slot_count = charges.shape
+    blocks = counts.shape[0]
+    capacity = slot_count // blocks
+    slabs = lax.axis_size("wide")
+    planes = MESH_X // slabs
+    block_rows = MESH_Y // blocks
+    live_mask = jnp.arange(capacity, dtype=jnp.int32)[None, :] < counts[:, None]
+    charge_blocks = jnp.where(
+        live_mask[None], charges.reshape(channels, blocks, capacity), jnp.zeros((), jnp.bfloat16)
+    )
+    bases = base_cell.reshape(3, blocks, capacity)
+    row_start = jnp.arange(blocks, dtype=jnp.int32)[:, None] * block_rows
+    packed = (bases[0] - device * planes) + 8 * (bases[1] - row_start) + 64 * bases[2]
+    geometry = jnp.concatenate(
+        [cell_offset.reshape(3, blocks, capacity), packed.astype(jnp.float32)[None]], axis=0
+    )
+    geometry = lax.all_gather(geometry, "wide", axis=0, tiled=False)
+    charge_blocks = lax.all_to_all(charge_blocks, "wide", split_axis=0, concat_axis=0, tiled=True)
+
+    width = lax.dynamic_index_in_dim(widths, device, keepdims=False)
+    points = np.arange(MESH_X)
+    folded_points = np.where(points * 2 > MESH_X, points - MESH_X, points) / MESH_X
+    squares = (folded_points**2).astype(np.float32)
+    first = np.array([1.0, 26.0, 66.0, 26.0, 1.0, 0.0]) / 120.0
+    angles = 2.0 * math.pi * points[:, None] * np.arange(ORDER)[None, :] / MESH_X
+    inverse = (1.0 / ((np.cos(angles) @ first) ** 2 + (np.sin(angles) @ first) ** 2)).astype(np.float32)
+    gains = jnp.exp(-(math.pi**2) * squares / (width * width)) * inverse
+    scale = 2.0 / (math.pi * MESH_X * MESH_Y * MESH_Z)
+    pairs = gains[:, None] * (gains * scale)[None, :]
+    pair_squares = squares[:, None] + squares[None, :]
+    one, two, three = cas_terms(MESH_X)
+    right_a = np.concatenate([np.concatenate([one, two], axis=1)] * 2, axis=0)
+    right_b = np.concatenate([three, one], axis=0)
+    left_a = np.concatenate([np.concatenate([one, one], axis=1), np.concatenate([two, two], axis=1)], axis=0)
+    left_b = np.concatenate([three, one], axis=1)
+
+    whole = pl.BlockSpec(memory_space=pltpu.VMEM)
+    scalars = pl.BlockSpec(memory_space=pltpu.SMEM)
+    result = pl.pallas_call(
+        channel_kernel,
+        out_shape=jax.ShapeDtypeStruct((slabs, 4, blocks, capacity), jnp.float32),
+        in_specs=[whole] * 4 + [scalars] * 2 + [whole] * 4,
+        out_specs=whole,
+        scratch_shapes=[
+            pltpu.VMEM((MESH_X + ORDER - 1, MESH_Y + 8, MESH_Z), jnp.float32),
+            pltpu.VMEM((MESH_X * MESH_Y, MESH_Z), jnp.float32),
+            pltpu.VMEM((6 * ORDER, slabs * blocks, capacity), jnp.float32),
+            pltpu.VMEM((4, slabs * blocks, capacity), jnp.int32),
+        ],
+        compiler_params=pltpu.CompilerParams(vmem_limit_bytes=52 * 1024 * 1024),
+        name="channel",
+    )(
+        geometry, charge_blocks.astype(jnp.float32), pairs, jnp.asarray(pair_squares), gains,
+        jnp.asarray(squares), jnp.asarray(right_a), jnp.asarray(right_b), jnp.asarray(left_a),
+        jnp.asarray(left_b),
+    )
+    returned = lax.all_to_all(result, "wide", split_axis=0, concat_axis=0, tiled=True)
+    atom_potential = jnp.where(live_mask[None], returned[:, 0], 0.0).reshape(channels, slot_count)
+    forces = jnp.sum(returned[:, 1:], axis=0).reshape(3, slot_count)
+    return (atom_potential, forces)
+
+
+def shards(charges, cell_offset, base_cell, counts, widths):
+    if lax.axis_size("wide") == charges.shape[0] and MESH_X == 8 * lax.axis_size("wide"):
+        return channel_shards(charges, cell_offset, base_cell, counts, widths)
+    return slab_shards(charges, cell_offset, base_cell, counts, widths)
+
+
 def solution(mesh):
     in_specs = (
         P(None, ("groups", "wide")),

time: 1420 us -> 310 us (0.22)
  blocking collectives: 432 us -> 0 us
  waiting for transfers between devices: 433 us -> 52.2 us
  matrix products: 279 us -> 0 us
  Pallas kernels: 0 us -> 222 us
  local copies, waits for them, and re-layouts: 168 us -> 4.52 us
  other arithmetic: 78.9 us -> 3.47 us
    all_to_all x1 -> x0, blocking collectives: 432 us -> none  [shards(): lax.all_to_all(filtered, 'wide', split_axis=1, concat_axis=2, tiled=True)]
    dot_general x52 -> x0, matrix products: 279 us -> none  [the longest x16 177 us: project(): return jnp.einsum(pattern, data, table, precision=highest)]
    all_to_all x1 -> x2, waiting for transfers between devices: 294 us -> 27.4 us  [the longest x1 22.8 us: channel_shards(): lax.all_to_all(result, 'wide', split_axis=0, concat_axis=0, tiled=True)]
    pallas_call x0 -> x1, Pallas kernels: none -> 222 us  [channel_shards(): pl.pallas_call(channel_kernel, out_shape=jax.ShapeDtypeStruct((slabs, 4,...]
    ppermute x2 -> x0, waiting for transfers between devices: 139 us -> none  [shifted(): return lax.ppermute(block, axis, route)]
    dynamic_slice x96 -> x1, local copies, waits for them, and re-layouts: 43.7 us -> 0.61 us  [channel_shards(): width = lax.dynamic_index_in_dim(widths, device, keepdims=False)]
    slice x11 -> x1, local copies, waits for them, and re-layouts: 39.5 us -> 0.02 us  [channel_shards(): returned[:, 0]]
    another operation x2 -> x0, local copies, waits for them, and re-layouts: 37.7 us -> none  [turn(): return jnp.stack([real_out, imag_out])]
  transfers between devices with their start and end apart: 3 -> 3, of which waited for: 3 -> 3; matrix products, arithmetic and copies ran while one was open for 0% -> 1% of each run, Pallas kernels for 0% -> 0%
where the time goes in v1:
time: 310 us; the launch traced here: 309 us
  Pallas kernels  222 us (72%)
  waiting for transfers between devices  52.2 us (17%)
  between operations  15.5 us (5%)
  starting transfers between devices  11.1 us (4%)
  local copies, waits for them, and re-layouts  4.52 us (1%)
  other arithmetic  3.47 us (1%)
    pallas_call x1, Pallas kernels, channel_shards(): pl.pallas_call(channel_kernel, out_shape=jax.ShapeDtypeStruct((slabs, 4,...  222 us
    all_gather x1, waiting for transfers between devices, channel_shards(): geometry = lax.all_gather(geometry, 'wide', axis=0, tiled=False)  24.8 us
    all_to_all x1, waiting for transfers between devices, channel_shards(): lax.all_to_all(result, 'wide', split_axis=0, concat_axis=0, tiled=True)  22.8 us
    all_to_all x1, starting transfers between devices, channel_shards(): lax.all_to_all(charge_blocks, 'wide', split_axis=0, concat_axis=0, tiled=...  7.39 us
  transfers between devices with their start and end apart: 3, of which 3 were waited for; matrix products, arithmetic and copies ran while one was open for 1% of the time, Pallas kernels for 0%

profile of v1, /device:TPU:0, one launch (start us, length us, event | category | flops | bytes accessed | tf_op | source)
XLA Modules:
  0.0 308.7 jit_solution(9088613532921385614)
XLA Ops:
  7.2 0.0 all-gather.3.cloned.1.call-start
  7.2 1.1 slice_reduce_fusion.1
  8.4 0.8 copy-done.7
  9.2 0.1 add_convert_fusion
  9.3 0.6 pad_maximum_fusion
  9.9 0.2 copy-done.6
  10.1 0.6 copy-done.8
  10.7 0.1 iota_compare_fusion
  10.8 0.7 bitcast_select_fusion
  11.5 7.4 %all-to-all-start = ((bf16[16,16,256]{2,1,0:T(8,128)(2,1)}), bf16[16,16,256]{2,1,0:T(8,128)(2,1)S(1)}, u32[]{:S(2)}, u32[]{:S(2)}) async-start(bf16[16,16,256]{2,1,0:T(8,128)(2,1)} %bitcast_select_fusion), calls=%async_computation | async-start | bytes 262144 | tf_op jit(solution)/shard_map/all_to_all | solution.py:487
  18.9 0.6 copy-done.11
  19.5 0.6 dynamic_slice.4
  21.4 0.6 copy-done.9
  22.1 0.1 broadcast_multiply_fusion.pair_ref
  22.2 4.6 %all-to-all-done = bf16[16,16,256]{2,1,0:T(8,128)(2,1)S(1)} async-done(((bf16[16,16,256]{2,1,0:T(8,128)(2,1)}), bf16[16,16,256]{2,1,0:T(8,128)(2,1)S(1)}, u32[]{:S(2)}, u32[]{:S(2)}) %all-to-all-start) | async-done | bytes 131104 | tf_op jit(solution)/shard_map/all_to_all | solution.py:487
  26.9 24.8 %all-gather.3.cloned.1.call-done = f32[64,16,256]{2,1,0:T(8,128)} async-done(((f32[4,16,256]{2,1,0:T(8,128)}), f32[64,16,256]{2,1,0:T(8,128)}) %all-gather.3.cloned.1.call-update) | async-done | bytes 1048592 | tf_op jit(solution)/shard_map/all_gather | solution.py:486
  51.7 221.9 %channel.1 = f32[16,4,16,256]{3,2,1,0:T(8,128)} custom-call(f32[16,4,16,256]{3,2,1,0:T(8,128)} %bitcast.18, f32[16,16,256]{2,1,0:T(8,128)S(1)} %convert_element_type.14.charge_ref, f32[128,128]{1,0:T(8,128)S(1)} %broadcast_multiply_fusion.pair_ref, f32[128,128]{1,0:T(8,128)S(1)} %copy-done.2, f32[128]{0:T(128)S(1)} %get-tuple-element.6.gain_ref, ...), custom_call_target="tpu_custom_call" | custom-call | tf_op jit(solution)/shard_map/channel/pallas_call | solution.py:508
  273.6 3.7 %all-to-all-start.1 = ((f32[16,4,16,256]{3,2,1,0:T(8,128)}), f32[16,4,16,256]{3,2,1,0:T(8,128)S(1)}, u32[]{:S(2)}, u32[]{:S(2)}) async-start(f32[16,4,16,256]{3,2,1,0:T(8,128)} %channel.1), calls=%async_computation.1 | async-start | bytes 2097152 | tf_op jit(solution)/shard_map/all_to_all | solution.py:526
  277.3 0.1 lt.34
  277.4 22.8 %all-to-all-done.1 = f32[16,4,16,256]{3,2,1,0:T(8,128)S(1)} async-done(((f32[16,4,16,256]{3,2,1,0:T(8,128)}), f32[16,4,16,256]{3,2,1,0:T(8,128)S(1)}, u32[]{:S(2)}, u32[]{:S(2)}) %all-to-all-start.1) | async-done | bytes 1048608 | tf_op jit(solution)/shard_map/all_to_all | solution.py:526
  300.2 0.2 copy.18
  300.4 0.1 slice_reduce_fusion
  300.5 0.7 copy.19
  301.1 0.7 broadcast_select_fusion
  (32 shorter events, 0.2 us)
Async XLA Ops:
  7.2 44.5 %all-gather.3.cloned.1.call-start = ((), (), s32[]{:S(2)}) async-start(), calls=%async_computation.2 | async-start | bytes 1114112 | tf_op jit(solution)/shard_map/all_gather | solution.py:486
  8.3 0.8 copy-start.7
  9.2 0.9 copy-start.6
  10.1 0.7 copy-start.8
  11.5 15.3 %all-to-all-start = ((bf16[16,16,256]{2,1,0:T(8,128)(2,1)}), bf16[16,16,256]{2,1,0:T(8,128)(2,1)S(1)}, u32[]{:S(2)}, u32[]{:S(2)}) async-start(bf16[16,16,256]{2,1,0:T(8,128)(2,1)} %bitcast_select_fusion), calls=%async_computation | async-start | bytes 262144 | tf_op jit(solution)/shard_map/all_to_all | solution.py:487
  18.9 0.7 copy-start.11
  21.4 0.7 copy-start.9
  21.4 0.7 copy-start.10
  22.1 29.6 %copy-start.4 = (bf16[128,256]{1,0:T(8,128)(2,1)S(1)}, bf16[128,256]{1,0:T(8,128)(2,1)}, u32[]{:S(2)}) copy-start(bf16[128,256]{1,0:T(8,128)(2,1)} %constant.45.clone.left_b_ref) | copy-start | bytes 196612
  22.2 29.5 %copy-start = (bf16[256,256]{1,0:T(8,128)(2,1)S(1)}, bf16[256,256]{1,0:T(8,128)(2,1)}, u32[]{:S(2)}) copy-start(bf16[256,256]{1,0:T(8,128)(2,1)} %constant.42.clone.right_a_ref) | copy-start | bytes 393220
  22.2 29.5 %copy-start.1 = (bf16[256,256]{1,0:T(8,128)(2,1)S(1)}, bf16[256,256]{1,0:T(8,128)(2,1)}, u32[]{:S(2)}) copy-start(bf16[256,256]{1,0:T(8,128)(2,1)} %constant.44.clone.left_a_ref) | copy-start | bytes 393220
  22.2 29.5 %copy-start.2 = (f32[128,128]{1,0:T(8,128)S(1)}, f32[128,128]{1,0:T(8,128)}, u32[]{:S(2)}) copy-start(f32[128,128]{1,0:T(8,128)} %constant.40.clone.square_ref) | copy-start | bytes 196612
  22.2 29.5 %copy-start.3 = (bf16[256,128]{1,0:T(8,128)(2,1)S(1)}, bf16[256,128]{1,0:T(8,128)(2,1)}, u32[]{:S(2)}) copy-start(bf16[256,128]{1,0:T(8,128)(2,1)} %constant.43.clone.right_b_ref) | copy-start | bytes 196612
  26.9 24.9 %copy-start.5 = (f32[128]{0:T(128)S(1)}, f32[128]{0:T(128)}, u32[]{:S(2)}) copy-start(f32[128]{0:T(128)} %constant.41.clone.y_square_ref) | copy-start | bytes 1540
  273.6 26.6 %all-to-all-start.1 = ((f32[16,4,16,256]{3,2,1,0:T(8,128)}), f32[16,4,16,256]{3,2,1,0:T(8,128)S(1)}, u32[]{:S(2)}, u32[]{:S(2)}) async-start(f32[16,4,16,256]{3,2,1,0:T(8,128)} %channel.1), calls=%async_computation.1 | async-start | bytes 2097152 | tf_op jit(solution)/shard_map/all_to_all | solution.py:526
Sparse Core Ops, SparseCore 0:
  10.7 40.9 all-gather.2

commit v2 on v1

--- a/solution.py
+++ b/solution.py
@@ -250,7 +250,7 @@
     angles = (points[:, None] * points[None, :] % length) * (2.0 * math.pi / length)
     left = (np.cos(angles) + np.sin(angles)).astype(np.float32)
     terms = []
-    for _ in range(3):
+    for _ in range(2):
         term = left.astype(jnp.bfloat16)
         terms.append(term)
         left = left - term.astype(np.float32)
@@ -258,38 +258,29 @@
 
 
 def split(values):
-    terms = []
-    for _ in range(3):
-        term = values.astype(jnp.bfloat16)
-        terms.append(term)
-        values = values - term.astype(jnp.float32)
-    return terms
+    first = values.astype(jnp.bfloat16)
+    return first, (values - first.astype(jnp.float32)).astype(jnp.bfloat16)
 
 
 def dot32(a, b, contract_b=0):
     return lax.dot_general(a, b, (((1,), (contract_b,)), ((), ())), preferred_element_type=jnp.float32)
 
 
-def cas_lanes(values, right_a, right_b):
-    first, second, third = split(values)
-    wide = dot32(jnp.concatenate([first, second], axis=1), right_a)
-    rest = dot32(jnp.concatenate([first, third], axis=1), right_b)
+def cas_lanes(values, right):
+    sums = dot32(jnp.concatenate(split(values), axis=1), right)
     length = values.shape[1]
-    return wide[:, :length] + (wide[:, length:] + rest)
-
-
-def cas_rows(values, left_a, left_b):
-    first, second, third = split(values)
-    wide = dot32(left_a, jnp.concatenate([first, second], axis=0))
-    rest = dot32(left_b, jnp.concatenate([first, third], axis=0))
-    length = values.shape[0]
-    return wide[:length] + (wide[length:] + rest)
+    return sums[:, :length] + sums[:, length:]
+
+
+def cas_rows(values, left):
+    first, second = split(values)
+    return dot32(left, jnp.concatenate([first, second, first], axis=0))
 
 
 def channel_kernel(
     geometry_ref, charge_ref, pair_ref, square_ref, gain_ref, y_square_ref,
-    right_a_ref, right_b_ref, left_a_ref, left_b_ref, out_ref,
-    grid_ref, turned_ref, spline_ref, place_ref,
+    right_ref, left_ref, out_ref,
+    grid_ref, turned_ref, window_ref, spline_ref, place_ref,
 ):
     slabs, _, blocks, capacity = geometry_ref.shape
     planes = MESH_X // slabs
@@ -308,9 +299,13 @@
         place_ref[3, span, :] = packed >> 9
         for dimension in range(3):
             weights, slopes = spline_lists(geometry_ref[slab, dimension], ORDER)
-            for position in range(ORDER):
-                spline_ref[dimension * 2 * ORDER + position, span, :] = weights[position]
-                spline_ref[(dimension * 2 + 1) * ORDER + position, span, :] = slopes[position]
+            for kind, values in enumerate((weights, slopes)):
+                for position in range(8):
+                    value = values[position] if position < ORDER else jnp.zeros_like(values[0])
+                    for half in range(capacity // 128):
+                        spline_ref[
+                            2 * dimension + kind, half, pl.ds(slab * blocks * 8 + position, blocks, stride=8), :
+                        ] = value[:, half * 128 : (half + 1) * 128]
         return carry
 
     lax.fori_loop(0, slabs, prepare, 0)
@@ -320,48 +315,57 @@
         return carry
 
     lax.fori_loop(0, far, clear, 0)
-    points = lax.broadcasted_iota(jnp.int32, (frame, capacity), 0)
-
-    def local_table(dimension, block, kinds):
-        distance = points - place_ref[dimension, pl.ds(block, 1), :]
-        matches = [distance == position for position in range(ORDER)]
+    points = lax.broadcasted_iota(jnp.int32, (8, capacity), 0)
+
+    def row_of(dimension, block):
+        return jnp.broadcast_to(place_ref[dimension, pl.ds(block, 1), :], (8, capacity))
+
+    def cyclic_tables(dimension, block, kinds):
+        base = row_of(dimension, block)
+        index = (points - base) & 7
+        span = pl.ds(pl.multiple_of(block * 8, 8), 8)
         tables = []
         for kind in kinds:
-            table = jnp.zeros((frame, capacity), jnp.float32)
-            for position in range(ORDER):
-                row = spline_ref[(dimension * 2 + kind) * ORDER + position, pl.ds(block, 1), :]
-                table = jnp.where(matches[position], row, table)
-            tables.append(table)
-        return tables
+            values = jnp.concatenate(
+                [spline_ref[2 * dimension + kind, half, span, :] for half in range(capacity // 128)], axis=1
+            )
+            tables.append(jnp.take_along_axis(values, index, axis=0, mode="promise_in_bounds"))
+        return base, points >= base, tables
 
     def z_tables(block, kinds):
-        tables = local_table(2, block, kinds)
-        tile = jnp.broadcast_to(place_ref[3, pl.ds(block, 1), :], (8, capacity))
-        here = [tile == index for index in range(MESH_Z // 8)]
+        unused, own, tables = cyclic_tables(2, block, kinds)
+        tile = row_of(3, block)
+        tile = jnp.where(own, tile, (tile + 1) & (MESH_Z // 8 - 1)).astype(jnp.float32)
+        tile = jnp.concatenate([tile, tile - 1.0], axis=0).astype(jnp.bfloat16)
+        here = [tile == jnp.bfloat16(2 * index) for index in range(MESH_Z // 16)]
         results = []
         for table in tables:
-            low, high = table[:8], table[8:]
-            pieces = [
-                jnp.where(here[index], low, jnp.where(here[index - 1], high, 0.0))
-                for index in range(MESH_Z // 8)
-            ]
-            results.append(jnp.concatenate(pieces, axis=0).astype(jnp.bfloat16))
+            twice = jnp.concatenate([table, table], axis=0).astype(jnp.bfloat16)
+            results.append(
+                jnp.concatenate([jnp.where(mask, twice, jnp.zeros_like(twice)) for mask in here], axis=0)
+            )
         return results
 
     def spread(slab, block):
         place = slab * blocks + block
-        (x_table,) = local_table(0, place, (0,))
-        (y_table,) = local_table(1, place, (0,))
+        x_base, unused, (x_table,) = cyclic_tables(0, place, (0,))
+        unused, y_own, (y_table,) = cyclic_tables(1, place, (0,))
         (z_table,) = z_tables(place, (0,))
-        charge = charge_ref[slab, pl.ds(block, 1), :]
-        products = jnp.concatenate(
-            [
-                ((x_table[index : index + 1] * y_table) * charge).astype(jnp.bfloat16)
-                for index in range(extent)
-            ],
-            axis=0,
-        )
-        sums = dot32(products, z_table, 1)
+        charge = jnp.broadcast_to(charge_ref[slab, pl.ds(block, 1), :], (8, capacity))
+        x_place = jnp.concatenate([x_base, x_base], axis=0).astype(jnp.float32).astype(jnp.bfloat16)
+        low, high = [], []
+        for index in range(planes):
+            product = (x_table[index : index + 1] * y_table) * charge
+            pair = jnp.concatenate(
+                [jnp.where(y_own, product, 0.0), jnp.where(y_own, 0.0, product)], axis=0
+            ).astype(jnp.bfloat16)
+            if index < border:
+                own = x_place <= jnp.bfloat16(index)
+                low.append(jnp.where(own, pair, jnp.zeros_like(pair)))
+                high.append(jnp.where(own, jnp.zeros_like(pair), pair))
+            else:
+                low.append(pair)
+        sums = dot32(jnp.concatenate(low + high, axis=0), z_table, 1)
         row_span = pl.ds(pl.multiple_of(block * rows, rows), frame)
         for index in range(extent):
             grid_ref[slab * planes + index, row_span, :] += sums[index * frame : (index + 1) * frame]
@@ -370,13 +374,12 @@
         spread(step // blocks, step % blocks)
         return carry
 
-    lax.fori_loop(0, slabs * blocks, spread_step, 0)
+    lax.fori_loop(0, slabs * blocks, spread_step, 0, unroll=16)
 
     for index in range(border):
         grid_ref[index] += grid_ref[MESH_X + index]
 
-    right_a, right_b = right_a_ref[...], right_b_ref[...]
-    left_a, left_b = left_a_ref[...], left_b_ref[...]
+    right, left = right_ref[...], left_ref[...]
 
     def forward(step, carry):
         both = []
@@ -384,9 +387,9 @@
             plane = 2 * step + index
             both.append(grid_ref[plane, 0:8, :] + grid_ref[plane, MESH_Y : MESH_Y + 8, :])
             both.append(grid_ref[plane, 8:MESH_Y, :])
-        along_z = cas_lanes(jnp.concatenate(both, axis=0), right_a, right_b)
+        along_z = cas_lanes(jnp.concatenate(both, axis=0), right)
         along_y = cas_rows(
-            jnp.concatenate([along_z[:MESH_Y], along_z[MESH_Y:]], axis=1), left_a, left_b
+            jnp.concatenate([along_z[:MESH_Y], along_z[MESH_Y:]], axis=1), left
         )
         for index in range(2):
             turned_ref[pl.ds(2 * step + index, MESH_Y, stride=MESH_X), :] = along_y[
@@ -394,64 +397,74 @@
             ]
         return carry
 
-    lax.fori_loop(0, MESH_X // 2, forward, 0)
+    lax.fori_loop(0, MESH_X // 2, forward, 0, unroll=16)
 
     def filtering(step, carry):
         spans = [pl.ds(pl.multiple_of((2 * step + index) * MESH_X, MESH_X), MESH_X) for index in range(2)]
         lines = jnp.concatenate([turned_ref[span, :] for span in spans], axis=1)
-        spectrum = cas_rows(lines, left_a, left_b)
+        spectrum = cas_rows(lines, left)
         filters = []
         for index in range(2):
             total = square_ref[...] + y_square_ref[2 * step + index]
             positive = total > 0
             safe = jnp.where(positive, total, 1.0)
             filters.append(jnp.where(positive, pair_ref[...] * gain_ref[2 * step + index] / safe, 0.0))
-        lines = cas_rows(spectrum * jnp.concatenate(filters, axis=1), left_a, left_b)
+        lines = cas_rows(spectrum * jnp.concatenate(filters, axis=1), left)
         for index, span in enumerate(spans):
             turned_ref[span, :] = lines[:, index * MESH_Z : (index + 1) * MESH_Z]
         return carry
 
-    lax.fori_loop(0, MESH_Y // 2, filtering, 0)
+    lax.fori_loop(0, MESH_Y // 2, filtering, 0, unroll=16)
 
     def backward(step, carry):
         both = jnp.concatenate(
             [turned_ref[pl.ds(2 * step + index, MESH_Y, stride=MESH_X), :] for index in range(2)], axis=1
         )
-        along_y = cas_rows(both, left_a, left_b)
+        along_y = cas_rows(both, left)
         field = cas_lanes(
-            jnp.concatenate([along_y[:, :MESH_Z], along_y[:, MESH_Z:]], axis=0), right_a, right_b
-        )
-        rounded = field.astype(jnp.bfloat16).astype(jnp.float32)
+            jnp.concatenate([along_y[:, :MESH_Z], along_y[:, MESH_Z:]], axis=0), right
+        )
         for index in range(2):
-            grid_ref[2 * step + index, 0:MESH_Y, :] = rounded[index * MESH_Y : (index + 1) * MESH_Y]
-            grid_ref[2 * step + index, MESH_Y : MESH_Y + 8, :] = rounded[index * MESH_Y : index * MESH_Y + 8]
-        return carry
-
-    lax.fori_loop(0, MESH_X // 2, backward, 0)
+            plane = field[index * MESH_Y : (index + 1) * MESH_Y]
+            plane = jnp.concatenate([plane, plane[:8]], axis=0)
+            for block in range(blocks):
+                window_ref[2 * step + index, block] = plane[block * rows : block * rows + frame].astype(jnp.bfloat16)
+        return carry
+
+    lax.fori_loop(0, MESH_X // 2, backward, 0, unroll=16)
 
     for index in range(border):
-        grid_ref[MESH_X + index] = grid_ref[index]
+        window_ref[MESH_X + index] = window_ref[index]
 
     def gather(slab, block):
         place = slab * blocks + block
-        x_table, x_slope = local_table(0, place, (0, 1))
-        y_table, y_slope = local_table(1, place, (0, 1))
+        x_base, unused, (x_table, x_slope) = cyclic_tables(0, place, (0, 1))
+        unused, y_own, (y_table, y_slope) = cyclic_tables(1, place, (0, 1))
         z_table, z_slope = z_tables(place, (0, 1))
         charge = charge_ref[slab, pl.ds(block, 1), :]
-        row_span = pl.ds(pl.multiple_of(block * rows, rows), frame)
         window = jnp.concatenate(
-            [grid_ref[slab * planes + index, row_span, :] for index in range(extent)], axis=0
-        ).astype(jnp.bfloat16)
+            [window_ref[slab * planes + index, block] for index in range(extent)], axis=0
+        )
+
+        def chosen(near, index, own):
+            def rows_of(plane):
+                return jnp.where(
+                    y_own, near[plane * frame : plane * frame + 8], near[plane * frame + 8 : plane * frame + 16]
+                )
+
+            if index < border:
+                return jnp.where(own, rows_of(index), rows_of(planes + index))
+            return rows_of(index)
+
         near = dot32(window, z_table)
         near_z = dot32(window, z_slope)
-        plain = jnp.zeros((frame, capacity), jnp.float32)
-        sloped = jnp.zeros((frame, capacity), jnp.float32)
-        plain_z = jnp.zeros((frame, capacity), jnp.float32)
-        for index in range(extent):
-            part = near[index * frame : (index + 1) * frame]
+        plain = sloped = plain_z = 0.0
+        for index in range(planes):
+            own = x_base <= index
+            part = chosen(near, index, own)
             plain += x_table[index : index + 1] * part
             sloped += x_slope[index : index + 1] * part
-            plain_z += x_table[index : index + 1] * near_z[index * frame : (index + 1) * frame]
+            plain_z += x_table[index : index + 1] * chosen(near_z, index, own)
         row = pl.ds(block, 1)
         out_ref[slab, 0, row, :] = jnp.sum(y_table * plain, axis=0, keepdims=True)
         out_ref[slab, 1, row, :] = -charge * jnp.sum(y_table * sloped, axis=0, keepdims=True)
@@ -462,7 +475,7 @@
         gather(step // blocks, step % blocks)
         return carry
 
-    lax.fori_loop(0, slabs * blocks, gather_step, 0)
+    lax.fori_loop(0, slabs * blocks, gather_step, 0, unroll=16)
 
 
 def channel_shards(charges, cell_offset, base_cell, counts, widths):
@@ -497,31 +510,29 @@
     scale = 2.0 / (math.pi * MESH_X * MESH_Y * MESH_Z)
     pairs = gains[:, None] * (gains * scale)[None, :]
     pair_squares = squares[:, None] + squares[None, :]
-    one, two, three = cas_terms(MESH_X)
-    right_a = np.concatenate([np.concatenate([one, two], axis=1)] * 2, axis=0)
-    right_b = np.concatenate([three, one], axis=0)
-    left_a = np.concatenate([np.concatenate([one, one], axis=1), np.concatenate([two, two], axis=1)], axis=0)
-    left_b = np.concatenate([three, one], axis=1)
+    one, two = cas_terms(MESH_X)
+    right = np.concatenate([np.concatenate([one, two], axis=1)] * 2, axis=0)
+    left = np.concatenate([one, one, two], axis=1)
 
     whole = pl.BlockSpec(memory_space=pltpu.VMEM)
     scalars = pl.BlockSpec(memory_space=pltpu.SMEM)
     result = pl.pallas_call(
         channel_kernel,
         out_shape=jax.ShapeDtypeStruct((slabs, 4, blocks, capacity), jnp.float32),
-        in_specs=[whole] * 4 + [scalars] * 2 + [whole] * 4,
+        in_specs=[whole] * 4 + [scalars] * 2 + [whole] * 2,
         out_specs=whole,
         scratch_shapes=[
             pltpu.VMEM((MESH_X + ORDER - 1, MESH_Y + 8, MESH_Z), jnp.float32),
             pltpu.VMEM((MESH_X * MESH_Y, MESH_Z), jnp.float32),
-            pltpu.VMEM((6 * ORDER, slabs * blocks, capacity), jnp.float32),
+            pltpu.VMEM((MESH_X + ORDER - 1, blocks, 16, MESH_Z), jnp.bfloat16),
+            pltpu.VMEM((6, capacity // 128, slabs * blocks * 8, 128), jnp.float32),
             pltpu.VMEM((4, slabs * blocks, capacity), jnp.int32),
         ],
         compiler_params=pltpu.CompilerParams(vmem_limit_bytes=52 * 1024 * 1024),
         name="channel",
     )(
         geometry, charge_blocks.astype(jnp.float32), pairs, jnp.asarray(pair_squares), gains,
-        jnp.asarray(squares), jnp.asarray(right_a), jnp.asarray(right_b), jnp.asarray(left_a),
-        jnp.asarray(left_b),
+        jnp.asarray(squares), jnp.asarray(right), jnp.asarray(left),
     )
     returned = lax.all_to_all(result, "wide", split_axis=0, concat_axis=0, tiled=True)
     atom_potential = jnp.where(live_mask[None], returned[:, 0], 0.0).reshape(channels, slot_count)

time: 310 us -> 148 us (0.48)
  Pallas kernels: 222 us -> 59.9 us
    pallas_call x1, Pallas kernels: 222 us -> 59.9 us  [channel_shards(): pl.pallas_call(channel_kernel, out_shape=jax.ShapeDtypeStruct((slabs, 4,...]
where the time goes in v2:
time: 148 us; the launch traced here: 147 us
  Pallas kernels  59.9 us (40%)
  waiting for transfers between devices  52.2 us (35%)
  between operations  15.5 us (10%)
  starting transfers between devices  11.1 us (8%)
  local copies, waits for them, and re-layouts  4.55 us (3%)
  other arithmetic  3.47 us (2%)
    pallas_call x1, Pallas kernels, channel_shards(): pl.pallas_call(channel_kernel, out_shape=jax.ShapeDtypeStruct((slabs, 4,...  59.9 us
    all_gather x1, waiting for transfers between devices, channel_shards(): geometry = lax.all_gather(geometry, 'wide', axis=0, tiled=False)  24.8 us
    all_to_all x1, waiting for transfers between devices, channel_shards(): lax.all_to_all(result, 'wide', split_axis=0, concat_axis=0, tiled=True)  22.8 us
    all_to_all x1, starting transfers between devices, channel_shards(): lax.all_to_all(charge_blocks, 'wide', split_axis=0, concat_axis=0, tiled=...  7.39 us
    all_to_all x1, waiting for transfers between devices, channel_shards(): lax.all_to_all(charge_blocks, 'wide', split_axis=0, concat_axis=0, tiled=...  4.57 us
    unnamed x26, local copies, waits for them, and re-layouts  3.79 us
    all_to_all x1, starting transfers between devices, channel_shards(): lax.all_to_all(result, 'wide', split_axis=0, concat_axis=0, tiled=True)  3.65 us
  transfers between devices with their start and end apart: 3, of which 3 were waited for; matrix products, arithmetic and copies ran while one was open for 1% of the time, Pallas kernels for 0%

profile of v2, /device:TPU:0, one launch (start us, length us, event | category | flops | bytes accessed | tf_op | source)
XLA Modules:
  0.0 146.7 jit_solution(13032573801026887921)
XLA Ops:
  7.2 0.0 all-gather.3.cloned.1.call-start
  7.2 1.1 slice_reduce_fusion.1
  8.4 0.8 copy-done.5
  9.2 0.1 add_convert_fusion
  9.3 0.6 pad_maximum_fusion
  9.9 0.2 copy-done.4
  10.1 0.6 copy-done.6
  10.7 0.1 iota_compare_fusion
  10.8 0.7 bitcast_select_fusion
  11.5 7.4 %all-to-all-start = ((bf16[16,16,256]{2,1,0:T(8,128)(2,1)}), bf16[16,16,256]{2,1,0:T(8,128)(2,1)S(1)}, u32[]{:S(2)}, u32[]{:S(2)}) async-start(bf16[16,16,256]{2,1,0:T(8,128)(2,1)} %bitcast_select_fusion), calls=%async_computation | async-start | bytes 262144 | tf_op jit(solution)/shard_map/all_to_all | solution.py:500
  18.9 0.6 copy-done.9
  19.5 0.6 dynamic_slice.4
  21.5 0.6 copy-done.7
  22.1 0.1 broadcast_multiply_fusion.pair_ref
  22.3 4.6 %all-to-all-done = bf16[16,16,256]{2,1,0:T(8,128)(2,1)S(1)} async-done(((bf16[16,16,256]{2,1,0:T(8,128)(2,1)}), bf16[16,16,256]{2,1,0:T(8,128)(2,1)S(1)}, u32[]{:S(2)}, u32[]{:S(2)}) %all-to-all-start) | async-done | bytes 131104 | tf_op jit(solution)/shard_map/all_to_all | solution.py:500
  26.9 24.8 %all-gather.3.cloned.1.call-done = f32[64,16,256]{2,1,0:T(8,128)} async-done(((f32[4,16,256]{2,1,0:T(8,128)}), f32[64,16,256]{2,1,0:T(8,128)}) %all-gather.3.cloned.1.call-update) | async-done | bytes 1048592 | tf_op jit(solution)/shard_map/all_gather | solution.py:499
  51.7 59.9 %channel.1 = f32[16,4,16,256]{3,2,1,0:T(8,128)} custom-call(f32[16,4,16,256]{3,2,1,0:T(8,128)} %bitcast.18, f32[16,16,256]{2,1,0:T(8,128)S(1)} %convert_element_type.14.charge_ref, f32[128,128]{1,0:T(8,128)S(1)} %broadcast_multiply_fusion.pair_ref, f32[128,128]{1,0:T(8,128)S(1)} %copy-done.2, f32[128]{0:T(128)S(1)} %get-tuple-element.6.gain_ref, ...), custom_call_target="tpu_custom_call" | custom-call | tf_op jit(solution)/shard_map/channel/pallas_call | solution.py:519
  111.6 3.7 %all-to-all-start.1 = ((f32[16,4,16,256]{3,2,1,0:T(8,128)}), f32[16,4,16,256]{3,2,1,0:T(8,128)S(1)}, u32[]{:S(2)}, u32[]{:S(2)}) async-start(f32[16,4,16,256]{3,2,1,0:T(8,128)} %channel.1), calls=%async_computation.1 | async-start | bytes 2097152 | tf_op jit(solution)/shard_map/all_to_all | solution.py:537
  115.3 0.1 lt.34
  115.4 22.8 %all-to-all-done.1 = f32[16,4,16,256]{3,2,1,0:T(8,128)S(1)} async-done(((f32[16,4,16,256]{3,2,1,0:T(8,128)}), f32[16,4,16,256]{3,2,1,0:T(8,128)S(1)}, u32[]{:S(2)}, u32[]{:S(2)}) %all-to-all-start.1) | async-done | bytes 1048608 | tf_op jit(solution)/shard_map/all_to_all | solution.py:537
  138.2 0.2 copy.16
  138.4 0.1 slice_reduce_fusion
  138.4 0.7 copy.17
  139.1 0.7 broadcast_select_fusion
  (28 shorter events, 0.2 us)
Async XLA Ops:
  7.2 44.5 %all-gather.3.cloned.1.call-start = ((), (), s32[]{:S(2)}) async-start(), calls=%async_computation.2 | async-start | bytes 1114112 | tf_op jit(solution)/shard_map/all_gather | solution.py:499
  8.3 0.8 copy-start.5
  9.2 0.9 copy-start.4
  10.1 0.7 copy-start.6
  11.5 15.3 %all-to-all-start = ((bf16[16,16,256]{2,1,0:T(8,128)(2,1)}), bf16[16,16,256]{2,1,0:T(8,128)(2,1)S(1)}, u32[]{:S(2)}, u32[]{:S(2)}) async-start(bf16[16,16,256]{2,1,0:T(8,128)(2,1)} %bitcast_select_fusion), calls=%async_computation | async-start | bytes 262144 | tf_op jit(solution)/shard_map/all_to_all | solution.py:500
  18.9 0.7 copy-start.9
  21.4 0.7 copy-start.7
  21.4 0.7 copy-start.8
  22.2 29.5 %copy-start = (bf16[256,256]{1,0:T(8,128)(2,1)S(1)}, bf16[256,256]{1,0:T(8,128)(2,1)}, u32[]{:S(2)}) copy-start(bf16[256,256]{1,0:T(8,128)(2,1)} %constant.38.clone.right_ref) | copy-start | bytes 393220
  22.2 29.5 %copy-start.1 = (bf16[128,384]{1,0:T(8,128)(2,1)S(1)}, bf16[128,384]{1,0:T(8,128)(2,1)}, u32[]{:S(2)}) copy-start(bf16[128,384]{1,0:T(8,128)(2,1)} %constant.39.clone.left_ref) | copy-start | bytes 294916
  22.2 29.5 %copy-start.2 = (f32[128,128]{1,0:T(8,128)S(1)}, f32[128,128]{1,0:T(8,128)}, u32[]{:S(2)}) copy-start(f32[128,128]{1,0:T(8,128)} %constant.36.clone.square_ref) | copy-start | bytes 196612
  26.9 24.9 %copy-start.3 = (f32[128]{0:T(128)S(1)}, f32[128]{0:T(128)}, u32[]{:S(2)}) copy-start(f32[128]{0:T(128)} %constant.37.clone.y_square_ref) | copy-start | bytes 1540
  111.6 26.6 %all-to-all-start.1 = ((f32[16,4,16,256]{3,2,1,0:T(8,128)}), f32[16,4,16,256]{3,2,1,0:T(8,128)S(1)}, u32[]{:S(2)}, u32[]{:S(2)}) async-start(f32[16,4,16,256]{3,2,1,0:T(8,128)} %channel.1), calls=%async_computation.1 | async-start | bytes 2097152 | tf_op jit(solution)/shard_map/all_to_all | solution.py:537
Sparse Core Ops, SparseCore 0:
  10.7 40.9 all-gather.2

commit v3 on v2

--- a/solution.py
+++ b/solution.py
@@ -278,11 +278,11 @@
 
 
 def channel_kernel(
-    geometry_ref, charge_ref, pair_ref, square_ref, gain_ref, y_square_ref,
+    offset_ref, base_ref, charge_ref, pair_ref, square_ref, order_ref, gain_ref, y_square_ref,
     right_ref, left_ref, out_ref,
     grid_ref, turned_ref, window_ref, spline_ref, place_ref,
 ):
-    slabs, _, blocks, capacity = geometry_ref.shape
+    slabs, _, blocks, capacity = offset_ref.shape
     planes = MESH_X // slabs
     rows = MESH_Y // blocks
     border = ORDER - 1
@@ -291,14 +291,14 @@
     far = MESH_X + border
 
     def prepare(slab, carry):
-        packed = geometry_ref[slab, 3].astype(jnp.int32)
         span = pl.ds(pl.multiple_of(slab * blocks, blocks), blocks)
-        place_ref[0, span, :] = packed & 7
-        place_ref[1, span, :] = (packed >> 3) & 7
-        place_ref[2, span, :] = (packed >> 6) & 7
-        place_ref[3, span, :] = packed >> 9
+        z_base = base_ref[slab, 2].astype(jnp.float32).astype(jnp.int32)
+        for dimension in range(2):
+            place_ref[dimension, span, :] = base_ref[slab, dimension].astype(jnp.float32).astype(jnp.int32)
+        place_ref[2, span, :] = z_base & 7
+        place_ref[3, span, :] = z_base >> 3
         for dimension in range(3):
-            weights, slopes = spline_lists(geometry_ref[slab, dimension], ORDER)
+            weights, slopes = spline_lists(offset_ref[slab, dimension], ORDER)
             for kind, values in enumerate((weights, slopes)):
                 for position in range(8):
                     value = values[position] if position < ORDER else jnp.zeros_like(values[0])
@@ -346,12 +346,13 @@
             )
         return results
 
-    def spread(slab, block):
-        place = slab * blocks + block
+    def spread(turn_index, block):
+        place = turn_index * blocks + block
+        slab = order_ref[turn_index]
         x_base, unused, (x_table,) = cyclic_tables(0, place, (0,))
         unused, y_own, (y_table,) = cyclic_tables(1, place, (0,))
         (z_table,) = z_tables(place, (0,))
-        charge = jnp.broadcast_to(charge_ref[slab, pl.ds(block, 1), :], (8, capacity))
+        charge = jnp.broadcast_to(charge_ref[turn_index, pl.ds(block, 1), :], (8, capacity))
         x_place = jnp.concatenate([x_base, x_base], axis=0).astype(jnp.float32).astype(jnp.bfloat16)
         low, high = [], []
         for index in range(planes):
@@ -436,12 +437,13 @@
     for index in range(border):
         window_ref[MESH_X + index] = window_ref[index]
 
-    def gather(slab, block):
-        place = slab * blocks + block
+    def gather(turn_index, block):
+        place = turn_index * blocks + block
+        slab = order_ref[turn_index]
         x_base, unused, (x_table, x_slope) = cyclic_tables(0, place, (0, 1))
         unused, y_own, (y_table, y_slope) = cyclic_tables(1, place, (0, 1))
         z_table, z_slope = z_tables(place, (0, 1))
-        charge = charge_ref[slab, pl.ds(block, 1), :]
+        charge = charge_ref[turn_index, pl.ds(block, 1), :]
         window = jnp.concatenate(
             [window_ref[slab * planes + index, block] for index in range(extent)], axis=0
         )
@@ -492,12 +494,27 @@
     )
     bases = base_cell.reshape(3, blocks, capacity)
     row_start = jnp.arange(blocks, dtype=jnp.int32)[:, None] * block_rows
-    packed = (bases[0] - device * planes) + 8 * (bases[1] - row_start) + 64 * bases[2]
-    geometry = jnp.concatenate(
-        [cell_offset.reshape(3, blocks, capacity), packed.astype(jnp.float32)[None]], axis=0
-    )
-    geometry = lax.all_gather(geometry, "wide", axis=0, tiled=False)
-    charge_blocks = lax.all_to_all(charge_blocks, "wide", split_axis=0, concat_axis=0, tiled=True)
+    cells = jnp.stack([bases[0] - device * planes, bases[1] - row_start, bases[2]]).astype(jnp.bfloat16)
+    offsets = cell_offset.reshape(1, 3, blocks, capacity)
+    cells = cells[None]
+    parts = charge_blocks[None]
+    order = jnp.zeros((1,), jnp.int32)
+    distance = slabs // 2
+    while distance > 0:
+        route = [(index, index ^ distance) for index in range(slabs)]
+        upper = (device & distance) > 0
+        first, second = parts[:, :distance], parts[:, distance:]
+        kept, sent = jnp.where(upper, second, first), jnp.where(upper, first, second)
+        offsets = jnp.concatenate([offsets, lax.ppermute(offsets, "wide", route)], axis=0)
+        count = cells.shape[0]
+        bundle = jnp.concatenate([cells.reshape((-1,) + cells.shape[2:]), sent.reshape((-1,) + sent.shape[2:])], axis=0)
+        bundle = lax.ppermute(bundle, "wide", route)
+        cells = jnp.concatenate([cells, bundle[: 3 * count].reshape(cells.shape)], axis=0)
+        parts = jnp.concatenate([kept, bundle[3 * count :].reshape(kept.shape)], axis=0)
+        order = jnp.concatenate([order, order ^ distance])
+        distance //= 2
+    charge_blocks = parts[:, 0]
+    order = order ^ device
 
     width = lax.dynamic_index_in_dim(widths, device, keepdims=False)
     points = np.arange(MESH_X)
@@ -519,7 +536,7 @@
     result = pl.pallas_call(
         channel_kernel,
         out_shape=jax.ShapeDtypeStruct((slabs, 4, blocks, capacity), jnp.float32),
-        in_specs=[whole] * 4 + [scalars] * 2 + [whole] * 2,
+        in_specs=[whole] * 5 + [scalars] * 3 + [whole] * 2,
         out_specs=whole,
         scratch_shapes=[
             pltpu.VMEM((MESH_X + ORDER - 1, MESH_Y + 8, MESH_Z), jnp.float32),
@@ -531,7 +548,7 @@
         compiler_params=pltpu.CompilerParams(vmem_limit_bytes=52 * 1024 * 1024),
         name="channel",
     )(
-        geometry, charge_blocks.astype(jnp.float32), pairs, jnp.asarray(pair_squares), gains,
+        offsets, cells, charge_blocks.astype(jnp.float32), pairs, jnp.asarray(pair_squares), order, gains,
         jnp.asarray(squares), jnp.asarray(right), jnp.asarray(left),
     )
     returned = lax.all_to_all(result, "wide", split_axis=0, concat_axis=0, tiled=True)

time: 148 us -> 120 us (0.81)
  waiting for transfers between devices: 52.2 us -> 32.8 us
  between operations: 15.5 us -> 2.4 us
  starting transfers between devices: 11.1 us -> 17.1 us
  other arithmetic: 3.47 us -> 1.52 us
    all_gather x1 -> x0, waiting for transfers between devices: 24.8 us -> none  [channel_shards(): geometry = lax.all_gather(geometry, 'wide', axis=0, tiled=False)]
    ppermute x0 -> x8, starting transfers between devices: none -> 10.3 us  [the longest x4 8.47 us: channel_shards(): lax.ppermute(offsets, 'wide', route)]
    ppermute x0 -> x8, waiting for transfers between devices: none -> 9.97 us  [the longest x4 7.46 us: channel_shards(): bundle = lax.ppermute(bundle, 'wide', route)]
    all_to_all x1 -> x0, starting transfers between devices: 7.39 us -> none  [channel_shards(): lax.all_to_all(charge_blocks, 'wide', split_axis=0, concat_axis=0, tiled=...]
    all_to_all x1 -> x0, waiting for transfers between devices: 4.57 us -> none  [channel_shards(): lax.all_to_all(charge_blocks, 'wide', split_axis=0, concat_axis=0, tiled=...]
    all_to_all x1, starting transfers between devices: 3.65 us -> 6.79 us  [channel_shards(): lax.all_to_all(result, 'wide', split_axis=0, concat_axis=0, tiled=True)]
    unnamed x26 -> x34, local copies, waits for them, and re-layouts: 3.79 us -> 4.23 us
  transfers between devices with their start and end apart: 3 -> 9, of which waited for: 3 -> 7; matrix products, arithmetic and copies ran while one was open for 1% -> 1% of each run, Pallas kernels for 0% -> 0%
where the time goes in v3:
time: 120 us; the launch traced here: 119 us
  Pallas kernels  59.9 us (50%)
  waiting for transfers between devices  32.8 us (27%)
  starting transfers between devices  17.1 us (14%)
  local copies, waits for them, and re-layouts  5.11 us (4%)
  between operations  2.4 us (2%)
  other arithmetic  1.52 us (1%)
    pallas_call x1, Pallas kernels, channel_shards(): pl.pallas_call(channel_kernel, out_shape=jax.ShapeDtypeStruct((slabs, 4,...  59.9 us
    all_to_all x1, waiting for transfers between devices, channel_shards(): lax.all_to_all(result, 'wide', split_axis=0, concat_axis=0, tiled=True)  22.8 us
    ppermute x4, starting transfers between devices, channel_shards(): lax.ppermute(offsets, 'wide', route)  8.47 us
    ppermute x4, waiting for transfers between devices, channel_shards(): bundle = lax.ppermute(bundle, 'wide', route)  7.46 us
    all_to_all x1, starting transfers between devices, channel_shards(): lax.all_to_all(result, 'wide', split_axis=0, concat_axis=0, tiled=True)  6.79 us
    unnamed x34, local copies, waits for them, and re-layouts  4.23 us
    ppermute x4, waiting for transfers between devices, channel_shards(): lax.ppermute(offsets, 'wide', route)  2.52 us
  transfers between devices with their start and end apart: 9, of which 7 were waited for; matrix products, arithmetic and copies ran while one was open for 1% of the time, Pallas kernels for 0%

profile of v3, /device:TPU:0, one launch (start us, length us, event | category | flops | bytes accessed | tf_op | source)
XLA Modules:
  0.0 118.8 jit_solution(5823997724086949757)
XLA Ops:
  0.6 0.9 constant_dynamic-update-slice_fusion.4
  1.5 4.1 %collective-permute-start = (f32[1,3,16,256]{3,2,1,0:T(8,128)S(1)}, f32[1,3,16,256]{3,2,1,0:T(8,128)S(1)}, u32[]{:S(2)}, u32[]{:S(2)}) collective-permute-start(f32[1,3,16,256]{3,2,1,0:T(8,128)S(1)} %get-tuple-element.7), channel_id=1, source_target_pairs={{0,8},{1,9},{2,10},{3,11},{4,12},{5,13},{6,14},{7,15},{8,0},{9,1},... | collective-permute-start | bytes 147464 | tf_op jit(solution)/shard_map/ppermute | solution.py:508
  5.7 0.1 convert_reduce_fusion.1
  5.8 0.6 copy-done.6
  7.0 0.6 copy-done.9
  7.6 0.6 dynamic_slice.4
  9.6 0.6 copy-done.7
  10.4 1.9 %collective-permute-start.1 = (f32[2,3,16,256]{3,2,1,0:T(8,128)S(1)}, f32[2,3,16,256]{3,2,1,0:T(8,128)S(1)}, u32[]{:S(2)}, u32[]{:S(2)}) collective-permute-start(f32[2,3,16,256]{3,2,1,0:T(8,128)S(1)} %pad_maximum_fusion.6), channel_id=1, source_target_pairs={{0,4},{1,5},{2,6},{3,7},{4,0},{5,1},{6,2},{7,3},{8,12},{9,13},{10,... | collective-permute-start | bytes 294920 | tf_op jit(solution)/shard_map/ppermute | solution.py:508
  12.3 1.6 %collective-permute-done.4 = bf16[11,16,256]{2,1,0:T(8,128)(2,1)S(1)} collective-permute-done((bf16[11,16,256]{2,1,0:T(8,128)(2,1)S(1)}, bf16[11,16,256]{2,1,0:T(8,128)(2,1)S(1)}, u32[]{:S(2)}, u32[]{:S(2)}) %collective-permute-start.4) | collective-permute-done | bytes 90144 | tf_op jit(solution)/shard_map/ppermute | solution.py:511
  14.1 2.1 %collective-permute-done.1 = f32[2,3,16,256]{3,2,1,0:T(8,128)S(1)} collective-permute-done((f32[2,3,16,256]{3,2,1,0:T(8,128)S(1)}, f32[2,3,16,256]{3,2,1,0:T(8,128)S(1)}, u32[]{:S(2)}, u32[]{:S(2)}) %collective-permute-start.1) | collective-permute-done | bytes 98336 | tf_op jit(solution)/shard_map/ppermute | solution.py:508
  16.2 1.9 %collective-permute-start.2 = (f32[4,3,16,256]{3,2,1,0:T(8,128)S(1)}, f32[4,3,16,256]{3,2,1,0:T(8,128)S(1)}, u32[]{:S(2)}, u32[]{:S(2)}) collective-permute-start(f32[4,3,16,256]{3,2,1,0:T(8,128)S(1)} %pad_maximum_fusion.2), channel_id=1, source_target_pairs={{0,2},{1,3},{2,0},{3,1},{4,6},{5,7},{6,4},{7,5},{8,10},{9,11},{10,... | collective-permute-start | bytes 589832 | tf_op jit(solution)/shard_map/ppermute | solution.py:508
  18.0 0.8 collective-permute-done.5
  18.9 1.6 %collective-permute-start.6 = (bf16[20,16,256]{2,1,0:T(8,128)(2,1)S(1)}, bf16[20,16,256]{2,1,0:T(8,128)(2,1)S(1)}, u32[]{:S(2)}, u32[]{:S(2)}) collective-permute-start(bf16[20,16,256]{2,1,0:T(8,128)(2,1)S(1)} %pad_maximum_fusion.4), channel_id=1, source_target_pairs={{0,2},{1,3},{2,0},{3,1},{4,6},{5,7},{6,4},{7,5},{8,10},{9,11},{10,... | collective-permute-start | bytes 491528 | tf_op jit(solution)/shard_map/ppermute | solution.py:511
  20.5 4.2 %collective-permute-done.6 = bf16[20,16,256]{2,1,0:T(8,128)(2,1)S(1)} collective-permute-done((bf16[20,16,256]{2,1,0:T(8,128)(2,1)S(1)}, bf16[20,16,256]{2,1,0:T(8,128)(2,1)S(1)}, u32[]{:S(2)}, u32[]{:S(2)}) %collective-permute-start.6) | collective-permute-done | bytes 163872 | tf_op jit(solution)/shard_map/ppermute | solution.py:511
  25.0 0.5 collective-permute-start.3
  25.6 0.9 collective-permute-done.7
  26.6 0.4 collective-permute-done.3
  27.1 0.4 copy-done
  27.5 59.9 %channel.1 = f32[16,4,16,256]{3,2,1,0:T(8,128)} custom-call(f32[16,3,16,256]{3,2,1,0:T(8,128)S(1)} %constant_dynamic-update-slice_fusion.offset_ref, bf16[16,3,16,256]{3,2,1,0:T(8,128)(2,1)S(1)} %constant_dynamic-update-slice_fusion.5.base_ref, f32[16,16,256]{2,1,0:T(8,128)S(1)} %fusion.charge_ref, f32[128,128]{1,0:T(8,128)S(1)} %broadcast_multiply_fusion.pair_ref, ...), custom_call_target="tpu_custom_call" | custom-call | tf_op jit(solution)/shard_map/channel/pallas_call | solution.py:536
  87.4 6.8 %all-to-all-start = ((f32[16,4,16,256]{3,2,1,0:T(8,128)}), f32[16,4,16,256]{3,2,1,0:T(8,128)S(1)}, u32[]{:S(2)}, u32[]{:S(2)}) async-start(f32[16,4,16,256]{3,2,1,0:T(8,128)} %channel.1), calls=%async_computation | async-start | bytes 2097152 | tf_op jit(solution)/shard_map/all_to_all | solution.py:554
  94.3 22.8 %all-to-all-done = f32[16,4,16,256]{3,2,1,0:T(8,128)S(1)} async-done(((f32[16,4,16,256]{3,2,1,0:T(8,128)}), f32[16,4,16,256]{3,2,1,0:T(8,128)S(1)}, u32[]{:S(2)}, u32[]{:S(2)}) %all-to-all-start) | async-done | bytes 1048608 | tf_op jit(solution)/shard_map/all_to_all | solution.py:554
  117.2 0.2 copy.22
  117.4 0.7 copy.23
  118.0 0.7 broadcast_select_fusion
  (78 shorter events, 1.4 us)
Async XLA Ops:
  0.6 5.0 %copy-start.5 = (s32[3,4096]{1,0:T(4,128)S(1)}, s32[3,4096]{1,0:T(4,128)}, u32[]{:S(2)}) copy-start(s32[3,4096]{1,0:T(4,128)} %param.13) | copy-start | bytes 147460
  0.6 5.9 %copy-start.4 = (bf16[16,4096]{1,0:T(8,128)(2,1)S(1)}, bf16[16,4096]{1,0:T(8,128)(2,1)}, u32[]{:S(2)}) copy-start(bf16[16,4096]{1,0:T(8,128)(2,1)} %param.11) | copy-start | bytes 393220
  1.5 8.8 %collective-permute-start = (f32[1,3,16,256]{3,2,1,0:T(8,128)S(1)}, f32[1,3,16,256]{3,2,1,0:T(8,128)S(1)}, u32[]{:S(2)}, u32[]{:S(2)}) collective-permute-start(f32[1,3,16,256]{3,2,1,0:T(8,128)S(1)} %get-tuple-element.7), channel_id=1, source_target_pairs={{0,8},{1,9},{2,10},{3,11},{4,12},{5,13},{6,14},{7,15},{8,0},{9,1},... | collective-permute-start | bytes 147464 | tf_op jit(solution)/shard_map/ppermute | solution.py:508
  5.8 0.7 copy-start.6
  6.8 7.1 %collective-permute-start.4 = (bf16[11,16,256]{2,1,0:T(8,128)(2,1)S(1)}, bf16[11,16,256]{2,1,0:T(8,128)(2,1)S(1)}, u32[]{:S(2)}, u32[]{:S(2)}) collective-permute-start(bf16[11,16,256]{2,1,0:T(8,128)(2,1)S(1)} %pad_maximum_fusion.8), channel_id=1, source_target_pairs={{0,8},{1,9},{2,10},{3,11},{4,12},{5,13},{6,14},{7,15},{8,0},{9,1},... | collective-permute-start | bytes 270344 | tf_op jit(solution)/shard_map/ppermute | solution.py:511
  6.9 0.7 copy-start.9
  8.2 1.3 %copy-start.10 = (s32[16]{0:T(128)S(1)}, s32[16]{0:T(128)}, u32[]{:S(2)}) copy-start(s32[16]{0:T(128)} %constant.15.clone.1) | copy-start | bytes 196
  9.5 0.7 copy-start.7
  9.5 0.7 copy-start.8
  10.4 5.8 %collective-permute-start.1 = (f32[2,3,16,256]{3,2,1,0:T(8,128)S(1)}, f32[2,3,16,256]{3,2,1,0:T(8,128)S(1)}, u32[]{:S(2)}, u32[]{:S(2)}) collective-permute-start(f32[2,3,16,256]{3,2,1,0:T(8,128)S(1)} %pad_maximum_fusion.6), channel_id=1, source_target_pairs={{0,4},{1,5},{2,6},{3,7},{4,0},{5,1},{6,2},{7,3},{8,12},{9,13},{10,... | collective-permute-start | bytes 294920 | tf_op jit(solution)/shard_map/ppermute | solution.py:508
  14.0 4.9 %collective-permute-start.5 = (bf16[14,16,256]{2,1,0:T(8,128)(2,1)S(1)}, bf16[14,16,256]{2,1,0:T(8,128)(2,1)S(1)}, u32[]{:S(2)}, u32[]{:S(2)}) collective-permute-start(bf16[14,16,256]{2,1,0:T(8,128)(2,1)S(1)} %pad_maximum_fusion.5), channel_id=1, source_target_pairs={{0,4},{1,5},{2,6},{3,7},{4,0},{5,1},{6,2},{7,3},{8,12},{9,13},{10,... | collective-permute-start | bytes 344072 | tf_op jit(solution)/shard_map/ppermute | solution.py:511
  16.2 8.8 %collective-permute-start.2 = (f32[4,3,16,256]{3,2,1,0:T(8,128)S(1)}, f32[4,3,16,256]{3,2,1,0:T(8,128)S(1)}, u32[]{:S(2)}, u32[]{:S(2)}) collective-permute-start(f32[4,3,16,256]{3,2,1,0:T(8,128)S(1)} %pad_maximum_fusion.2), channel_id=1, source_target_pairs={{0,2},{1,3},{2,0},{3,1},{4,6},{5,7},{6,4},{7,5},{8,10},{9,11},{10,... | collective-permute-start | bytes 589832 | tf_op jit(solution)/shard_map/ppermute | solution.py:508
  18.9 5.8 %collective-permute-start.6 = (bf16[20,16,256]{2,1,0:T(8,128)(2,1)S(1)}, bf16[20,16,256]{2,1,0:T(8,128)(2,1)S(1)}, u32[]{:S(2)}, u32[]{:S(2)}) collective-permute-start(bf16[20,16,256]{2,1,0:T(8,128)(2,1)S(1)} %pad_maximum_fusion.4), channel_id=1, source_target_pairs={{0,2},{1,3},{2,0},{3,1},{4,6},{5,7},{6,4},{7,5},{8,10},{9,11},{10,... | collective-permute-start | bytes 491528 | tf_op jit(solution)/shard_map/ppermute | solution.py:511
  24.9 1.6 %collective-permute-start.7 = (bf16[32,16,256]{2,1,0:T(8,128)(2,1)S(1)}, bf16[32,16,256]{2,1,0:T(8,128)(2,1)S(1)}, u32[]{:S(2)}, u32[]{:S(2)}) collective-permute-start(bf16[32,16,256]{2,1,0:T(8,128)(2,1)S(1)} %pad_maximum_fusion.1), channel_id=1, source_target_pairs={{0,1},{1,0},{2,3},{3,2},{4,5},{5,4},{6,7},{7,6},{8,9},{9,8},{10,11... | collective-permute-start | bytes 786440 | tf_op jit(solution)/shard_map/ppermute | solution.py:511
  25.0 2.0 %collective-permute-start.3 = (f32[8,3,16,256]{3,2,1,0:T(8,128)S(1)}, f32[8,3,16,256]{3,2,1,0:T(8,128)S(1)}, u32[]{:S(2)}, u32[]{:S(2)}) collective-permute-start(f32[8,3,16,256]{3,2,1,0:T(8,128)S(1)} %pad_maximum_fusion), channel_id=1, source_target_pairs={{0,1},{1,0},{2,3},{3,2},{4,5},{5,4},{6,7},{7,6},{8,9},{9,8},{10,11... | collective-permute-start | bytes 1179656 | tf_op jit(solution)/shard_map/ppermute | solution.py:508
  26.6 0.9 copy-start
  26.6 1.0 copy-start.1
  26.6 0.9 copy-start.2
  26.6 0.9 copy-start.3
  87.4 29.7 %all-to-all-start = ((f32[16,4,16,256]{3,2,1,0:T(8,128)}), f32[16,4,16,256]{3,2,1,0:T(8,128)S(1)}, u32[]{:S(2)}, u32[]{:S(2)}) async-start(f32[16,4,16,256]{3,2,1,0:T(8,128)} %channel.1), calls=%async_computation | async-start | bytes 2097152 | tf_op jit(solution)/shard_map/all_to_all | solution.py:554

commit v4 on v3

--- a/solution.py
+++ b/solution.py
@@ -277,12 +277,27 @@
     return dot32(left, jnp.concatenate([first, second, first], axis=0))
 
 
+def level_of(largest):
+    logarithm = jnp.log(jnp.maximum(largest, 1e-36)) * (1.0 / math.log(2.0))
+    level = jnp.floor(logarithm + 1e-3).astype(jnp.int32) + 1 - 15 + 126
+    return jnp.clip(level, 0, 250)
+
+
+def power_of_two(level, sign):
+    value = jnp.full(level.shape, 2.0 ** (-126 * sign), jnp.float32)
+    for bit in range(7):
+        value = value * jnp.where((level >> bit) & 1 > 0, 2.0 ** (sign * 2**bit), 1.0)
+    return value * jnp.where((level >> 7) & 1 > 0, 2.0 ** (sign * 64), 1.0) * jnp.where((level >> 7) & 1 > 0, 2.0 ** (sign * 64), 1.0)
+
+
 def channel_kernel(
-    offset_ref, base_ref, charge_ref, pair_ref, square_ref, order_ref, gain_ref, y_square_ref,
-    right_ref, left_ref, out_ref,
-    grid_ref, turned_ref, window_ref, spline_ref, place_ref,
+    offset_ref, base_ref, charge_ref, far_offset_ref, far_ref, inverse_hbm, order_ref, widths_ref,
+    right_hbm, left_hbm, out_ref,
+    grid_ref, turned_ref, window_ref, spline_ref, place_ref, pair_ref, gain_ref, value_ref, charged_ref,
+    inverse_ref, right_ref, left_ref, inverse_done, right_done, left_done,
 ):
-    slabs, _, blocks, capacity = offset_ref.shape
+    near, _, blocks, capacity = offset_ref.shape
+    slabs = 2 * near
     planes = MESH_X // slabs
     rows = MESH_Y // blocks
     border = ORDER - 1
@@ -290,15 +305,24 @@
     extent = planes + border
     far = MESH_X + border
 
-    def prepare(slab, carry):
+    loads = [
+        pltpu.make_async_copy(inverse_hbm, inverse_ref, inverse_done),
+        pltpu.make_async_copy(right_hbm, right_ref, right_done),
+        pltpu.make_async_copy(left_hbm, left_ref, left_done),
+    ]
+    for load in loads:
+        load.start()
+
+    def prepare(slab, offset_at, base_at, charge):
         span = pl.ds(pl.multiple_of(slab * blocks, blocks), blocks)
-        z_base = base_ref[slab, 2].astype(jnp.float32).astype(jnp.int32)
-        for dimension in range(2):
-            place_ref[dimension, span, :] = base_ref[slab, dimension].astype(jnp.float32).astype(jnp.int32)
-        place_ref[2, span, :] = z_base & 7
-        place_ref[3, span, :] = z_base >> 3
+        charged_ref[slab] = charge.astype(jnp.float32)
+        bases = [base_at(dimension).astype(jnp.float32).astype(jnp.int32) for dimension in range(3)]
+        place_ref[0, span, :] = bases[0] & 7
+        place_ref[1, span, :] = bases[1] & 7
+        place_ref[2, span, :] = bases[2] & 7
+        place_ref[3, span, :] = bases[2] >> 3
         for dimension in range(3):
-            weights, slopes = spline_lists(offset_ref[slab, dimension], ORDER)
+            weights, slopes = spline_lists(offset_at(dimension), ORDER)
             for kind, values in enumerate((weights, slopes)):
                 for position in range(8):
                     value = values[position] if position < ORDER else jnp.zeros_like(values[0])
@@ -306,9 +330,23 @@
                         spline_ref[
                             2 * dimension + kind, half, pl.ds(slab * blocks * 8 + position, blocks, stride=8), :
                         ] = value[:, half * 128 : (half + 1) * 128]
-        return carry
-
-    lax.fori_loop(0, slabs, prepare, 0)
+
+    def prepare_both(index, carry):
+        prepare(
+            index,
+            lambda dimension: offset_ref[index, dimension],
+            lambda dimension: base_ref[index, dimension],
+            charge_ref[index],
+        )
+        prepare(
+            near + index,
+            lambda dimension: far_offset_ref[index, dimension],
+            lambda dimension: far_ref[3 * index + dimension],
+            far_ref[3 * near + index],
+        )
+        return carry
+
+    lax.fori_loop(0, near, prepare_both, 0)
 
     def clear(plane, carry):
         grid_ref[plane] = jnp.zeros(grid_ref.shape[1:], jnp.float32)
@@ -352,7 +390,7 @@
         x_base, unused, (x_table,) = cyclic_tables(0, place, (0,))
         unused, y_own, (y_table,) = cyclic_tables(1, place, (0,))
         (z_table,) = z_tables(place, (0,))
-        charge = jnp.broadcast_to(charge_ref[turn_index, pl.ds(block, 1), :], (8, capacity))
+        charge = jnp.broadcast_to(charged_ref[turn_index, pl.ds(block, 1), :], (8, capacity))
         x_place = jnp.concatenate([x_base, x_base], axis=0).astype(jnp.float32).astype(jnp.bfloat16)
         low, high = [], []
         for index in range(planes):
@@ -380,7 +418,22 @@
     for index in range(border):
         grid_ref[index] += grid_ref[MESH_X + index]
 
+    for load in loads:
+        load.wait()
     right, left = right_ref[...], left_ref[...]
+    width = widths_ref[order_ref[0]]
+
+    def squares(dimension):
+        index = lax.broadcasted_iota(jnp.int32, (MESH_X, MESH_Z), dimension)
+        index = jnp.where(index * 2 > MESH_X, index - MESH_X, index).astype(jnp.float32) / MESH_X
+        return index * index
+
+    across, along = squares(0), squares(1)
+    decay = -(math.pi**2) / (width * width)
+    gain_ref[...] = jnp.exp(decay * across) * inverse_ref[0]
+    scale = 2.0 / (math.pi * MESH_X * MESH_Y * MESH_Z)
+    pair_ref[0] = gain_ref[...] * (jnp.exp(decay * along) * (inverse_ref[1] * scale))
+    pair_ref[1] = across + along
 
     def forward(step, carry):
         both = []
@@ -406,10 +459,12 @@
         spectrum = cas_rows(lines, left)
         filters = []
         for index in range(2):
-            total = square_ref[...] + y_square_ref[2 * step + index]
+            row = 2 * step + index
+            frequency = jnp.where(row * 2 > MESH_Y, row - MESH_Y, row).astype(jnp.float32) / MESH_Y
+            total = pair_ref[1] + frequency * frequency
             positive = total > 0
             safe = jnp.where(positive, total, 1.0)
-            filters.append(jnp.where(positive, pair_ref[...] * gain_ref[2 * step + index] / safe, 0.0))
+            filters.append(jnp.where(positive, pair_ref[0] * gain_ref[pl.ds(row, 1), :] / safe, 0.0))
         lines = cas_rows(spectrum * jnp.concatenate(filters, axis=1), left)
         for index, span in enumerate(spans):
             turned_ref[span, :] = lines[:, index * MESH_Z : (index + 1) * MESH_Z]
@@ -443,7 +498,7 @@
         x_base, unused, (x_table, x_slope) = cyclic_tables(0, place, (0, 1))
         unused, y_own, (y_table, y_slope) = cyclic_tables(1, place, (0, 1))
         z_table, z_slope = z_tables(place, (0, 1))
-        charge = charge_ref[turn_index, pl.ds(block, 1), :]
+        charge = charged_ref[turn_index, pl.ds(block, 1), :]
         window = jnp.concatenate(
             [window_ref[slab * planes + index, block] for index in range(extent)], axis=0
         )
@@ -458,8 +513,8 @@
                 return jnp.where(own, rows_of(index), rows_of(planes + index))
             return rows_of(index)
 
-        near = dot32(window, z_table)
-        near_z = dot32(window, z_slope)
+        both = dot32(window, jnp.concatenate([z_table, z_slope], axis=1))
+        near, near_z = both[:, :capacity], both[:, capacity:]
         plain = sloped = plain_z = 0.0
         for index in range(planes):
             own = x_base <= index
@@ -468,16 +523,37 @@
             sloped += x_slope[index : index + 1] * part
             plain_z += x_table[index : index + 1] * chosen(near_z, index, own)
         row = pl.ds(block, 1)
-        out_ref[slab, 0, row, :] = jnp.sum(y_table * plain, axis=0, keepdims=True)
-        out_ref[slab, 1, row, :] = -charge * jnp.sum(y_table * sloped, axis=0, keepdims=True)
-        out_ref[slab, 2, row, :] = -charge * jnp.sum(y_slope * plain, axis=0, keepdims=True)
-        out_ref[slab, 3, row, :] = -charge * jnp.sum(y_table * plain_z, axis=0, keepdims=True)
+        value_ref[slab, 0, row, :] = jnp.sum(y_table * plain, axis=0, keepdims=True)
+        value_ref[slab, 1, row, :] = -charge * jnp.sum(y_table * sloped, axis=0, keepdims=True)
+        value_ref[slab, 2, row, :] = -charge * jnp.sum(y_slope * plain, axis=0, keepdims=True)
+        value_ref[slab, 3, row, :] = -charge * jnp.sum(y_table * plain_z, axis=0, keepdims=True)
 
     def gather_step(step, carry):
         gather(step // blocks, step % blocks)
         return carry
 
     lax.fori_loop(0, slabs * blocks, gather_step, 0, unroll=16)
+    halves = capacity // 128
+    lines = lax.broadcasted_iota(jnp.int32, (4 * halves, 128), 0)
+    shift = 1.5 * 2.0**23
+
+    def encode(slab, carry):
+        pieces = [
+            value_ref[slab, kind, :, half * 128 : (half + 1) * 128] for kind in range(4) for half in range(halves)
+        ]
+        largest = jnp.zeros((4 * halves, 128), jnp.float32)
+        for line, piece in enumerate(pieces):
+            largest = jnp.where(lines == line, jnp.max(jnp.abs(piece), axis=0, keepdims=True), largest)
+        level = level_of(largest)
+        inverse_scale = power_of_two(level, -1)
+        for line, piece in enumerate(pieces):
+            codes = (piece * inverse_scale[line : line + 1] + shift) - shift
+            out_ref[slab, pl.ds(line * blocks, blocks), :] = codes.astype(jnp.int32).astype(jnp.int16)
+        rest = jnp.zeros((blocks - 4 * halves, 128), jnp.int32)
+        out_ref[slab, pl.ds(4 * halves * blocks, blocks), :] = jnp.concatenate([level, rest], axis=0).astype(jnp.int16)
+        return carry
+
+    lax.fori_loop(0, slabs, encode, 0, unroll=8)
 
 
 def channel_shards(charges, cell_offset, base_cell, counts, widths):
@@ -486,17 +562,12 @@
     blocks = counts.shape[0]
     capacity = slot_count // blocks
     slabs = lax.axis_size("wide")
-    planes = MESH_X // slabs
-    block_rows = MESH_Y // blocks
     live_mask = jnp.arange(capacity, dtype=jnp.int32)[None, :] < counts[:, None]
     charge_blocks = jnp.where(
         live_mask[None], charges.reshape(channels, blocks, capacity), jnp.zeros((), jnp.bfloat16)
     )
-    bases = base_cell.reshape(3, blocks, capacity)
-    row_start = jnp.arange(blocks, dtype=jnp.int32)[:, None] * block_rows
-    cells = jnp.stack([bases[0] - device * planes, bases[1] - row_start, bases[2]]).astype(jnp.bfloat16)
+    cells = base_cell.astype(jnp.bfloat16).reshape(1, 3, blocks, capacity)
     offsets = cell_offset.reshape(1, 3, blocks, capacity)
-    cells = cells[None]
     parts = charge_blocks[None]
     order = jnp.zeros((1,), jnp.int32)
     distance = slabs // 2
@@ -505,38 +576,35 @@
         upper = (device & distance) > 0
         first, second = parts[:, :distance], parts[:, distance:]
         kept, sent = jnp.where(upper, second, first), jnp.where(upper, first, second)
-        offsets = jnp.concatenate([offsets, lax.ppermute(offsets, "wide", route)], axis=0)
         count = cells.shape[0]
         bundle = jnp.concatenate([cells.reshape((-1,) + cells.shape[2:]), sent.reshape((-1,) + sent.shape[2:])], axis=0)
+        arrived = lax.ppermute(offsets, "wide", route)
         bundle = lax.ppermute(bundle, "wide", route)
-        cells = jnp.concatenate([cells, bundle[: 3 * count].reshape(cells.shape)], axis=0)
-        parts = jnp.concatenate([kept, bundle[3 * count :].reshape(kept.shape)], axis=0)
         order = jnp.concatenate([order, order ^ distance])
+        if distance > 1:
+            offsets = jnp.concatenate([offsets, arrived], axis=0)
+            cells = jnp.concatenate([cells, bundle[: 3 * count].reshape(cells.shape)], axis=0)
+            parts = jnp.concatenate([kept, bundle[3 * count :].reshape(kept.shape)], axis=0)
         distance //= 2
-    charge_blocks = parts[:, 0]
     order = order ^ device
 
-    width = lax.dynamic_index_in_dim(widths, device, keepdims=False)
     points = np.arange(MESH_X)
-    folded_points = np.where(points * 2 > MESH_X, points - MESH_X, points) / MESH_X
-    squares = (folded_points**2).astype(np.float32)
     first = np.array([1.0, 26.0, 66.0, 26.0, 1.0, 0.0]) / 120.0
     angles = 2.0 * math.pi * points[:, None] * np.arange(ORDER)[None, :] / MESH_X
     inverse = (1.0 / ((np.cos(angles) @ first) ** 2 + (np.sin(angles) @ first) ** 2)).astype(np.float32)
-    gains = jnp.exp(-(math.pi**2) * squares / (width * width)) * inverse
-    scale = 2.0 / (math.pi * MESH_X * MESH_Y * MESH_Z)
-    pairs = gains[:, None] * (gains * scale)[None, :]
-    pair_squares = squares[:, None] + squares[None, :]
+    inverse = np.stack([np.repeat(inverse[:, None], MESH_Z, axis=1), np.repeat(inverse[None], MESH_X, axis=0)])
     one, two = cas_terms(MESH_X)
     right = np.concatenate([np.concatenate([one, two], axis=1)] * 2, axis=0)
     left = np.concatenate([one, one, two], axis=1)
 
+    halves = capacity // 128
     whole = pl.BlockSpec(memory_space=pltpu.VMEM)
+    away = pl.BlockSpec(memory_space=pltpu.HBM)
     scalars = pl.BlockSpec(memory_space=pltpu.SMEM)
     result = pl.pallas_call(
         channel_kernel,
-        out_shape=jax.ShapeDtypeStruct((slabs, 4, blocks, capacity), jnp.float32),
-        in_specs=[whole] * 5 + [scalars] * 3 + [whole] * 2,
+        out_shape=jax.ShapeDtypeStruct((slabs, (4 * halves + 1) * blocks, 128), jnp.int16),
+        in_specs=[whole] * 5 + [away] + [scalars] * 2 + [away] * 2,
         out_specs=whole,
         scratch_shapes=[
             pltpu.VMEM((MESH_X + ORDER - 1, MESH_Y + 8, MESH_Z), jnp.float32),
@@ -544,16 +612,31 @@
             pltpu.VMEM((MESH_X + ORDER - 1, blocks, 16, MESH_Z), jnp.bfloat16),
             pltpu.VMEM((6, capacity // 128, slabs * blocks * 8, 128), jnp.float32),
             pltpu.VMEM((4, slabs * blocks, capacity), jnp.int32),
+            pltpu.VMEM((2, MESH_X, MESH_Z), jnp.float32),
+            pltpu.VMEM((MESH_Y, MESH_Z), jnp.float32),
+            pltpu.VMEM((slabs, 4, blocks, capacity), jnp.float32),
+            pltpu.VMEM((slabs, blocks, capacity), jnp.float32),
+            pltpu.VMEM(inverse.shape, jnp.float32),
+            pltpu.VMEM(right.shape, jnp.bfloat16),
+            pltpu.VMEM(left.shape, jnp.bfloat16),
+            pltpu.SemaphoreType.DMA,
+            pltpu.SemaphoreType.DMA,
+            pltpu.SemaphoreType.DMA,
         ],
         compiler_params=pltpu.CompilerParams(vmem_limit_bytes=52 * 1024 * 1024),
         name="channel",
     )(
-        offsets, cells, charge_blocks.astype(jnp.float32), pairs, jnp.asarray(pair_squares), order, gains,
-        jnp.asarray(squares), jnp.asarray(right), jnp.asarray(left),
+        offsets, cells, kept[:, 0], arrived, bundle, jnp.asarray(inverse), order, widths,
+        jnp.asarray(right), jnp.asarray(left),
     )
     returned = lax.all_to_all(result, "wide", split_axis=0, concat_axis=0, tiled=True)
-    atom_potential = jnp.where(live_mask[None], returned[:, 0], 0.0).reshape(channels, slot_count)
-    forces = jnp.sum(returned[:, 1:], axis=0).reshape(3, slot_count)
+    codes = returned[:, : 4 * halves * blocks].reshape(channels, 4, halves, blocks, 128)
+    levels = returned[:, 4 * halves * blocks : 4 * halves * blocks + 4 * halves].astype(jnp.int32)
+    scales = power_of_two(levels, 1).reshape(channels, 4, halves, 1, 128)
+    values = codes.astype(jnp.float32) * scales
+    potential = jnp.moveaxis(values[:, 0], 1, 2).reshape(channels, blocks, capacity)
+    atom_potential = jnp.where(live_mask[None], potential, 0.0).reshape(channels, slot_count)
+    forces = jnp.moveaxis(jnp.sum(values[:, 1:], axis=0), 1, 2).reshape(3, slot_count)
     return (atom_potential, forces)
 
 

time: 120 us -> 112 us (0.933)
  waiting for transfers between devices: 32.8 us -> 25.3 us
  starting transfers between devices: 17.1 us -> 20 us
  local copies, waits for them, and re-layouts: 5.11 us -> 3.48 us
  between operations: 2.4 us -> 0.98 us
    all_to_all x1, waiting for transfers between devices: 22.8 us -> 15.4 us  [channel_shards(): lax.all_to_all(result, 'wide', split_axis=0, concat_axis=0, tiled=True)]
    unnamed x34 -> x23, local copies, waits for them, and re-layouts: 4.23 us -> 2.22 us
    ppermute x4, waiting for transfers between devices: 7.46 us -> 6.15 us  [channel_shards(): bundle = lax.ppermute(bundle, 'wide', route)]
    ppermute x4, waiting for transfers between devices: 2.52 us -> 3.77 us  [channel_shards(): arrived = lax.ppermute(offsets, 'wide', route)]
  transfers between devices with their start and end apart: 9 -> 9, of which waited for: 7 -> 8; matrix products, arithmetic and copies ran while one was open for 1% -> 0% of each run, Pallas kernels for 0% -> 0%
where the time goes in v4:
time: 112 us; the launch traced here: 111 us
  Pallas kernels  60.1 us (54%)
  waiting for transfers between devices  25.3 us (23%)
  starting transfers between devices  20 us (18%)
  local copies, waits for them, and re-layouts  3.48 us (3%)
  other arithmetic  1.4 us (1%)
    pallas_call x1, Pallas kernels, channel_shards(): pl.pallas_call(channel_kernel, out_shape=jax.ShapeDtypeStruct((slabs, (4...  60.1 us
    all_to_all x1, waiting for transfers between devices, channel_shards(): lax.all_to_all(result, 'wide', split_axis=0, concat_axis=0, tiled=True)  15.4 us
    ppermute x4, starting transfers between devices, channel_shards(): arrived = lax.ppermute(offsets, 'wide', route)  8.99 us
    all_to_all x1, starting transfers between devices, channel_shards(): lax.all_to_all(result, 'wide', split_axis=0, concat_axis=0, tiled=True)  7.99 us
    ppermute x4, waiting for transfers between devices, channel_shards(): bundle = lax.ppermute(bundle, 'wide', route)  6.15 us
    ppermute x4, waiting for transfers between devices, channel_shards(): arrived = lax.ppermute(offsets, 'wide', route)  3.77 us
    ppermute x4, starting transfers between devices, channel_shards(): bundle = lax.ppermute(bundle, 'wide', route)  2.97 us
  transfers between devices with their start and end apart: 9, of which 8 were waited for; matrix products, arithmetic and copies ran while one was open for 0% of the time, Pallas kernels for 0%

profile of v4, /device:TPU:0, one launch (start us, length us, event | category | flops | bytes accessed | tf_op | source)
XLA Modules:
  0.0 111.3 jit_solution(12193082380620860628)
XLA Ops:
  0.6 0.9 constant_dynamic-update-slice_fusion.3
  1.5 4.1 %collective-permute-start = (f32[1,3,16,256]{3,2,1,0:T(8,128)S(1)}, f32[1,3,16,256]{3,2,1,0:T(8,128)S(1)}, u32[]{:S(2)}, u32[]{:S(2)}) collective-permute-start(f32[1,3,16,256]{3,2,1,0:T(8,128)S(1)} %get-tuple-element.3), channel_id=1, source_target_pairs={{0,8},{1,9},{2,10},{3,11},{4,12},{5,13},{6,14},{7,15},{8,0},{9,1},... | collective-permute-start | bytes 147464 | tf_op jit(solution)/shard_map/ppermute | solution.py:581
  5.7 0.6 copy-done.6
  6.4 0.1 copy-done.5
  6.7 1.5 %collective-permute-done = f32[1,3,16,256]{3,2,1,0:T(8,128)S(1)} collective-permute-done((f32[1,3,16,256]{3,2,1,0:T(8,128)S(1)}, f32[1,3,16,256]{3,2,1,0:T(8,128)S(1)}, u32[]{:S(2)}, u32[]{:S(2)}) %collective-permute-start) | collective-permute-done | bytes 49184 | tf_op jit(solution)/shard_map/ppermute | solution.py:581
  8.2 3.2 %collective-permute-start.1 = (f32[2,3,16,256]{3,2,1,0:T(8,128)S(1)}, f32[2,3,16,256]{3,2,1,0:T(8,128)S(1)}, u32[]{:S(2)}, u32[]{:S(2)}) collective-permute-start(f32[2,3,16,256]{3,2,1,0:T(8,128)S(1)} %pad_maximum_fusion.5), channel_id=1, source_target_pairs={{0,4},{1,5},{2,6},{3,7},{4,0},{5,1},{6,2},{7,3},{8,12},{9,13},{10,... | collective-permute-start | bytes 294920 | tf_op jit(solution)/shard_map/ppermute | solution.py:581
  11.5 1.6 %collective-permute-done.3 = bf16[11,16,256]{2,1,0:T(8,128)(2,1)S(1)} collective-permute-done((bf16[11,16,256]{2,1,0:T(8,128)(2,1)S(1)}, bf16[11,16,256]{2,1,0:T(8,128)(2,1)S(1)}, u32[]{:S(2)}, u32[]{:S(2)}) %collective-permute-start.3) | collective-permute-done | bytes 90144 | tf_op jit(solution)/shard_map/ppermute | solution.py:582
  13.2 1.2 %collective-permute-start.4 = (bf16[14,16,256]{2,1,0:T(8,128)(2,1)S(1)}, bf16[14,16,256]{2,1,0:T(8,128)(2,1)S(1)}, u32[]{:S(2)}, u32[]{:S(2)}) collective-permute-start(bf16[14,16,256]{2,1,0:T(8,128)(2,1)S(1)} %pad_maximum_fusion.4), channel_id=1, source_target_pairs={{0,4},{1,5},{2,6},{3,7},{4,0},{5,1},{6,2},{7,3},{8,12},{9,13},{10,... | collective-permute-start | bytes 344072 | tf_op jit(solution)/shard_map/ppermute | solution.py:582
  14.4 0.2 collective-permute-done.1
  14.6 1.6 %collective-permute-start.2 = (f32[4,3,16,256]{3,2,1,0:T(8,128)S(1)}, f32[4,3,16,256]{3,2,1,0:T(8,128)S(1)}, u32[]{:S(2)}, u32[]{:S(2)}) collective-permute-start(f32[4,3,16,256]{3,2,1,0:T(8,128)S(1)} %pad_maximum_fusion.1), channel_id=1, source_target_pairs={{0,2},{1,3},{2,0},{3,1},{4,6},{5,7},{6,4},{7,5},{8,10},{9,11},{10,... | collective-permute-start | bytes 589832 | tf_op jit(solution)/shard_map/ppermute | solution.py:581
  16.2 1.8 %collective-permute-done.4 = bf16[14,16,256]{2,1,0:T(8,128)(2,1)S(1)} collective-permute-done((bf16[14,16,256]{2,1,0:T(8,128)(2,1)S(1)}, bf16[14,16,256]{2,1,0:T(8,128)(2,1)S(1)}, u32[]{:S(2)}, u32[]{:S(2)}) %collective-permute-start.4) | collective-permute-done | bytes 114720 | tf_op jit(solution)/shard_map/ppermute | solution.py:582
  18.2 1.6 %collective-permute-start.5 = (bf16[20,16,256]{2,1,0:T(8,128)(2,1)S(1)}, bf16[20,16,256]{2,1,0:T(8,128)(2,1)S(1)}, u32[]{:S(2)}, u32[]{:S(2)}) collective-permute-start(bf16[20,16,256]{2,1,0:T(8,128)(2,1)S(1)} %pad_maximum_fusion.3), channel_id=1, source_target_pairs={{0,2},{1,3},{2,0},{3,1},{4,6},{5,7},{6,4},{7,5},{8,10},{9,11},{10,... | collective-permute-start | bytes 491528 | tf_op jit(solution)/shard_map/ppermute | solution.py:582
  19.8 2.0 %collective-permute-done.2 = f32[4,3,16,256]{3,2,1,0:T(8,128)S(1)} collective-permute-done((f32[4,3,16,256]{3,2,1,0:T(8,128)S(1)}, f32[4,3,16,256]{3,2,1,0:T(8,128)S(1)}, u32[]{:S(2)}, u32[]{:S(2)}) %collective-permute-start.2) | collective-permute-done | bytes 196640 | tf_op jit(solution)/shard_map/ppermute | solution.py:581
  21.9 1.7 %collective-permute-done.5 = bf16[20,16,256]{2,1,0:T(8,128)(2,1)S(1)} collective-permute-done((bf16[20,16,256]{2,1,0:T(8,128)(2,1)S(1)}, bf16[20,16,256]{2,1,0:T(8,128)(2,1)S(1)}, u32[]{:S(2)}, u32[]{:S(2)}) %collective-permute-start.5) | collective-permute-done | bytes 163872 | tf_op jit(solution)/shard_map/ppermute | solution.py:582
  23.8 0.5 copy-done.7
  24.3 1.0 collective-permute-done.7.far_ref
  25.4 60.1 %channel.1 = s16[16,144,128]{2,1,0:T(8,128)(2,1)} custom-call(f32[8,3,16,256]{3,2,1,0:T(8,128)S(1)} %constant_dynamic-update-slice_fusion.offset_ref, bf16[8,3,16,256]{3,2,1,0:T(8,128)(2,1)S(1)} %pad_maximum_fusion.2.base_ref, bf16[8,16,256]{2,1,0:T(8,128)(2,1)S(1)} %get-tuple-element.5.charge_ref, ...), custom_call_target="tpu_custom_call" | custom-call | tf_op jit(solution)/shard_map/channel/pallas_call | solution.py:604
  85.5 8.0 %all-to-all-start = ((s16[16,144,128]{2,1,0:T(8,128)(2,1)}), s16[16,144,128]{2,1,0:T(8,128)(2,1)S(1)}, u32[]{:S(2)}, u32[]{:S(2)}) async-start(s16[16,144,128]{2,1,0:T(8,128)(2,1)} %channel.1), calls=%async_computation | async-start | bytes 1179648 | tf_op jit(solution)/shard_map/all_to_all | solution.py:632
  93.6 15.4 %all-to-all-done = s16[16,144,128]{2,1,0:T(8,128)(2,1)S(1)} async-done(((s16[16,144,128]{2,1,0:T(8,128)(2,1)}), s16[16,144,128]{2,1,0:T(8,128)(2,1)S(1)}, u32[]{:S(2)}, u32[]{:S(2)}) %all-to-all-start) | async-done | bytes 589856 | tf_op jit(solution)/shard_map/all_to_all | solution.py:632
  109.2 0.2 convert_multiply_fusion
  109.5 0.1 copy.29
  109.6 0.2 reshape.114
  109.9 0.7 reshape.115
  110.5 0.7 broadcast_select_fusion
  (56 shorter events, 1.0 us)
Async XLA Ops:
  0.6 5.0 %copy-start.4 = (bf16[16,4096]{1,0:T(8,128)(2,1)S(1)}, bf16[16,4096]{1,0:T(8,128)(2,1)}, u32[]{:S(2)}) copy-start(bf16[16,4096]{1,0:T(8,128)(2,1)} %param.8) | copy-start | bytes 393220
  1.5 6.7 %collective-permute-start = (f32[1,3,16,256]{3,2,1,0:T(8,128)S(1)}, f32[1,3,16,256]{3,2,1,0:T(8,128)S(1)}, u32[]{:S(2)}, u32[]{:S(2)}) collective-permute-start(f32[1,3,16,256]{3,2,1,0:T(8,128)S(1)} %get-tuple-element.3), channel_id=1, source_target_pairs={{0,8},{1,9},{2,10},{3,11},{4,12},{5,13},{6,14},{7,15},{8,0},{9,1},... | collective-permute-start | bytes 147464 | tf_op jit(solution)/shard_map/ppermute | solution.py:581
  5.6 0.7 copy-start.6
  5.6 0.9 copy-start.5
  6.6 6.5 %collective-permute-start.3 = (bf16[11,16,256]{2,1,0:T(8,128)(2,1)S(1)}, bf16[11,16,256]{2,1,0:T(8,128)(2,1)S(1)}, u32[]{:S(2)}, u32[]{:S(2)}) collective-permute-start(bf16[11,16,256]{2,1,0:T(8,128)(2,1)S(1)} %pad_maximum_fusion.7), channel_id=1, source_target_pairs={{0,8},{1,9},{2,10},{3,11},{4,12},{5,13},{6,14},{7,15},{8,0},{9,1},... | collective-permute-start | bytes 270344 | tf_op jit(solution)/shard_map/ppermute | solution.py:582
  8.2 6.4 %collective-permute-start.1 = (f32[2,3,16,256]{3,2,1,0:T(8,128)S(1)}, f32[2,3,16,256]{3,2,1,0:T(8,128)S(1)}, u32[]{:S(2)}, u32[]{:S(2)}) collective-permute-start(f32[2,3,16,256]{3,2,1,0:T(8,128)S(1)} %pad_maximum_fusion.5), channel_id=1, source_target_pairs={{0,4},{1,5},{2,6},{3,7},{4,0},{5,1},{6,2},{7,3},{8,12},{9,13},{10,... | collective-permute-start | bytes 294920 | tf_op jit(solution)/shard_map/ppermute | solution.py:581
  13.2 4.9 %collective-permute-start.4 = (bf16[14,16,256]{2,1,0:T(8,128)(2,1)S(1)}, bf16[14,16,256]{2,1,0:T(8,128)(2,1)S(1)}, u32[]{:S(2)}, u32[]{:S(2)}) collective-permute-start(bf16[14,16,256]{2,1,0:T(8,128)(2,1)S(1)} %pad_maximum_fusion.4), channel_id=1, source_target_pairs={{0,4},{1,5},{2,6},{3,7},{4,0},{5,1},{6,2},{7,3},{8,12},{9,13},{10,... | collective-permute-start | bytes 344072 | tf_op jit(solution)/shard_map/ppermute | solution.py:582
  14.6 7.2 %collective-permute-start.2 = (f32[4,3,16,256]{3,2,1,0:T(8,128)S(1)}, f32[4,3,16,256]{3,2,1,0:T(8,128)S(1)}, u32[]{:S(2)}, u32[]{:S(2)}) collective-permute-start(f32[4,3,16,256]{3,2,1,0:T(8,128)S(1)} %pad_maximum_fusion.1), channel_id=1, source_target_pairs={{0,2},{1,3},{2,0},{3,1},{4,6},{5,7},{6,4},{7,5},{8,10},{9,11},{10,... | collective-permute-start | bytes 589832 | tf_op jit(solution)/shard_map/ppermute | solution.py:581
  18.2 5.4 %collective-permute-start.5 = (bf16[20,16,256]{2,1,0:T(8,128)(2,1)S(1)}, bf16[20,16,256]{2,1,0:T(8,128)(2,1)S(1)}, u32[]{:S(2)}, u32[]{:S(2)}) collective-permute-start(bf16[20,16,256]{2,1,0:T(8,128)(2,1)S(1)} %pad_maximum_fusion.3), channel_id=1, source_target_pairs={{0,2},{1,3},{2,0},{3,1},{4,6},{5,7},{6,4},{7,5},{8,10},{9,11},{10,... | collective-permute-start | bytes 491528 | tf_op jit(solution)/shard_map/ppermute | solution.py:582
  21.8 3.5 %collective-permute-start.6 = (f32[8,3,16,256]{3,2,1,0:T(8,128)S(1)}, f32[8,3,16,256]{3,2,1,0:T(8,128)S(1)}, u32[]{:S(2)}, u32[]{:S(2)}) collective-permute-start(f32[8,3,16,256]{3,2,1,0:T(8,128)S(1)} %constant_dynamic-update-slice_fusion.offset_ref), channel_id=1, source_target_pairs={{0,1},{1,0},{2,3},{3,2},{4,5},{5,4},{6,7},{7,6},{8,9},{9,8},{10,11... | collective-permute-start | bytes 1179656 | tf_op jit(solution)/shard_map/ppermute | solution.py:581
  23.6 0.7 copy-start.7
  23.6 1.7 %copy-start = (f32[2,128,128]{2,1,0:T(8,128)S(1)}, f32[2,128,128]{2,1,0:T(8,128)}, u32[]{:S(2)}) copy-start(f32[2,128,128]{2,1,0:T(8,128)} %constant.21.clone.inverse_hbm) | copy-start | bytes 393220
  23.7 1.7 %copy-start.1 = (bf16[256,256]{1,0:T(8,128)(2,1)S(1)}, bf16[256,256]{1,0:T(8,128)(2,1)}, u32[]{:S(2)}) copy-start(bf16[256,256]{1,0:T(8,128)(2,1)} %constant.22.clone.right_hbm) | copy-start | bytes 393220
  23.7 1.7 %copy-start.2 = (bf16[128,384]{1,0:T(8,128)(2,1)S(1)}, bf16[128,384]{1,0:T(8,128)(2,1)}, u32[]{:S(2)}) copy-start(bf16[128,384]{1,0:T(8,128)(2,1)} %constant.23.clone.left_hbm) | copy-start | bytes 294916
  23.7 1.6 %collective-permute-start.7 = (bf16[32,16,256]{2,1,0:T(8,128)(2,1)S(1)}, bf16[32,16,256]{2,1,0:T(8,128)(2,1)S(1)}, u32[]{:S(2)}, u32[]{:S(2)}) collective-permute-start(bf16[32,16,256]{2,1,0:T(8,128)(2,1)S(1)} %pad_maximum_fusion), channel_id=1, source_target_pairs={{0,1},{1,0},{2,3},{3,2},{4,5},{5,4},{6,7},{7,6},{8,9},{9,8},{10,11... | collective-permute-start | bytes 786440 | tf_op jit(solution)/shard_map/ppermute | solution.py:582
  24.3 1.0 copy-start.3
  85.5 23.5 %all-to-all-start = ((s16[16,144,128]{2,1,0:T(8,128)(2,1)}), s16[16,144,128]{2,1,0:T(8,128)(2,1)S(1)}, u32[]{:S(2)}, u32[]{:S(2)}) async-start(s16[16,144,128]{2,1,0:T(8,128)(2,1)} %channel.1), calls=%async_computation | async-start | bytes 1179648 | tf_op jit(solution)/shard_map/all_to_all | solution.py:632

commit v5 on v4

--- a/solution.py
+++ b/solution.py
@@ -273,8 +273,9 @@
 
 
 def cas_rows(values, left):
-    first, second = split(values)
-    return dot32(left, jnp.concatenate([first, second, first], axis=0))
+    sums = dot32(left, jnp.concatenate(split(values), axis=0))
+    length = values.shape[0]
+    return sums[:length] + sums[length:]
 
 
 def level_of(largest):
@@ -413,7 +414,7 @@
         spread(step // blocks, step % blocks)
         return carry
 
-    lax.fori_loop(0, slabs * blocks, spread_step, 0, unroll=16)
+    lax.fori_loop(0, slabs * blocks, spread_step, 0, unroll=32)
 
     for index in range(border):
         grid_ref[index] += grid_ref[MESH_X + index]
@@ -451,7 +452,7 @@
             ]
         return carry
 
-    lax.fori_loop(0, MESH_X // 2, forward, 0, unroll=16)
+    lax.fori_loop(0, MESH_X // 2, forward, 0, unroll=32)
 
     def filtering(step, carry):
         spans = [pl.ds(pl.multiple_of((2 * step + index) * MESH_X, MESH_X), MESH_X) for index in range(2)]
@@ -470,7 +471,7 @@
             turned_ref[span, :] = lines[:, index * MESH_Z : (index + 1) * MESH_Z]
         return carry
 
-    lax.fori_loop(0, MESH_Y // 2, filtering, 0, unroll=16)
+    lax.fori_loop(0, MESH_Y // 2, filtering, 0, unroll=32)
 
     def backward(step, carry):
         both = jnp.concatenate(
@@ -487,7 +488,7 @@
                 window_ref[2 * step + index, block] = plane[block * rows : block * rows + frame].astype(jnp.bfloat16)
         return carry
 
-    lax.fori_loop(0, MESH_X // 2, backward, 0, unroll=16)
+    lax.fori_loop(0, MESH_X // 2, backward, 0, unroll=32)
 
     for index in range(border):
         window_ref[MESH_X + index] = window_ref[index]
@@ -532,7 +533,7 @@
         gather(step // blocks, step % blocks)
         return carry
 
-    lax.fori_loop(0, slabs * blocks, gather_step, 0, unroll=16)
+    lax.fori_loop(0, slabs * blocks, gather_step, 0, unroll=32)
     halves = capacity // 128
     lines = lax.broadcasted_iota(jnp.int32, (4 * halves, 128), 0)
     shift = 1.5 * 2.0**23
@@ -595,7 +596,7 @@
     inverse = np.stack([np.repeat(inverse[:, None], MESH_Z, axis=1), np.repeat(inverse[None], MESH_X, axis=0)])
     one, two = cas_terms(MESH_X)
     right = np.concatenate([np.concatenate([one, two], axis=1)] * 2, axis=0)
-    left = np.concatenate([one, one, two], axis=1)
+    left = np.concatenate([np.concatenate([one, one], axis=1), np.concatenate([two, two], axis=1)], axis=0)
 
     halves = capacity // 128
     whole = pl.BlockSpec(memory_space=pltpu.VMEM)

time: 112 us -> 107 us (0.955)
  Pallas kernels: 60.1 us -> 55.5 us
    pallas_call x1, Pallas kernels: 60.1 us -> 55.5 us  [channel_shards(): pl.pallas_call(channel_kernel, out_shape=jax.ShapeDtypeStruct((slabs, (4...]
where the time goes in v5:
time: 107 us
  Pallas kernels  55.5 us (52%)
  waiting for transfers between devices  25.3 us (24%)
  starting transfers between devices  20 us (19%)
  local copies, waits for them, and re-layouts  3.48 us (3%)
  other arithmetic  1.4 us (1%)
    pallas_call x1, Pallas kernels, channel_shards(): pl.pallas_call(channel_kernel, out_shape=jax.ShapeDtypeStruct((slabs, (4...  55.5 us
    all_to_all x1, waiting for transfers between devices, channel_shards(): lax.all_to_all(result, 'wide', split_axis=0, concat_axis=0, tiled=True)  15.4 us
    ppermute x4, starting transfers between devices, channel_shards(): arrived = lax.ppermute(offsets, 'wide', route)  8.99 us
    all_to_all x1, starting transfers between devices, channel_shards(): lax.all_to_all(result, 'wide', split_axis=0, concat_axis=0, tiled=True)  8 us
    ppermute x4, waiting for transfers between devices, channel_shards(): bundle = lax.ppermute(bundle, 'wide', route)  6.15 us
    ppermute x4, waiting for transfers between devices, channel_shards(): arrived = lax.ppermute(offsets, 'wide', route)  3.77 us
    ppermute x4, starting transfers between devices, channel_shards(): bundle = lax.ppermute(bundle, 'wide', route)  2.97 us
    unnamed x23, local copies, waits for them, and re-layouts  2.22 us
  transfers between devices with their start and end apart: 9, of which 8 were waited for; matrix products, arithmetic and copies ran while one was open for 0% of the time, Pallas kernels for 0%

profile of v5, /device:TPU:0, one launch (start us, length us, event | category | flops | bytes accessed | tf_op | source)
XLA Modules:
  0.0 106.7 jit_solution(6086846195602408840)
XLA Ops:
  0.6 0.9 constant_dynamic-update-slice_fusion.3
  1.5 4.1 %collective-permute-start = (f32[1,3,16,256]{3,2,1,0:T(8,128)S(1)}, f32[1,3,16,256]{3,2,1,0:T(8,128)S(1)}, u32[]{:S(2)}, u32[]{:S(2)}) collective-permute-start(f32[1,3,16,256]{3,2,1,0:T(8,128)S(1)} %get-tuple-element.3), channel_id=1, source_target_pairs={{0,8},{1,9},{2,10},{3,11},{4,12},{5,13},{6,14},{7,15},{8,0},{9,1},... | collective-permute-start | bytes 147464 | tf_op jit(solution)/shard_map/ppermute | solution.py:582
  5.7 0.6 copy-done.6
  6.4 0.1 copy-done.5
  6.7 1.5 %collective-permute-done = f32[1,3,16,256]{3,2,1,0:T(8,128)S(1)} collective-permute-done((f32[1,3,16,256]{3,2,1,0:T(8,128)S(1)}, f32[1,3,16,256]{3,2,1,0:T(8,128)S(1)}, u32[]{:S(2)}, u32[]{:S(2)}) %collective-permute-start) | collective-permute-done | bytes 49184 | tf_op jit(solution)/shard_map/ppermute | solution.py:582
  8.2 3.2 %collective-permute-start.1 = (f32[2,3,16,256]{3,2,1,0:T(8,128)S(1)}, f32[2,3,16,256]{3,2,1,0:T(8,128)S(1)}, u32[]{:S(2)}, u32[]{:S(2)}) collective-permute-start(f32[2,3,16,256]{3,2,1,0:T(8,128)S(1)} %pad_maximum_fusion.5), channel_id=1, source_target_pairs={{0,4},{1,5},{2,6},{3,7},{4,0},{5,1},{6,2},{7,3},{8,12},{9,13},{10,... | collective-permute-start | bytes 294920 | tf_op jit(solution)/shard_map/ppermute | solution.py:582
  11.5 1.6 %collective-permute-done.3 = bf16[11,16,256]{2,1,0:T(8,128)(2,1)S(1)} collective-permute-done((bf16[11,16,256]{2,1,0:T(8,128)(2,1)S(1)}, bf16[11,16,256]{2,1,0:T(8,128)(2,1)S(1)}, u32[]{:S(2)}, u32[]{:S(2)}) %collective-permute-start.3) | collective-permute-done | bytes 90144 | tf_op jit(solution)/shard_map/ppermute | solution.py:583
  13.2 1.2 %collective-permute-start.4 = (bf16[14,16,256]{2,1,0:T(8,128)(2,1)S(1)}, bf16[14,16,256]{2,1,0:T(8,128)(2,1)S(1)}, u32[]{:S(2)}, u32[]{:S(2)}) collective-permute-start(bf16[14,16,256]{2,1,0:T(8,128)(2,1)S(1)} %pad_maximum_fusion.4), channel_id=1, source_target_pairs={{0,4},{1,5},{2,6},{3,7},{4,0},{5,1},{6,2},{7,3},{8,12},{9,13},{10,... | collective-permute-start | bytes 344072 | tf_op jit(solution)/shard_map/ppermute | solution.py:583
  14.4 0.2 collective-permute-done.1
  14.6 1.6 %collective-permute-start.2 = (f32[4,3,16,256]{3,2,1,0:T(8,128)S(1)}, f32[4,3,16,256]{3,2,1,0:T(8,128)S(1)}, u32[]{:S(2)}, u32[]{:S(2)}) collective-permute-start(f32[4,3,16,256]{3,2,1,0:T(8,128)S(1)} %pad_maximum_fusion.1), channel_id=1, source_target_pairs={{0,2},{1,3},{2,0},{3,1},{4,6},{5,7},{6,4},{7,5},{8,10},{9,11},{10,... | collective-permute-start | bytes 589832 | tf_op jit(solution)/shard_map/ppermute | solution.py:582
  16.2 1.8 %collective-permute-done.4 = bf16[14,16,256]{2,1,0:T(8,128)(2,1)S(1)} collective-permute-done((bf16[14,16,256]{2,1,0:T(8,128)(2,1)S(1)}, bf16[14,16,256]{2,1,0:T(8,128)(2,1)S(1)}, u32[]{:S(2)}, u32[]{:S(2)}) %collective-permute-start.4) | collective-permute-done | bytes 114720 | tf_op jit(solution)/shard_map/ppermute | solution.py:583
  18.2 1.6 %collective-permute-start.5 = (bf16[20,16,256]{2,1,0:T(8,128)(2,1)S(1)}, bf16[20,16,256]{2,1,0:T(8,128)(2,1)S(1)}, u32[]{:S(2)}, u32[]{:S(2)}) collective-permute-start(bf16[20,16,256]{2,1,0:T(8,128)(2,1)S(1)} %pad_maximum_fusion.3), channel_id=1, source_target_pairs={{0,2},{1,3},{2,0},{3,1},{4,6},{5,7},{6,4},{7,5},{8,10},{9,11},{10,... | collective-permute-start | bytes 491528 | tf_op jit(solution)/shard_map/ppermute | solution.py:583
  19.8 2.0 %collective-permute-done.2 = f32[4,3,16,256]{3,2,1,0:T(8,128)S(1)} collective-permute-done((f32[4,3,16,256]{3,2,1,0:T(8,128)S(1)}, f32[4,3,16,256]{3,2,1,0:T(8,128)S(1)}, u32[]{:S(2)}, u32[]{:S(2)}) %collective-permute-start.2) | collective-permute-done | bytes 196640 | tf_op jit(solution)/shard_map/ppermute | solution.py:582
  21.9 1.7 %collective-permute-done.5 = bf16[20,16,256]{2,1,0:T(8,128)(2,1)S(1)} collective-permute-done((bf16[20,16,256]{2,1,0:T(8,128)(2,1)S(1)}, bf16[20,16,256]{2,1,0:T(8,128)(2,1)S(1)}, u32[]{:S(2)}, u32[]{:S(2)}) %collective-permute-start.5) | collective-permute-done | bytes 163872 | tf_op jit(solution)/shard_map/ppermute | solution.py:583
  23.8 0.5 copy-done.7
  24.3 1.0 collective-permute-done.7.far_ref
  25.4 55.5 %channel.1 = s16[16,144,128]{2,1,0:T(8,128)(2,1)} custom-call(f32[8,3,16,256]{3,2,1,0:T(8,128)S(1)} %constant_dynamic-update-slice_fusion.offset_ref, bf16[8,3,16,256]{3,2,1,0:T(8,128)(2,1)S(1)} %pad_maximum_fusion.2.base_ref, bf16[8,16,256]{2,1,0:T(8,128)(2,1)S(1)} %get-tuple-element.5.charge_ref, ...), custom_call_target="tpu_custom_call" | custom-call | tf_op jit(solution)/shard_map/channel/pallas_call | solution.py:605
  80.9 8.0 %all-to-all-start = ((s16[16,144,128]{2,1,0:T(8,128)(2,1)}), s16[16,144,128]{2,1,0:T(8,128)(2,1)S(1)}, u32[]{:S(2)}, u32[]{:S(2)}) async-start(s16[16,144,128]{2,1,0:T(8,128)(2,1)} %channel.1), calls=%async_computation | async-start | bytes 1179648 | tf_op jit(solution)/shard_map/all_to_all | solution.py:633
  89.0 15.4 %all-to-all-done = s16[16,144,128]{2,1,0:T(8,128)(2,1)S(1)} async-done(((s16[16,144,128]{2,1,0:T(8,128)(2,1)}), s16[16,144,128]{2,1,0:T(8,128)(2,1)S(1)}, u32[]{:S(2)}, u32[]{:S(2)}) %all-to-all-start) | async-done | bytes 589856 | tf_op jit(solution)/shard_map/all_to_all | solution.py:633
  104.6 0.2 convert_multiply_fusion
  104.9 0.1 copy.29
  105.0 0.2 reshape.114
  105.3 0.7 reshape.115
  106.0 0.7 broadcast_select_fusion
  (56 shorter events, 1.0 us)
Async XLA Ops:
  0.6 5.0 %copy-start.4 = (bf16[16,4096]{1,0:T(8,128)(2,1)S(1)}, bf16[16,4096]{1,0:T(8,128)(2,1)}, u32[]{:S(2)}) copy-start(bf16[16,4096]{1,0:T(8,128)(2,1)} %param.8) | copy-start | bytes 393220
  1.5 6.7 %collective-permute-start = (f32[1,3,16,256]{3,2,1,0:T(8,128)S(1)}, f32[1,3,16,256]{3,2,1,0:T(8,128)S(1)}, u32[]{:S(2)}, u32[]{:S(2)}) collective-permute-start(f32[1,3,16,256]{3,2,1,0:T(8,128)S(1)} %get-tuple-element.3), channel_id=1, source_target_pairs={{0,8},{1,9},{2,10},{3,11},{4,12},{5,13},{6,14},{7,15},{8,0},{9,1},... | collective-permute-start | bytes 147464 | tf_op jit(solution)/shard_map/ppermute | solution.py:582
  5.6 0.7 copy-start.6
  5.6 0.9 copy-start.5
  6.6 6.5 %collective-permute-start.3 = (bf16[11,16,256]{2,1,0:T(8,128)(2,1)S(1)}, bf16[11,16,256]{2,1,0:T(8,128)(2,1)S(1)}, u32[]{:S(2)}, u32[]{:S(2)}) collective-permute-start(bf16[11,16,256]{2,1,0:T(8,128)(2,1)S(1)} %pad_maximum_fusion.7), channel_id=1, source_target_pairs={{0,8},{1,9},{2,10},{3,11},{4,12},{5,13},{6,14},{7,15},{8,0},{9,1},... | collective-permute-start | bytes 270344 | tf_op jit(solution)/shard_map/ppermute | solution.py:583
  8.2 6.4 %collective-permute-start.1 = (f32[2,3,16,256]{3,2,1,0:T(8,128)S(1)}, f32[2,3,16,256]{3,2,1,0:T(8,128)S(1)}, u32[]{:S(2)}, u32[]{:S(2)}) collective-permute-start(f32[2,3,16,256]{3,2,1,0:T(8,128)S(1)} %pad_maximum_fusion.5), channel_id=1, source_target_pairs={{0,4},{1,5},{2,6},{3,7},{4,0},{5,1},{6,2},{7,3},{8,12},{9,13},{10,... | collective-permute-start | bytes 294920 | tf_op jit(solution)/shard_map/ppermute | solution.py:582
  13.2 4.9 %collective-permute-start.4 = (bf16[14,16,256]{2,1,0:T(8,128)(2,1)S(1)}, bf16[14,16,256]{2,1,0:T(8,128)(2,1)S(1)}, u32[]{:S(2)}, u32[]{:S(2)}) collective-permute-start(bf16[14,16,256]{2,1,0:T(8,128)(2,1)S(1)} %pad_maximum_fusion.4), channel_id=1, source_target_pairs={{0,4},{1,5},{2,6},{3,7},{4,0},{5,1},{6,2},{7,3},{8,12},{9,13},{10,... | collective-permute-start | bytes 344072 | tf_op jit(solution)/shard_map/ppermute | solution.py:583
  14.6 7.2 %collective-permute-start.2 = (f32[4,3,16,256]{3,2,1,0:T(8,128)S(1)}, f32[4,3,16,256]{3,2,1,0:T(8,128)S(1)}, u32[]{:S(2)}, u32[]{:S(2)}) collective-permute-start(f32[4,3,16,256]{3,2,1,0:T(8,128)S(1)} %pad_maximum_fusion.1), channel_id=1, source_target_pairs={{0,2},{1,3},{2,0},{3,1},{4,6},{5,7},{6,4},{7,5},{8,10},{9,11},{10,... | collective-permute-start | bytes 589832 | tf_op jit(solution)/shard_map/ppermute | solution.py:582
  18.2 5.4 %collective-permute-start.5 = (bf16[20,16,256]{2,1,0:T(8,128)(2,1)S(1)}, bf16[20,16,256]{2,1,0:T(8,128)(2,1)S(1)}, u32[]{:S(2)}, u32[]{:S(2)}) collective-permute-start(bf16[20,16,256]{2,1,0:T(8,128)(2,1)S(1)} %pad_maximum_fusion.3), channel_id=1, source_target_pairs={{0,2},{1,3},{2,0},{3,1},{4,6},{5,7},{6,4},{7,5},{8,10},{9,11},{10,... | collective-permute-start | bytes 491528 | tf_op jit(solution)/shard_map/ppermute | solution.py:583
  21.8 3.5 %collective-permute-start.6 = (f32[8,3,16,256]{3,2,1,0:T(8,128)S(1)}, f32[8,3,16,256]{3,2,1,0:T(8,128)S(1)}, u32[]{:S(2)}, u32[]{:S(2)}) collective-permute-start(f32[8,3,16,256]{3,2,1,0:T(8,128)S(1)} %constant_dynamic-update-slice_fusion.offset_ref), channel_id=1, source_target_pairs={{0,1},{1,0},{2,3},{3,2},{4,5},{5,4},{6,7},{7,6},{8,9},{9,8},{10,11... | collective-permute-start | bytes 1179656 | tf_op jit(solution)/shard_map/ppermute | solution.py:582
  23.6 0.7 copy-start.7
  23.6 1.7 %copy-start = (f32[2,128,128]{2,1,0:T(8,128)S(1)}, f32[2,128,128]{2,1,0:T(8,128)}, u32[]{:S(2)}) copy-start(f32[2,128,128]{2,1,0:T(8,128)} %constant.21.clone.inverse_hbm) | copy-start | bytes 393220
  23.7 1.7 %copy-start.1 = (bf16[256,256]{1,0:T(8,128)(2,1)S(1)}, bf16[256,256]{1,0:T(8,128)(2,1)}, u32[]{:S(2)}) copy-start(bf16[256,256]{1,0:T(8,128)(2,1)} %constant.22.clone.right_hbm) | copy-start | bytes 393220
  23.7 1.7 %copy-start.2 = (bf16[256,256]{1,0:T(8,128)(2,1)S(1)}, bf16[256,256]{1,0:T(8,128)(2,1)}, u32[]{:S(2)}) copy-start(bf16[256,256]{1,0:T(8,128)(2,1)} %constant.23.clone.left_hbm) | copy-start | bytes 393220
  23.7 1.6 %collective-permute-start.7 = (bf16[32,16,256]{2,1,0:T(8,128)(2,1)S(1)}, bf16[32,16,256]{2,1,0:T(8,128)(2,1)S(1)}, u32[]{:S(2)}, u32[]{:S(2)}) collective-permute-start(bf16[32,16,256]{2,1,0:T(8,128)(2,1)S(1)} %pad_maximum_fusion), channel_id=1, source_target_pairs={{0,1},{1,0},{2,3},{3,2},{4,5},{5,4},{6,7},{7,6},{8,9},{9,8},{10,11... | collective-permute-start | bytes 786440 | tf_op jit(solution)/shard_map/ppermute | solution.py:583
  24.3 1.0 copy-start.3
  80.9 23.6 %all-to-all-start = ((s16[16,144,128]{2,1,0:T(8,128)(2,1)}), s16[16,144,128]{2,1,0:T(8,128)(2,1)S(1)}, u32[]{:S(2)}, u32[]{:S(2)}) async-start(s16[16,144,128]{2,1,0:T(8,128)(2,1)} %channel.1), calls=%async_computation | async-start | bytes 1179648 | tf_op jit(solution)/shard_map/all_to_all | solution.py:633

commit v6 on v5

--- a/solution.py
+++ b/solution.py
@@ -414,7 +414,7 @@
         spread(step // blocks, step % blocks)
         return carry
 
-    lax.fori_loop(0, slabs * blocks, spread_step, 0, unroll=32)
+    lax.fori_loop(0, slabs * blocks, spread_step, 0, unroll=64)
 
     for index in range(border):
         grid_ref[index] += grid_ref[MESH_X + index]
@@ -452,7 +452,7 @@
             ]
         return carry
 
-    lax.fori_loop(0, MESH_X // 2, forward, 0, unroll=32)
+    lax.fori_loop(0, MESH_X // 2, forward, 0, unroll=64)
 
     def filtering(step, carry):
         spans = [pl.ds(pl.multiple_of((2 * step + index) * MESH_X, MESH_X), MESH_X) for index in range(2)]
@@ -471,7 +471,7 @@
             turned_ref[span, :] = lines[:, index * MESH_Z : (index + 1) * MESH_Z]
         return carry
 
-    lax.fori_loop(0, MESH_Y // 2, filtering, 0, unroll=32)
+    lax.fori_loop(0, MESH_Y // 2, filtering, 0, unroll=64)
 
     def backward(step, carry):
         both = jnp.concatenate(
@@ -488,7 +488,7 @@
                 window_ref[2 * step + index, block] = plane[block * rows : block * rows + frame].astype(jnp.bfloat16)
         return carry
 
-    lax.fori_loop(0, MESH_X // 2, backward, 0, unroll=32)
+    lax.fori_loop(0, MESH_X // 2, backward, 0, unroll=64)
 
     for index in range(border):
         window_ref[MESH_X + index] = window_ref[index]
@@ -533,7 +533,7 @@
         gather(step // blocks, step % blocks)
         return carry
 
-    lax.fori_loop(0, slabs * blocks, gather_step, 0, unroll=32)
+    lax.fori_loop(0, slabs * blocks, gather_step, 0, unroll=64)
     halves = capacity // 128
     lines = lax.broadcasted_iota(jnp.int32, (4 * halves, 128), 0)
     shift = 1.5 * 2.0**23
@@ -609,9 +609,9 @@
         out_specs=whole,
         scratch_shapes=[
             pltpu.VMEM((MESH_X + ORDER - 1, MESH_Y + 8, MESH_Z), jnp.float32),
-            pltpu.VMEM((MESH_X * MESH_Y, MESH_Z), jnp.float32),
+            pltpu.VMEM((MESH_X * MESH_Y + MESH_X, MESH_Z), jnp.float32),
             pltpu.VMEM((MESH_X + ORDER - 1, blocks, 16, MESH_Z), jnp.bfloat16),
-            pltpu.VMEM((6, capacity // 128, slabs * blocks * 8, 128), jnp.float32),
+            pltpu.VMEM((6, capacity // 128, slabs * blocks * 8 + 8, 128), jnp.float32),
             pltpu.VMEM((4, slabs * blocks, capacity), jnp.int32),
             pltpu.VMEM((2, MESH_X, MESH_Z), jnp.float32),
             pltpu.VMEM((MESH_Y, MESH_Z), jnp.float32),

time: 107 us -> 105 us (0.981)
  Pallas kernels: 55.5 us -> 53.5 us
    pallas_call x1, Pallas kernels: 55.5 us -> 53.5 us  [channel_shards(): pl.pallas_call(channel_kernel, out_shape=jax.ShapeDtypeStruct((slabs, (4...]
  transfers between devices with their start and end apart: 9 -> 9, of which waited for: 8 -> 8; matrix products, arithmetic and copies ran while one was open for 0% -> 1% of each run, Pallas kernels for 0% -> 0%
where the time goes in v6:
time: 105 us
  Pallas kernels  53.5 us (51%)
  waiting for transfers between devices  25.3 us (24%)
  starting transfers between devices  20 us (19%)
  local copies, waits for them, and re-layouts  3.48 us (3%)
  other arithmetic  1.4 us (1%)
    pallas_call x1, Pallas kernels, channel_shards(): pl.pallas_call(channel_kernel, out_shape=jax.ShapeDtypeStruct((slabs, (4...  53.5 us
    all_to_all x1, waiting for transfers between devices, channel_shards(): lax.all_to_all(result, 'wide', split_axis=0, concat_axis=0, tiled=True)  15.4 us
    ppermute x4, starting transfers between devices, channel_shards(): arrived = lax.ppermute(offsets, 'wide', route)  8.99 us
    all_to_all x1, starting transfers between devices, channel_shards(): lax.all_to_all(result, 'wide', split_axis=0, concat_axis=0, tiled=True)  7.99 us
    ppermute x4, waiting for transfers between devices, channel_shards(): bundle = lax.ppermute(bundle, 'wide', route)  6.15 us
    ppermute x4, waiting for transfers between devices, channel_shards(): arrived = lax.ppermute(offsets, 'wide', route)  3.77 us
    ppermute x4, starting transfers between devices, channel_shards(): bundle = lax.ppermute(bundle, 'wide', route)  2.97 us
    unnamed x23, local copies, waits for them, and re-layouts  2.22 us
  transfers between devices with their start and end apart: 9, of which 8 were waited for; matrix products, arithmetic and copies ran while one was open for 1% of the time, Pallas kernels for 0%

profile of v6, /device:TPU:0, one launch (start us, length us, event | category | flops | bytes accessed | tf_op | source)
XLA Modules:
  0.0 104.6 jit_solution(243815192942385779)
XLA Ops:
  0.6 0.9 constant_dynamic-update-slice_fusion.3
  1.5 4.1 %collective-permute-start = (f32[1,3,16,256]{3,2,1,0:T(8,128)S(1)}, f32[1,3,16,256]{3,2,1,0:T(8,128)S(1)}, u32[]{:S(2)}, u32[]{:S(2)}) collective-permute-start(f32[1,3,16,256]{3,2,1,0:T(8,128)S(1)} %get-tuple-element.3), channel_id=1, source_target_pairs={{0,8},{1,9},{2,10},{3,11},{4,12},{5,13},{6,14},{7,15},{8,0},{9,1},... | collective-permute-start | bytes 147464 | tf_op jit(solution)/shard_map/ppermute | solution.py:582
  5.7 0.6 copy-done.6
  6.4 0.1 copy-done.5
  6.7 1.5 %collective-permute-done = f32[1,3,16,256]{3,2,1,0:T(8,128)S(1)} collective-permute-done((f32[1,3,16,256]{3,2,1,0:T(8,128)S(1)}, f32[1,3,16,256]{3,2,1,0:T(8,128)S(1)}, u32[]{:S(2)}, u32[]{:S(2)}) %collective-permute-start) | collective-permute-done | bytes 49184 | tf_op jit(solution)/shard_map/ppermute | solution.py:582
  8.2 3.2 %collective-permute-start.1 = (f32[2,3,16,256]{3,2,1,0:T(8,128)S(1)}, f32[2,3,16,256]{3,2,1,0:T(8,128)S(1)}, u32[]{:S(2)}, u32[]{:S(2)}) collective-permute-start(f32[2,3,16,256]{3,2,1,0:T(8,128)S(1)} %pad_maximum_fusion.5), channel_id=1, source_target_pairs={{0,4},{1,5},{2,6},{3,7},{4,0},{5,1},{6,2},{7,3},{8,12},{9,13},{10,... | collective-permute-start | bytes 294920 | tf_op jit(solution)/shard_map/ppermute | solution.py:582
  11.5 1.6 %collective-permute-done.3 = bf16[11,16,256]{2,1,0:T(8,128)(2,1)S(1)} collective-permute-done((bf16[11,16,256]{2,1,0:T(8,128)(2,1)S(1)}, bf16[11,16,256]{2,1,0:T(8,128)(2,1)S(1)}, u32[]{:S(2)}, u32[]{:S(2)}) %collective-permute-start.3) | collective-permute-done | bytes 90144 | tf_op jit(solution)/shard_map/ppermute | solution.py:583
  13.2 1.2 %collective-permute-start.4 = (bf16[14,16,256]{2,1,0:T(8,128)(2,1)S(1)}, bf16[14,16,256]{2,1,0:T(8,128)(2,1)S(1)}, u32[]{:S(2)}, u32[]{:S(2)}) collective-permute-start(bf16[14,16,256]{2,1,0:T(8,128)(2,1)S(1)} %pad_maximum_fusion.4), channel_id=1, source_target_pairs={{0,4},{1,5},{2,6},{3,7},{4,0},{5,1},{6,2},{7,3},{8,12},{9,13},{10,... | collective-permute-start | bytes 344072 | tf_op jit(solution)/shard_map/ppermute | solution.py:583
  14.4 0.2 collective-permute-done.1
  14.6 1.6 %collective-permute-start.2 = (f32[4,3,16,256]{3,2,1,0:T(8,128)S(1)}, f32[4,3,16,256]{3,2,1,0:T(8,128)S(1)}, u32[]{:S(2)}, u32[]{:S(2)}) collective-permute-start(f32[4,3,16,256]{3,2,1,0:T(8,128)S(1)} %pad_maximum_fusion.1), channel_id=1, source_target_pairs={{0,2},{1,3},{2,0},{3,1},{4,6},{5,7},{6,4},{7,5},{8,10},{9,11},{10,... | collective-permute-start | bytes 589832 | tf_op jit(solution)/shard_map/ppermute | solution.py:582
  16.2 1.8 %collective-permute-done.4 = bf16[14,16,256]{2,1,0:T(8,128)(2,1)S(1)} collective-permute-done((bf16[14,16,256]{2,1,0:T(8,128)(2,1)S(1)}, bf16[14,16,256]{2,1,0:T(8,128)(2,1)S(1)}, u32[]{:S(2)}, u32[]{:S(2)}) %collective-permute-start.4) | collective-permute-done | bytes 114720 | tf_op jit(solution)/shard_map/ppermute | solution.py:583
  18.2 1.6 %collective-permute-start.5 = (bf16[20,16,256]{2,1,0:T(8,128)(2,1)S(1)}, bf16[20,16,256]{2,1,0:T(8,128)(2,1)S(1)}, u32[]{:S(2)}, u32[]{:S(2)}) collective-permute-start(bf16[20,16,256]{2,1,0:T(8,128)(2,1)S(1)} %pad_maximum_fusion.3), channel_id=1, source_target_pairs={{0,2},{1,3},{2,0},{3,1},{4,6},{5,7},{6,4},{7,5},{8,10},{9,11},{10,... | collective-permute-start | bytes 491528 | tf_op jit(solution)/shard_map/ppermute | solution.py:583
  19.8 2.0 %collective-permute-done.2 = f32[4,3,16,256]{3,2,1,0:T(8,128)S(1)} collective-permute-done((f32[4,3,16,256]{3,2,1,0:T(8,128)S(1)}, f32[4,3,16,256]{3,2,1,0:T(8,128)S(1)}, u32[]{:S(2)}, u32[]{:S(2)}) %collective-permute-start.2) | collective-permute-done | bytes 196640 | tf_op jit(solution)/shard_map/ppermute | solution.py:582
  21.9 1.7 %collective-permute-done.5 = bf16[20,16,256]{2,1,0:T(8,128)(2,1)S(1)} collective-permute-done((bf16[20,16,256]{2,1,0:T(8,128)(2,1)S(1)}, bf16[20,16,256]{2,1,0:T(8,128)(2,1)S(1)}, u32[]{:S(2)}, u32[]{:S(2)}) %collective-permute-start.5) | collective-permute-done | bytes 163872 | tf_op jit(solution)/shard_map/ppermute | solution.py:583
  23.8 0.5 copy-done.7
  24.3 1.0 collective-permute-done.7.far_ref
  25.4 53.5 %channel.1 = s16[16,144,128]{2,1,0:T(8,128)(2,1)} custom-call(f32[8,3,16,256]{3,2,1,0:T(8,128)S(1)} %constant_dynamic-update-slice_fusion.offset_ref, bf16[8,3,16,256]{3,2,1,0:T(8,128)(2,1)S(1)} %pad_maximum_fusion.2.base_ref, bf16[8,16,256]{2,1,0:T(8,128)(2,1)S(1)} %get-tuple-element.5.charge_ref, ...), custom_call_target="tpu_custom_call" | custom-call | tf_op jit(solution)/shard_map/channel/pallas_call | solution.py:605
  78.8 8.0 %all-to-all-start = ((s16[16,144,128]{2,1,0:T(8,128)(2,1)}), s16[16,144,128]{2,1,0:T(8,128)(2,1)S(1)}, u32[]{:S(2)}, u32[]{:S(2)}) async-start(s16[16,144,128]{2,1,0:T(8,128)(2,1)} %channel.1), calls=%async_computation | async-start | bytes 1179648 | tf_op jit(solution)/shard_map/all_to_all | solution.py:633
  87.0 15.4 %all-to-all-done = s16[16,144,128]{2,1,0:T(8,128)(2,1)S(1)} async-done(((s16[16,144,128]{2,1,0:T(8,128)(2,1)}), s16[16,144,128]{2,1,0:T(8,128)(2,1)S(1)}, u32[]{:S(2)}, u32[]{:S(2)}) %all-to-all-start) | async-done | bytes 589856 | tf_op jit(solution)/shard_map/all_to_all | solution.py:633
  102.5 0.2 convert_multiply_fusion
  102.8 0.1 copy.29
  103.0 0.2 reshape.114
  103.2 0.7 reshape.115
  103.9 0.7 broadcast_select_fusion
  (56 shorter events, 1.0 us)
Async XLA Ops:
  0.6 5.0 %copy-start.4 = (bf16[16,4096]{1,0:T(8,128)(2,1)S(1)}, bf16[16,4096]{1,0:T(8,128)(2,1)}, u32[]{:S(2)}) copy-start(bf16[16,4096]{1,0:T(8,128)(2,1)} %param.8) | copy-start | bytes 393220
  1.5 6.7 %collective-permute-start = (f32[1,3,16,256]{3,2,1,0:T(8,128)S(1)}, f32[1,3,16,256]{3,2,1,0:T(8,128)S(1)}, u32[]{:S(2)}, u32[]{:S(2)}) collective-permute-start(f32[1,3,16,256]{3,2,1,0:T(8,128)S(1)} %get-tuple-element.3), channel_id=1, source_target_pairs={{0,8},{1,9},{2,10},{3,11},{4,12},{5,13},{6,14},{7,15},{8,0},{9,1},... | collective-permute-start | bytes 147464 | tf_op jit(solution)/shard_map/ppermute | solution.py:582
  5.6 0.7 copy-start.6
  5.6 0.9 copy-start.5
  6.6 6.5 %collective-permute-start.3 = (bf16[11,16,256]{2,1,0:T(8,128)(2,1)S(1)}, bf16[11,16,256]{2,1,0:T(8,128)(2,1)S(1)}, u32[]{:S(2)}, u32[]{:S(2)}) collective-permute-start(bf16[11,16,256]{2,1,0:T(8,128)(2,1)S(1)} %pad_maximum_fusion.7), channel_id=1, source_target_pairs={{0,8},{1,9},{2,10},{3,11},{4,12},{5,13},{6,14},{7,15},{8,0},{9,1},... | collective-permute-start | bytes 270344 | tf_op jit(solution)/shard_map/ppermute | solution.py:583
  8.2 6.4 %collective-permute-start.1 = (f32[2,3,16,256]{3,2,1,0:T(8,128)S(1)}, f32[2,3,16,256]{3,2,1,0:T(8,128)S(1)}, u32[]{:S(2)}, u32[]{:S(2)}) collective-permute-start(f32[2,3,16,256]{3,2,1,0:T(8,128)S(1)} %pad_maximum_fusion.5), channel_id=1, source_target_pairs={{0,4},{1,5},{2,6},{3,7},{4,0},{5,1},{6,2},{7,3},{8,12},{9,13},{10,... | collective-permute-start | bytes 294920 | tf_op jit(solution)/shard_map/ppermute | solution.py:582
  13.2 4.9 %collective-permute-start.4 = (bf16[14,16,256]{2,1,0:T(8,128)(2,1)S(1)}, bf16[14,16,256]{2,1,0:T(8,128)(2,1)S(1)}, u32[]{:S(2)}, u32[]{:S(2)}) collective-permute-start(bf16[14,16,256]{2,1,0:T(8,128)(2,1)S(1)} %pad_maximum_fusion.4), channel_id=1, source_target_pairs={{0,4},{1,5},{2,6},{3,7},{4,0},{5,1},{6,2},{7,3},{8,12},{9,13},{10,... | collective-permute-start | bytes 344072 | tf_op jit(solution)/shard_map/ppermute | solution.py:583
  14.6 7.2 %collective-permute-start.2 = (f32[4,3,16,256]{3,2,1,0:T(8,128)S(1)}, f32[4,3,16,256]{3,2,1,0:T(8,128)S(1)}, u32[]{:S(2)}, u32[]{:S(2)}) collective-permute-start(f32[4,3,16,256]{3,2,1,0:T(8,128)S(1)} %pad_maximum_fusion.1), channel_id=1, source_target_pairs={{0,2},{1,3},{2,0},{3,1},{4,6},{5,7},{6,4},{7,5},{8,10},{9,11},{10,... | collective-permute-start | bytes 589832 | tf_op jit(solution)/shard_map/ppermute | solution.py:582
  18.2 5.4 %collective-permute-start.5 = (bf16[20,16,256]{2,1,0:T(8,128)(2,1)S(1)}, bf16[20,16,256]{2,1,0:T(8,128)(2,1)S(1)}, u32[]{:S(2)}, u32[]{:S(2)}) collective-permute-start(bf16[20,16,256]{2,1,0:T(8,128)(2,1)S(1)} %pad_maximum_fusion.3), channel_id=1, source_target_pairs={{0,2},{1,3},{2,0},{3,1},{4,6},{5,7},{6,4},{7,5},{8,10},{9,11},{10,... | collective-permute-start | bytes 491528 | tf_op jit(solution)/shard_map/ppermute | solution.py:583
  21.8 3.5 %collective-permute-start.6 = (f32[8,3,16,256]{3,2,1,0:T(8,128)S(1)}, f32[8,3,16,256]{3,2,1,0:T(8,128)S(1)}, u32[]{:S(2)}, u32[]{:S(2)}) collective-permute-start(f32[8,3,16,256]{3,2,1,0:T(8,128)S(1)} %constant_dynamic-update-slice_fusion.offset_ref), channel_id=1, source_target_pairs={{0,1},{1,0},{2,3},{3,2},{4,5},{5,4},{6,7},{7,6},{8,9},{9,8},{10,11... | collective-permute-start | bytes 1179656 | tf_op jit(solution)/shard_map/ppermute | solution.py:582
  23.6 0.7 copy-start.7
  23.6 1.7 %copy-start = (f32[2,128,128]{2,1,0:T(8,128)S(1)}, f32[2,128,128]{2,1,0:T(8,128)}, u32[]{:S(2)}) copy-start(f32[2,128,128]{2,1,0:T(8,128)} %constant.21.clone.inverse_hbm) | copy-start | bytes 393220
  23.7 1.7 %copy-start.1 = (bf16[256,256]{1,0:T(8,128)(2,1)S(1)}, bf16[256,256]{1,0:T(8,128)(2,1)}, u32[]{:S(2)}) copy-start(bf16[256,256]{1,0:T(8,128)(2,1)} %constant.22.clone.right_hbm) | copy-start | bytes 393220
  23.7 1.7 %copy-start.2 = (bf16[256,256]{1,0:T(8,128)(2,1)S(1)}, bf16[256,256]{1,0:T(8,128)(2,1)}, u32[]{:S(2)}) copy-start(bf16[256,256]{1,0:T(8,128)(2,1)} %constant.23.clone.left_hbm) | copy-start | bytes 393220
  23.7 1.6 %collective-permute-start.7 = (bf16[32,16,256]{2,1,0:T(8,128)(2,1)S(1)}, bf16[32,16,256]{2,1,0:T(8,128)(2,1)S(1)}, u32[]{:S(2)}, u32[]{:S(2)}) collective-permute-start(bf16[32,16,256]{2,1,0:T(8,128)(2,1)S(1)} %pad_maximum_fusion), channel_id=1, source_target_pairs={{0,1},{1,0},{2,3},{3,2},{4,5},{5,4},{6,7},{7,6},{8,9},{9,8},{10,11... | collective-permute-start | bytes 786440 | tf_op jit(solution)/shard_map/ppermute | solution.py:583
  24.3 1.0 %copy-start.3 = (f32[16]{0:T(128)S(1)}, f32[16]{0:T(128)}, u32[]{:S(2)}) copy-start(f32[16]{0:T(128)} %widths_ref.1) | copy-start | bytes 196
  78.8 23.5 %all-to-all-start = ((s16[16,144,128]{2,1,0:T(8,128)(2,1)}), s16[16,144,128]{2,1,0:T(8,128)(2,1)S(1)}, u32[]{:S(2)}, u32[]{:S(2)}) async-start(s16[16,144,128]{2,1,0:T(8,128)(2,1)} %channel.1), calls=%async_computation | async-start | bytes 1179648 | tf_op jit(solution)/shard_map/all_to_all | solution.py:633

commit v7 on v6

--- a/solution.py
+++ b/solution.py
@@ -572,20 +572,26 @@
     parts = charge_blocks[None]
     order = jnp.zeros((1,), jnp.int32)
     distance = slabs // 2
+    ahead = 2
+    ahead_route = [(index, index ^ ahead) for index in range(slabs)]
+    early_offsets = lax.ppermute(offsets, "wide", ahead_route)
+    early_cells = lax.ppermute(cells, "wide", ahead_route)
     while distance > 0:
         route = [(index, index ^ distance) for index in range(slabs)]
+        known = 1 if distance == ahead else 0
         upper = (device & distance) > 0
         first, second = parts[:, :distance], parts[:, distance:]
         kept, sent = jnp.where(upper, second, first), jnp.where(upper, first, second)
         count = cells.shape[0]
-        bundle = jnp.concatenate([cells.reshape((-1,) + cells.shape[2:]), sent.reshape((-1,) + sent.shape[2:])], axis=0)
-        arrived = lax.ppermute(offsets, "wide", route)
+        bundle = jnp.concatenate([cells[known:].reshape((-1,) + cells.shape[2:]), sent.reshape((-1,) + sent.shape[2:])], axis=0)
+        arrived = lax.ppermute(offsets[known:], "wide", route)
         bundle = lax.ppermute(bundle, "wide", route)
         order = jnp.concatenate([order, order ^ distance])
         if distance > 1:
-            offsets = jnp.concatenate([offsets, arrived], axis=0)
-            cells = jnp.concatenate([cells, bundle[: 3 * count].reshape(cells.shape)], axis=0)
-            parts = jnp.concatenate([kept, bundle[3 * count :].reshape(kept.shape)], axis=0)
+            offsets = jnp.concatenate([offsets, early_offsets, arrived] if known else [offsets, arrived], axis=0)
+            fresh = bundle[: 3 * (count - known)].reshape((-1,) + cells.shape[1:])
+            cells = jnp.concatenate([cells, early_cells, fresh] if known else [cells, fresh], axis=0)
+            parts = jnp.concatenate([kept, bundle[3 * (count - known) :].reshape(kept.shape)], axis=0)
         distance //= 2
     order = order ^ device
 

time: 105 us -> 104 us (level)
  starting transfers between devices: 20 us -> 17.8 us
  waiting for transfers between devices: 25.3 us -> 26.4 us
    ppermute x4, waiting for transfers between devices: 6.15 us -> 9.25 us  [channel_shards(): bundle = lax.ppermute(bundle, 'wide', route)]
    ppermute x4 -> x6, waiting for transfers between devices: 3.77 us -> 1.73 us  [the longest x4 1.72 us: channel_shards(): arrived = lax.ppermute(offsets[known:], 'wide', route)]
    all_to_all x1, starting transfers between devices: 7.99 us -> 6.26 us  [channel_shards(): lax.all_to_all(result, 'wide', split_axis=0, concat_axis=0, tiled=True)]
    ppermute x4 -> x6, starting transfers between devices: 8.99 us -> 8.94 us  [the longest x4 7.17 us: channel_shards(): arrived = lax.ppermute(offsets[known:], 'wide', route)]
    unnamed x23 -> x27, local copies, waits for them, and re-layouts: 2.22 us -> 2.24 us
  transfers between devices with their start and end apart: 9 -> 11, of which waited for: 8 -> 6; matrix products, arithmetic and copies ran while one was open for 1% -> 1% of each run, Pallas kernels for 0% -> 0%
where the time goes in v7:
time: 104 us
  Pallas kernels  53.5 us (51%)
  waiting for transfers between devices  26.4 us (25%)
  starting transfers between devices  17.8 us (17%)
  local copies, waits for them, and re-layouts  3.5 us (3%)
  other arithmetic  1.37 us (1%)
    pallas_call x1, Pallas kernels, channel_shards(): pl.pallas_call(channel_kernel, out_shape=jax.ShapeDtypeStruct((slabs, (4...  53.5 us
    all_to_all x1, waiting for transfers between devices, channel_shards(): lax.all_to_all(result, 'wide', split_axis=0, concat_axis=0, tiled=True)  15.4 us
    ppermute x4, waiting for transfers between devices, channel_shards(): bundle = lax.ppermute(bundle, 'wide', route)  9.25 us
    ppermute x4, starting transfers between devices, channel_shards(): arrived = lax.ppermute(offsets[known:], 'wide', route)  7.17 us
    all_to_all x1, starting transfers between devices, channel_shards(): lax.all_to_all(result, 'wide', split_axis=0, concat_axis=0, tiled=True)  6.26 us
    ppermute x4, starting transfers between devices, channel_shards(): bundle = lax.ppermute(bundle, 'wide', route)  2.62 us
    unnamed x27, local copies, waits for them, and re-layouts  2.24 us
  transfers between devices with their start and end apart: 11, of which 6 were waited for; matrix products, arithmetic and copies ran while one was open for 1% of the time, Pallas kernels for 0%

profile of v7, /device:TPU:0, one launch (start us, length us, event | category | flops | bytes accessed | tf_op | source)
XLA Modules:
  0.0 103.6 jit_solution(18428283756455193407)
XLA Ops:
  0.6 0.9 constant_dynamic-update-slice_fusion.4
  1.5 4.1 %collective-permute-start = (f32[1,3,16,256]{3,2,1,0:T(8,128)S(1)}, f32[1,3,16,256]{3,2,1,0:T(8,128)S(1)}, u32[]{:S(2)}, u32[]{:S(2)}) collective-permute-start(f32[1,3,16,256]{3,2,1,0:T(8,128)S(1)} %get-tuple-element.5), channel_id=1, source_target_pairs={{0,8},{1,9},{2,10},{3,11},{4,12},{5,13},{6,14},{7,15},{8,0},{9,1},... | collective-permute-start | bytes 147464 | tf_op jit(solution)/shard_map/ppermute | solution.py:587
  5.6 1.5 %collective-permute-start.2 = (f32[1,3,16,256]{3,2,1,0:T(8,128)S(1)}, f32[1,3,16,256]{3,2,1,0:T(8,128)S(1)}, u32[]{:S(2)}, u32[]{:S(2)}) collective-permute-start(f32[1,3,16,256]{3,2,1,0:T(8,128)S(1)} %get-tuple-element.5), channel_id=1, source_target_pairs={{0,2},{1,3},{2,0},{3,1},{4,6},{5,7},{6,4},{7,5},{8,10},{9,11},{10,... | collective-permute-start | bytes 147464 | tf_op jit(solution)/shard_map/ppermute | solution.py:577
  7.2 0.6 copy-done.6
  8.1 0.4 collective-permute-start.4
  8.5 0.2 collective-permute-start.6
  8.8 1.9 %collective-permute-start.1 = (f32[2,3,16,256]{3,2,1,0:T(8,128)S(1)}, f32[2,3,16,256]{3,2,1,0:T(8,128)S(1)}, u32[]{:S(2)}, u32[]{:S(2)}) collective-permute-start(f32[2,3,16,256]{3,2,1,0:T(8,128)S(1)} %pad_maximum_fusion.4), channel_id=1, source_target_pairs={{0,4},{1,5},{2,6},{3,7},{4,0},{5,1},{6,2},{7,3},{8,12},{9,13},{10,... | collective-permute-start | bytes 294920 | tf_op jit(solution)/shard_map/ppermute | solution.py:587
  10.7 3.4 %collective-permute-done.4 = bf16[11,16,256]{2,1,0:T(8,128)(2,1)S(1)} collective-permute-done((bf16[11,16,256]{2,1,0:T(8,128)(2,1)S(1)}, bf16[11,16,256]{2,1,0:T(8,128)(2,1)S(1)}, u32[]{:S(2)}, u32[]{:S(2)}) %collective-permute-start.4) | collective-permute-done | bytes 90144 | tf_op jit(solution)/shard_map/ppermute | solution.py:588
  14.2 1.5 %collective-permute-start.5 = (bf16[14,16,256]{2,1,0:T(8,128)(2,1)S(1)}, bf16[14,16,256]{2,1,0:T(8,128)(2,1)S(1)}, u32[]{:S(2)}, u32[]{:S(2)}) collective-permute-start(bf16[14,16,256]{2,1,0:T(8,128)(2,1)S(1)} %pad_maximum_fusion.3), channel_id=1, source_target_pairs={{0,4},{1,5},{2,6},{3,7},{4,0},{5,1},{6,2},{7,3},{8,12},{9,13},{10,... | collective-permute-start | bytes 344072 | tf_op jit(solution)/shard_map/ppermute | solution.py:588
  15.7 1.1 %collective-permute-start.3 = (f32[3,3,16,256]{3,2,1,0:T(8,128)S(1)}, f32[3,3,16,256]{3,2,1,0:T(8,128)S(1)}, u32[]{:S(2)}, u32[]{:S(2)}) collective-permute-start(f32[3,3,16,256]{3,2,1,0:T(8,128)S(1)} %pad_maximum_fusion.1), channel_id=1, source_target_pairs={{0,2},{1,3},{2,0},{3,1},{4,6},{5,7},{6,4},{7,5},{8,10},{9,11},{10,... | collective-permute-start | bytes 442376 | tf_op jit(solution)/shard_map/ppermute | solution.py:587
  16.8 2.2 %collective-permute-done.5 = bf16[14,16,256]{2,1,0:T(8,128)(2,1)S(1)} collective-permute-done((bf16[14,16,256]{2,1,0:T(8,128)(2,1)S(1)}, bf16[14,16,256]{2,1,0:T(8,128)(2,1)S(1)}, u32[]{:S(2)}, u32[]{:S(2)}) %collective-permute-start.5) | collective-permute-done | bytes 114720 | tf_op jit(solution)/shard_map/ppermute | solution.py:588
  19.1 0.6 collective-permute-start.7
  19.8 1.7 %collective-permute-done.3 = f32[3,3,16,256]{3,2,1,0:T(8,128)S(1)} collective-permute-done((f32[3,3,16,256]{3,2,1,0:T(8,128)S(1)}, f32[3,3,16,256]{3,2,1,0:T(8,128)S(1)}, u32[]{:S(2)}, u32[]{:S(2)}) %collective-permute-start.3) | collective-permute-done | bytes 147488 | tf_op jit(solution)/shard_map/ppermute | solution.py:587
  21.6 2.7 %collective-permute-done.7 = bf16[17,16,256]{2,1,0:T(8,128)(2,1)S(1)} collective-permute-done((bf16[17,16,256]{2,1,0:T(8,128)(2,1)S(1)}, bf16[17,16,256]{2,1,0:T(8,128)(2,1)S(1)}, u32[]{:S(2)}, u32[]{:S(2)}) %collective-permute-start.7) | collective-permute-done | bytes 139296 | tf_op jit(solution)/shard_map/ppermute | solution.py:588
  24.5 0.5 copy-done.7
  25.0 1.0 collective-permute-done.9.far_ref
  26.0 53.5 %channel.1 = s16[16,144,128]{2,1,0:T(8,128)(2,1)} custom-call(f32[8,3,16,256]{3,2,1,0:T(8,128)S(1)} %constant_dynamic-update-slice_fusion.offset_ref, bf16[8,3,16,256]{3,2,1,0:T(8,128)(2,1)S(1)} %constant_dynamic-update-slice_fusion.5.base_ref, bf16[8,16,256]{2,1,0:T(8,128)(2,1)S(1)} %get-tuple-element.7.charge_ref, ...), custom_call_target="tpu_custom_call" | custom-call | tf_op jit(solution)/shard_map/channel/pallas_call | solution.py:611
  79.5 6.3 %all-to-all-start = ((s16[16,144,128]{2,1,0:T(8,128)(2,1)}), s16[16,144,128]{2,1,0:T(8,128)(2,1)S(1)}, u32[]{:S(2)}, u32[]{:S(2)}) async-start(s16[16,144,128]{2,1,0:T(8,128)(2,1)} %channel.1), calls=%async_computation | async-start | bytes 1179648 | tf_op jit(solution)/shard_map/all_to_all | solution.py:639
  85.9 15.4 %all-to-all-done = s16[16,144,128]{2,1,0:T(8,128)(2,1)S(1)} async-done(((s16[16,144,128]{2,1,0:T(8,128)(2,1)}), s16[16,144,128]{2,1,0:T(8,128)(2,1)S(1)}, u32[]{:S(2)}, u32[]{:S(2)}) %all-to-all-start) | async-done | bytes 589856 | tf_op jit(solution)/shard_map/all_to_all | solution.py:639
  101.5 0.2 convert_multiply_fusion
  101.8 0.1 copy.29
  101.9 0.2 reshape.114
  102.2 0.7 reshape.115
  102.8 0.7 broadcast_select_fusion
  (64 shorter events, 1.1 us)
Async XLA Ops:
  0.6 6.5 %copy-start.4 = (bf16[16,4096]{1,0:T(8,128)(2,1)S(1)}, bf16[16,4096]{1,0:T(8,128)(2,1)}, u32[]{:S(2)}) copy-start(bf16[16,4096]{1,0:T(8,128)(2,1)} %param.8) | copy-start | bytes 393220
  1.5 7.2 %collective-permute-start = (f32[1,3,16,256]{3,2,1,0:T(8,128)S(1)}, f32[1,3,16,256]{3,2,1,0:T(8,128)S(1)}, u32[]{:S(2)}, u32[]{:S(2)}) collective-permute-start(f32[1,3,16,256]{3,2,1,0:T(8,128)S(1)} %get-tuple-element.5), channel_id=1, source_target_pairs={{0,8},{1,9},{2,10},{3,11},{4,12},{5,13},{6,14},{7,15},{8,0},{9,1},... | collective-permute-start | bytes 147464 | tf_op jit(solution)/shard_map/ppermute | solution.py:587
  5.6 11.2 %collective-permute-start.2 = (f32[1,3,16,256]{3,2,1,0:T(8,128)S(1)}, f32[1,3,16,256]{3,2,1,0:T(8,128)S(1)}, u32[]{:S(2)}, u32[]{:S(2)}) collective-permute-start(f32[1,3,16,256]{3,2,1,0:T(8,128)S(1)} %get-tuple-element.5), channel_id=1, source_target_pairs={{0,2},{1,3},{2,0},{3,1},{4,6},{5,7},{6,4},{7,5},{8,10},{9,11},{10,... | collective-permute-start | bytes 147464 | tf_op jit(solution)/shard_map/ppermute | solution.py:577
  7.2 0.7 copy-start.6
  7.2 0.9 copy-start.5
  8.1 5.9 %collective-permute-start.4 = (bf16[11,16,256]{2,1,0:T(8,128)(2,1)S(1)}, bf16[11,16,256]{2,1,0:T(8,128)(2,1)S(1)}, u32[]{:S(2)}, u32[]{:S(2)}) collective-permute-start(bf16[11,16,256]{2,1,0:T(8,128)(2,1)S(1)} %pad_maximum_fusion.5), channel_id=1, source_target_pairs={{0,8},{1,9},{2,10},{3,11},{4,12},{5,13},{6,14},{7,15},{8,0},{9,1},... | collective-permute-start | bytes 270344 | tf_op jit(solution)/shard_map/ppermute | solution.py:588
  8.5 11.2 %collective-permute-start.6 = (bf16[1,3,16,256]{3,2,1,0:T(8,128)(2,1)S(1)}, bf16[1,3,16,256]{3,2,1,0:T(8,128)(2,1)S(1)}, u32[]{:S(2)}, u32[]{:S(2)}) collective-permute-start(bf16[1,3,16,256]{3,2,1,0:T(8,128)(2,1)S(1)} %get-tuple-element.3), channel_id=1, source_target_pairs={{0,2},{1,3},{2,0},{3,1},{4,6},{5,7},{6,4},{7,5},{8,10},{9,11},{10,... | collective-permute-start | bytes 73736 | tf_op jit(solution)/shard_map/ppermute | solution.py:578
  8.8 6.9 %collective-permute-start.1 = (f32[2,3,16,256]{3,2,1,0:T(8,128)S(1)}, f32[2,3,16,256]{3,2,1,0:T(8,128)S(1)}, u32[]{:S(2)}, u32[]{:S(2)}) collective-permute-start(f32[2,3,16,256]{3,2,1,0:T(8,128)S(1)} %pad_maximum_fusion.4), channel_id=1, source_target_pairs={{0,4},{1,5},{2,6},{3,7},{4,0},{5,1},{6,2},{7,3},{8,12},{9,13},{10,... | collective-permute-start | bytes 294920 | tf_op jit(solution)/shard_map/ppermute | solution.py:587
  14.2 4.9 %collective-permute-start.5 = (bf16[14,16,256]{2,1,0:T(8,128)(2,1)S(1)}, bf16[14,16,256]{2,1,0:T(8,128)(2,1)S(1)}, u32[]{:S(2)}, u32[]{:S(2)}) collective-permute-start(bf16[14,16,256]{2,1,0:T(8,128)(2,1)S(1)} %pad_maximum_fusion.3), channel_id=1, source_target_pairs={{0,4},{1,5},{2,6},{3,7},{4,0},{5,1},{6,2},{7,3},{8,12},{9,13},{10,... | collective-permute-start | bytes 344072 | tf_op jit(solution)/shard_map/ppermute | solution.py:588
  15.7 5.8 %collective-permute-start.3 = (f32[3,3,16,256]{3,2,1,0:T(8,128)S(1)}, f32[3,3,16,256]{3,2,1,0:T(8,128)S(1)}, u32[]{:S(2)}, u32[]{:S(2)}) collective-permute-start(f32[3,3,16,256]{3,2,1,0:T(8,128)S(1)} %pad_maximum_fusion.1), channel_id=1, source_target_pairs={{0,2},{1,3},{2,0},{3,1},{4,6},{5,7},{6,4},{7,5},{8,10},{9,11},{10,... | collective-permute-start | bytes 442376 | tf_op jit(solution)/shard_map/ppermute | solution.py:587
  19.1 5.1 %collective-permute-start.7 = (bf16[17,16,256]{2,1,0:T(8,128)(2,1)S(1)}, bf16[17,16,256]{2,1,0:T(8,128)(2,1)S(1)}, u32[]{:S(2)}, u32[]{:S(2)}) collective-permute-start(bf16[17,16,256]{2,1,0:T(8,128)(2,1)S(1)} %pad_maximum_fusion.2), channel_id=1, source_target_pairs={{0,2},{1,3},{2,0},{3,1},{4,6},{5,7},{6,4},{7,5},{8,10},{9,11},{10,... | collective-permute-start | bytes 417800 | tf_op jit(solution)/shard_map/ppermute | solution.py:588
  21.5 4.5 %collective-permute-start.8 = (f32[8,3,16,256]{3,2,1,0:T(8,128)S(1)}, f32[8,3,16,256]{3,2,1,0:T(8,128)S(1)}, u32[]{:S(2)}, u32[]{:S(2)}) collective-permute-start(f32[8,3,16,256]{3,2,1,0:T(8,128)S(1)} %constant_dynamic-update-slice_fusion.offset_ref), channel_id=1, source_target_pairs={{0,1},{1,0},{2,3},{3,2},{4,5},{5,4},{6,7},{7,6},{8,9},{9,8},{10,11... | collective-permute-start | bytes 1179656 | tf_op jit(solution)/shard_map/ppermute | solution.py:587
  24.3 0.7 copy-start.7
  24.3 1.7 %copy-start = (f32[2,128,128]{2,1,0:T(8,128)S(1)}, f32[2,128,128]{2,1,0:T(8,128)}, u32[]{:S(2)}) copy-start(f32[2,128,128]{2,1,0:T(8,128)} %constant.21.clone.inverse_hbm) | copy-start | bytes 393220
  24.3 1.7 %copy-start.1 = (bf16[256,256]{1,0:T(8,128)(2,1)S(1)}, bf16[256,256]{1,0:T(8,128)(2,1)}, u32[]{:S(2)}) copy-start(bf16[256,256]{1,0:T(8,128)(2,1)} %constant.22.clone.right_hbm) | copy-start | bytes 393220
  24.3 1.7 %copy-start.2 = (bf16[256,256]{1,0:T(8,128)(2,1)S(1)}, bf16[256,256]{1,0:T(8,128)(2,1)}, u32[]{:S(2)}) copy-start(bf16[256,256]{1,0:T(8,128)(2,1)} %constant.23.clone.left_hbm) | copy-start | bytes 393220
  24.4 1.6 %collective-permute-start.9 = (bf16[32,16,256]{2,1,0:T(8,128)(2,1)S(1)}, bf16[32,16,256]{2,1,0:T(8,128)(2,1)S(1)}, u32[]{:S(2)}, u32[]{:S(2)}) collective-permute-start(bf16[32,16,256]{2,1,0:T(8,128)(2,1)S(1)} %pad_maximum_fusion), channel_id=1, source_target_pairs={{0,1},{1,0},{2,3},{3,2},{4,5},{5,4},{6,7},{7,6},{8,9},{9,8},{10,11... | collective-permute-start | bytes 786440 | tf_op jit(solution)/shard_map/ppermute | solution.py:588
  25.0 1.0 %copy-start.3 = (f32[16]{0:T(128)S(1)}, f32[16]{0:T(128)}, u32[]{:S(2)}) copy-start(f32[16]{0:T(128)} %widths_ref.1) | copy-start | bytes 196
  79.5 21.8 %all-to-all-start = ((s16[16,144,128]{2,1,0:T(8,128)(2,1)}), s16[16,144,128]{2,1,0:T(8,128)(2,1)S(1)}, u32[]{:S(2)}, u32[]{:S(2)}) async-start(s16[16,144,128]{2,1,0:T(8,128)(2,1)} %channel.1), calls=%async_computation | async-start | bytes 1179648 | tf_op jit(solution)/shard_map/all_to_all | solution.py:639

commit v8 on v7

--- a/solution.py
+++ b/solution.py
@@ -347,13 +347,13 @@
         )
         return carry
 
-    lax.fori_loop(0, near, prepare_both, 0)
+    lax.fori_loop(0, near, prepare_both, 0, unroll=2)
 
     def clear(plane, carry):
         grid_ref[plane] = jnp.zeros(grid_ref.shape[1:], jnp.float32)
         return carry
 
-    lax.fori_loop(0, far, clear, 0)
+    lax.fori_loop(0, far, clear, 0, unroll=19)
     points = lax.broadcasted_iota(jnp.int32, (8, capacity), 0)
 
     def row_of(dimension, block):
@@ -554,7 +554,7 @@
         out_ref[slab, pl.ds(4 * halves * blocks, blocks), :] = jnp.concatenate([level, rest], axis=0).astype(jnp.int16)
         return carry
 
-    lax.fori_loop(0, slabs, encode, 0, unroll=8)
+    lax.fori_loop(0, slabs, encode, 0, unroll=16)
 
 
 def channel_shards(charges, cell_offset, base_cell, counts, widths):

time: 104 us -> 104 us (level)
  no operation moved by 1% of the time
where the time goes in v8:
time: 104 us; the launch traced here: 103 us
  Pallas kernels  53.2 us (51%)
  waiting for transfers between devices  26.4 us (25%)
  starting transfers between devices  17.8 us (17%)
  local copies, waits for them, and re-layouts  3.5 us (3%)
  other arithmetic  1.37 us (1%)
    pallas_call x1, Pallas kernels, channel_shards(): pl.pallas_call(channel_kernel, out_shape=jax.ShapeDtypeStruct((slabs, (4...  53.2 us
    all_to_all x1, waiting for transfers between devices, channel_shards(): lax.all_to_all(result, 'wide', split_axis=0, concat_axis=0, tiled=True)  15.4 us
    ppermute x4, waiting for transfers between devices, channel_shards(): bundle = lax.ppermute(bundle, 'wide', route)  9.25 us
    ppermute x4, starting transfers between devices, channel_shards(): arrived = lax.ppermute(offsets[known:], 'wide', route)  7.17 us
    all_to_all x1, starting transfers between devices, channel_shards(): lax.all_to_all(result, 'wide', split_axis=0, concat_axis=0, tiled=True)  6.28 us
    ppermute x4, starting transfers between devices, channel_shards(): bundle = lax.ppermute(bundle, 'wide', route)  2.62 us
    unnamed x27, local copies, waits for them, and re-layouts  2.24 us
  transfers between devices with their start and end apart: 11, of which 6 were waited for; matrix products, arithmetic and copies ran while one was open for 1% of the time, Pallas kernels for 0%

profile of v8, /device:TPU:0, one launch (start us, length us, event | category | flops | bytes accessed | tf_op | source)
XLA Modules:
  0.0 103.3 jit_solution(14455402334671119146)
XLA Ops:
  0.6 0.9 constant_dynamic-update-slice_fusion.4
  1.5 4.1 %collective-permute-start = (f32[1,3,16,256]{3,2,1,0:T(8,128)S(1)}, f32[1,3,16,256]{3,2,1,0:T(8,128)S(1)}, u32[]{:S(2)}, u32[]{:S(2)}) collective-permute-start(f32[1,3,16,256]{3,2,1,0:T(8,128)S(1)} %get-tuple-element.5), channel_id=1, source_target_pairs={{0,8},{1,9},{2,10},{3,11},{4,12},{5,13},{6,14},{7,15},{8,0},{9,1},... | collective-permute-start | bytes 147464 | tf_op jit(solution)/shard_map/ppermute | solution.py:587
  5.6 1.5 %collective-permute-start.2 = (f32[1,3,16,256]{3,2,1,0:T(8,128)S(1)}, f32[1,3,16,256]{3,2,1,0:T(8,128)S(1)}, u32[]{:S(2)}, u32[]{:S(2)}) collective-permute-start(f32[1,3,16,256]{3,2,1,0:T(8,128)S(1)} %get-tuple-element.5), channel_id=1, source_target_pairs={{0,2},{1,3},{2,0},{3,1},{4,6},{5,7},{6,4},{7,5},{8,10},{9,11},{10,... | collective-permute-start | bytes 147464 | tf_op jit(solution)/shard_map/ppermute | solution.py:577
  7.2 0.6 copy-done.6
  8.1 0.4 collective-permute-start.4
  8.5 0.2 collective-permute-start.6
  8.8 1.9 %collective-permute-start.1 = (f32[2,3,16,256]{3,2,1,0:T(8,128)S(1)}, f32[2,3,16,256]{3,2,1,0:T(8,128)S(1)}, u32[]{:S(2)}, u32[]{:S(2)}) collective-permute-start(f32[2,3,16,256]{3,2,1,0:T(8,128)S(1)} %pad_maximum_fusion.4), channel_id=1, source_target_pairs={{0,4},{1,5},{2,6},{3,7},{4,0},{5,1},{6,2},{7,3},{8,12},{9,13},{10,... | collective-permute-start | bytes 294920 | tf_op jit(solution)/shard_map/ppermute | solution.py:587
  10.7 3.4 %collective-permute-done.4 = bf16[11,16,256]{2,1,0:T(8,128)(2,1)S(1)} collective-permute-done((bf16[11,16,256]{2,1,0:T(8,128)(2,1)S(1)}, bf16[11,16,256]{2,1,0:T(8,128)(2,1)S(1)}, u32[]{:S(2)}, u32[]{:S(2)}) %collective-permute-start.4) | collective-permute-done | bytes 90144 | tf_op jit(solution)/shard_map/ppermute | solution.py:588
  14.2 1.5 %collective-permute-start.5 = (bf16[14,16,256]{2,1,0:T(8,128)(2,1)S(1)}, bf16[14,16,256]{2,1,0:T(8,128)(2,1)S(1)}, u32[]{:S(2)}, u32[]{:S(2)}) collective-permute-start(bf16[14,16,256]{2,1,0:T(8,128)(2,1)S(1)} %pad_maximum_fusion.3), channel_id=1, source_target_pairs={{0,4},{1,5},{2,6},{3,7},{4,0},{5,1},{6,2},{7,3},{8,12},{9,13},{10,... | collective-permute-start | bytes 344072 | tf_op jit(solution)/shard_map/ppermute | solution.py:588
  15.7 1.1 %collective-permute-start.3 = (f32[3,3,16,256]{3,2,1,0:T(8,128)S(1)}, f32[3,3,16,256]{3,2,1,0:T(8,128)S(1)}, u32[]{:S(2)}, u32[]{:S(2)}) collective-permute-start(f32[3,3,16,256]{3,2,1,0:T(8,128)S(1)} %pad_maximum_fusion.1), channel_id=1, source_target_pairs={{0,2},{1,3},{2,0},{3,1},{4,6},{5,7},{6,4},{7,5},{8,10},{9,11},{10,... | collective-permute-start | bytes 442376 | tf_op jit(solution)/shard_map/ppermute | solution.py:587
  16.8 2.2 %collective-permute-done.5 = bf16[14,16,256]{2,1,0:T(8,128)(2,1)S(1)} collective-permute-done((bf16[14,16,256]{2,1,0:T(8,128)(2,1)S(1)}, bf16[14,16,256]{2,1,0:T(8,128)(2,1)S(1)}, u32[]{:S(2)}, u32[]{:S(2)}) %collective-permute-start.5) | collective-permute-done | bytes 114720 | tf_op jit(solution)/shard_map/ppermute | solution.py:588
  19.1 0.6 collective-permute-start.7
  19.8 1.7 %collective-permute-done.3 = f32[3,3,16,256]{3,2,1,0:T(8,128)S(1)} collective-permute-done((f32[3,3,16,256]{3,2,1,0:T(8,128)S(1)}, f32[3,3,16,256]{3,2,1,0:T(8,128)S(1)}, u32[]{:S(2)}, u32[]{:S(2)}) %collective-permute-start.3) | collective-permute-done | bytes 147488 | tf_op jit(solution)/shard_map/ppermute | solution.py:587
  21.6 2.7 %collective-permute-done.7 = bf16[17,16,256]{2,1,0:T(8,128)(2,1)S(1)} collective-permute-done((bf16[17,16,256]{2,1,0:T(8,128)(2,1)S(1)}, bf16[17,16,256]{2,1,0:T(8,128)(2,1)S(1)}, u32[]{:S(2)}, u32[]{:S(2)}) %collective-permute-start.7) | collective-permute-done | bytes 139296 | tf_op jit(solution)/shard_map/ppermute | solution.py:588
  24.5 0.5 copy-done.7
  25.0 1.0 collective-permute-done.9.far_ref
  26.0 53.2 %channel.1 = s16[16,144,128]{2,1,0:T(8,128)(2,1)} custom-call(f32[8,3,16,256]{3,2,1,0:T(8,128)S(1)} %constant_dynamic-update-slice_fusion.offset_ref, bf16[8,3,16,256]{3,2,1,0:T(8,128)(2,1)S(1)} %constant_dynamic-update-slice_fusion.5.base_ref, bf16[8,16,256]{2,1,0:T(8,128)(2,1)S(1)} %get-tuple-element.7.charge_ref, ...), custom_call_target="tpu_custom_call" | custom-call | tf_op jit(solution)/shard_map/channel/pallas_call | solution.py:611
  79.2 6.3 %all-to-all-start = ((s16[16,144,128]{2,1,0:T(8,128)(2,1)}), s16[16,144,128]{2,1,0:T(8,128)(2,1)S(1)}, u32[]{:S(2)}, u32[]{:S(2)}) async-start(s16[16,144,128]{2,1,0:T(8,128)(2,1)} %channel.1), calls=%async_computation | async-start | bytes 1179648 | tf_op jit(solution)/shard_map/all_to_all | solution.py:639
  85.6 15.4 %all-to-all-done = s16[16,144,128]{2,1,0:T(8,128)(2,1)S(1)} async-done(((s16[16,144,128]{2,1,0:T(8,128)(2,1)}), s16[16,144,128]{2,1,0:T(8,128)(2,1)S(1)}, u32[]{:S(2)}, u32[]{:S(2)}) %all-to-all-start) | async-done | bytes 589856 | tf_op jit(solution)/shard_map/all_to_all | solution.py:639
  101.2 0.2 convert_multiply_fusion
  101.5 0.1 copy.29
  101.6 0.2 reshape.114
  101.9 0.7 reshape.115
  102.6 0.7 broadcast_select_fusion
  (64 shorter events, 1.1 us)
Async XLA Ops:
  0.6 6.5 %copy-start.4 = (bf16[16,4096]{1,0:T(8,128)(2,1)S(1)}, bf16[16,4096]{1,0:T(8,128)(2,1)}, u32[]{:S(2)}) copy-start(bf16[16,4096]{1,0:T(8,128)(2,1)} %param.8) | copy-start | bytes 393220
  1.5 7.2 %collective-permute-start = (f32[1,3,16,256]{3,2,1,0:T(8,128)S(1)}, f32[1,3,16,256]{3,2,1,0:T(8,128)S(1)}, u32[]{:S(2)}, u32[]{:S(2)}) collective-permute-start(f32[1,3,16,256]{3,2,1,0:T(8,128)S(1)} %get-tuple-element.5), channel_id=1, source_target_pairs={{0,8},{1,9},{2,10},{3,11},{4,12},{5,13},{6,14},{7,15},{8,0},{9,1},... | collective-permute-start | bytes 147464 | tf_op jit(solution)/shard_map/ppermute | solution.py:587
  5.6 11.2 %collective-permute-start.2 = (f32[1,3,16,256]{3,2,1,0:T(8,128)S(1)}, f32[1,3,16,256]{3,2,1,0:T(8,128)S(1)}, u32[]{:S(2)}, u32[]{:S(2)}) collective-permute-start(f32[1,3,16,256]{3,2,1,0:T(8,128)S(1)} %get-tuple-element.5), channel_id=1, source_target_pairs={{0,2},{1,3},{2,0},{3,1},{4,6},{5,7},{6,4},{7,5},{8,10},{9,11},{10,... | collective-permute-start | bytes 147464 | tf_op jit(solution)/shard_map/ppermute | solution.py:577
  7.2 0.7 copy-start.6
  7.2 0.9 copy-start.5
  8.1 5.9 %collective-permute-start.4 = (bf16[11,16,256]{2,1,0:T(8,128)(2,1)S(1)}, bf16[11,16,256]{2,1,0:T(8,128)(2,1)S(1)}, u32[]{:S(2)}, u32[]{:S(2)}) collective-permute-start(bf16[11,16,256]{2,1,0:T(8,128)(2,1)S(1)} %pad_maximum_fusion.5), channel_id=1, source_target_pairs={{0,8},{1,9},{2,10},{3,11},{4,12},{5,13},{6,14},{7,15},{8,0},{9,1},... | collective-permute-start | bytes 270344 | tf_op jit(solution)/shard_map/ppermute | solution.py:588
  8.5 11.2 %collective-permute-start.6 = (bf16[1,3,16,256]{3,2,1,0:T(8,128)(2,1)S(1)}, bf16[1,3,16,256]{3,2,1,0:T(8,128)(2,1)S(1)}, u32[]{:S(2)}, u32[]{:S(2)}) collective-permute-start(bf16[1,3,16,256]{3,2,1,0:T(8,128)(2,1)S(1)} %get-tuple-element.3), channel_id=1, source_target_pairs={{0,2},{1,3},{2,0},{3,1},{4,6},{5,7},{6,4},{7,5},{8,10},{9,11},{10,... | collective-permute-start | bytes 73736 | tf_op jit(solution)/shard_map/ppermute | solution.py:578
  8.8 6.9 %collective-permute-start.1 = (f32[2,3,16,256]{3,2,1,0:T(8,128)S(1)}, f32[2,3,16,256]{3,2,1,0:T(8,128)S(1)}, u32[]{:S(2)}, u32[]{:S(2)}) collective-permute-start(f32[2,3,16,256]{3,2,1,0:T(8,128)S(1)} %pad_maximum_fusion.4), channel_id=1, source_target_pairs={{0,4},{1,5},{2,6},{3,7},{4,0},{5,1},{6,2},{7,3},{8,12},{9,13},{10,... | collective-permute-start | bytes 294920 | tf_op jit(solution)/shard_map/ppermute | solution.py:587
  14.2 4.9 %collective-permute-start.5 = (bf16[14,16,256]{2,1,0:T(8,128)(2,1)S(1)}, bf16[14,16,256]{2,1,0:T(8,128)(2,1)S(1)}, u32[]{:S(2)}, u32[]{:S(2)}) collective-permute-start(bf16[14,16,256]{2,1,0:T(8,128)(2,1)S(1)} %pad_maximum_fusion.3), channel_id=1, source_target_pairs={{0,4},{1,5},{2,6},{3,7},{4,0},{5,1},{6,2},{7,3},{8,12},{9,13},{10,... | collective-permute-start | bytes 344072 | tf_op jit(solution)/shard_map/ppermute | solution.py:588
  15.7 5.8 %collective-permute-start.3 = (f32[3,3,16,256]{3,2,1,0:T(8,128)S(1)}, f32[3,3,16,256]{3,2,1,0:T(8,128)S(1)}, u32[]{:S(2)}, u32[]{:S(2)}) collective-permute-start(f32[3,3,16,256]{3,2,1,0:T(8,128)S(1)} %pad_maximum_fusion.1), channel_id=1, source_target_pairs={{0,2},{1,3},{2,0},{3,1},{4,6},{5,7},{6,4},{7,5},{8,10},{9,11},{10,... | collective-permute-start | bytes 442376 | tf_op jit(solution)/shard_map/ppermute | solution.py:587
  19.1 5.1 %collective-permute-start.7 = (bf16[17,16,256]{2,1,0:T(8,128)(2,1)S(1)}, bf16[17,16,256]{2,1,0:T(8,128)(2,1)S(1)}, u32[]{:S(2)}, u32[]{:S(2)}) collective-permute-start(bf16[17,16,256]{2,1,0:T(8,128)(2,1)S(1)} %pad_maximum_fusion.2), channel_id=1, source_target_pairs={{0,2},{1,3},{2,0},{3,1},{4,6},{5,7},{6,4},{7,5},{8,10},{9,11},{10,... | collective-permute-start | bytes 417800 | tf_op jit(solution)/shard_map/ppermute | solution.py:588
  21.5 4.5 %collective-permute-start.8 = (f32[8,3,16,256]{3,2,1,0:T(8,128)S(1)}, f32[8,3,16,256]{3,2,1,0:T(8,128)S(1)}, u32[]{:S(2)}, u32[]{:S(2)}) collective-permute-start(f32[8,3,16,256]{3,2,1,0:T(8,128)S(1)} %constant_dynamic-update-slice_fusion.offset_ref), channel_id=1, source_target_pairs={{0,1},{1,0},{2,3},{3,2},{4,5},{5,4},{6,7},{7,6},{8,9},{9,8},{10,11... | collective-permute-start | bytes 1179656 | tf_op jit(solution)/shard_map/ppermute | solution.py:587
  24.3 0.7 copy-start.7
  24.3 1.7 %copy-start = (f32[2,128,128]{2,1,0:T(8,128)S(1)}, f32[2,128,128]{2,1,0:T(8,128)}, u32[]{:S(2)}) copy-start(f32[2,128,128]{2,1,0:T(8,128)} %constant.21.clone.inverse_hbm) | copy-start | bytes 393220
  24.3 1.7 %copy-start.1 = (bf16[256,256]{1,0:T(8,128)(2,1)S(1)}, bf16[256,256]{1,0:T(8,128)(2,1)}, u32[]{:S(2)}) copy-start(bf16[256,256]{1,0:T(8,128)(2,1)} %constant.22.clone.right_hbm) | copy-start | bytes 393220
  24.3 1.7 %copy-start.2 = (bf16[256,256]{1,0:T(8,128)(2,1)S(1)}, bf16[256,256]{1,0:T(8,128)(2,1)}, u32[]{:S(2)}) copy-start(bf16[256,256]{1,0:T(8,128)(2,1)} %constant.23.clone.left_hbm) | copy-start | bytes 393220
  24.4 1.6 %collective-permute-start.9 = (bf16[32,16,256]{2,1,0:T(8,128)(2,1)S(1)}, bf16[32,16,256]{2,1,0:T(8,128)(2,1)S(1)}, u32[]{:S(2)}, u32[]{:S(2)}) collective-permute-start(bf16[32,16,256]{2,1,0:T(8,128)(2,1)S(1)} %pad_maximum_fusion), channel_id=1, source_target_pairs={{0,1},{1,0},{2,3},{3,2},{4,5},{5,4},{6,7},{7,6},{8,9},{9,8},{10,11... | collective-permute-start | bytes 786440 | tf_op jit(solution)/shard_map/ppermute | solution.py:588
  25.0 1.0 %copy-start.3 = (f32[16]{0:T(128)S(1)}, f32[16]{0:T(128)}, u32[]{:S(2)}) copy-start(f32[16]{0:T(128)} %widths_ref.1) | copy-start | bytes 196
  79.2 21.8 %all-to-all-start = ((s16[16,144,128]{2,1,0:T(8,128)(2,1)}), s16[16,144,128]{2,1,0:T(8,128)(2,1)S(1)}, u32[]{:S(2)}, u32[]{:S(2)}) async-start(s16[16,144,128]{2,1,0:T(8,128)(2,1)} %channel.1), calls=%async_computation | async-start | bytes 1179648 | tf_op jit(solution)/shard_map/all_to_all | solution.py:639
